TPU v7x, 32 devices: a whole 2x2x4 slice. The times are simulated.
32 devices in a mesh: replica: 4 (over y, x), fsdp: 8 (over z, core).
Axes of the slice: x: 2, y: 2, z: 4, core: 2. Of those that a mesh axis runs over, the one named last changes fastest.
Arguments:
- tokens: bfloat16 [2, 32, 512, 1536], P(None, ('replica', 'fsdp')), may hold values from -6 to 6
- cotangent: bfloat16 [2, 32, 512, 1536], P(None, ('replica', 'fsdp')), may hold values from -6 to 6
- lengths: int32 [2, 32], P(None, ('replica', 'fsdp')), may hold values from 128 to 512, as said below
- routes: int32 [2, 32, 512, 2], P(None, ('replica', 'fsdp')), may hold values from 0 to 2, as said below
- slot_index: int32 [2, 32, 512, 2], P(None, ('replica', 'fsdp')), may hold values from 0 to 511, as said below
- norm_gains: float32 [2, 1536], P(None, 'fsdp'), may hold values from 0.5 to 1.5
- norm_first: float32 [2, 1536], P(None, 'fsdp'), may hold values from -0.0034179688 to 0.0034179688
- norm_second: float32 [2, 1536], P(None, 'fsdp'), may hold values from 1.3e-06 to 5.3e-06
- in_proj: float32 [1536, 2560], P('fsdp'), may hold values from -0.15625 to 0.15625
- in_first: float32 [1536, 2560], P('fsdp'), may hold values from -0.0034179688 to 0.0034179688
- in_second: float32 [1536, 2560], P('fsdp'), may hold values from 1.3e-06 to 5.3e-06
- out_proj: float32 [1536, 1536], P('fsdp'), may hold values from -1.25 to 1.25
- out_first: float32 [1536, 1536], P('fsdp'), may hold values from -0.0034179688 to 0.0034179688
- out_second: float32 [1536, 1536], P('fsdp'), may hold values from 1.3e-06 to 5.3e-06
- router: float32 [1536, 3], P('fsdp'), may hold values from -0.109375 to 0.109375
- router_first: float32 [1536, 3], P('fsdp'), may hold values from -0.0034179688 to 0.0034179688
- router_second: float32 [1536, 3], P('fsdp'), may hold values from 1.3e-06 to 5.3e-06
- up_proj: float32 [3, 1536, 2048], P(None, 'fsdp'), may hold values from -0.15625 to 0.15625
- up_first: float32 [3, 1536, 2048], P(None, 'fsdp'), may hold values from -0.0034179688 to 0.0034179688
- up_second: float32 [3, 1536, 2048], P(None, 'fsdp'), may hold values from 1.3e-06 to 5.3e-06
- down_proj: float32 [3, 1024, 1536], P(None, 'fsdp'), may hold values from -0.5 to 0.5
- down_first: float32 [3, 1024, 1536], P(None, 'fsdp'), may hold values from -0.0034179688 to 0.0034179688
- down_second: float32 [3, 1024, 1536], P(None, 'fsdp'), may hold values from 1.3e-06 to 5.3e-06
Outputs:
- block_out: bfloat16 [2, 32, 512, 1536], P(None, ('replica', 'fsdp'))
- input_grad: bfloat16 [2, 32, 512, 1536], P(None, ('replica', 'fsdp'))
- grad_rms: float32 [5], replicated
- down_rms: float32 [1], replicated
- norm_grad: float32 [2, 1536], P(None, 'fsdp')
- norm_update: float32 [2, 1536], P(None, 'fsdp')
- norm_first_new: float32 [2, 1536], P(None, 'fsdp')
- norm_second_new: float32 [2, 1536], P(None, 'fsdp')
- in_grad: float32 [1536, 2560], P('fsdp')
- in_update: float32 [1536, 2560], P('fsdp')
- in_first_new: float32 [1536, 2560], P('fsdp')
- in_second_new: float32 [1536, 2560], P('fsdp')
- out_grad: float32 [1536, 1536], P('fsdp')
- out_update: float32 [1536, 1536], P('fsdp')
- out_first_new: float32 [1536, 1536], P('fsdp')
- out_second_new: float32 [1536, 1536], P('fsdp')
- router_grad: float32 [1536, 3], P('fsdp')
- router_update: float32 [1536, 3], P('fsdp')
- router_first_new: float32 [1536, 3], P('fsdp')
- router_second_new: float32 [1536, 3], P('fsdp')
- up_grad: float32 [3, 1536, 2048], P(None, 'fsdp')
- up_update: float32 [3, 1536, 2048], P(None, 'fsdp')
- up_first_new: float32 [3, 1536, 2048], P(None, 'fsdp')
- up_second_new: float32 [3, 1536, 2048], P(None, 'fsdp')
- down_grad: float32 [3, 1024, 1536], P(None, 'fsdp')
- down_update: float32 [3, 1024, 1536], P(None, 'fsdp')
- down_first_new: float32 [3, 1024, 1536], P(None, 'fsdp')
- down_second_new: float32 [3, 1024, 1536], P(None, 'fsdp')
Inputs may be any that keep to these rules, and one draw needn't show every extreme that they name: `lengths`: in every draw some sequence has exactly 512 valid tokens and some has exactly 128. `routes`: the two experts of a token differ. `slot_index`: for each sequence and expert, the tokens routed to it take distinct slots; its valid routed tokens take the lowest slots and its other routed tokens the slots after them; in every draw some expert takes all 512 tokens of some sequence.
All inputs are finite; a program needn't handle non-finite values.
Results may differ from a plain program's by a relative error of at most 0.015.
The roundings to bfloat16 on the way count: a program that leaves them out, or rounds other values in their place, can miss the bound.
Values may be sent and summed in bfloat16 or wider, within the bound.
No kernel may reach another device: no remote copies, remote signals or barrier semaphores. Data moves between devices by JAX's collectives and lax.ppermute only.
A program may use at most 384 MiB of HBM per device.

v0:
```python
import jax
import jax.numpy as jnp
from jax import lax
from jax.sharding import PartitionSpec as P

QUERY_HEADS = 24
KEY_VALUE_HEADS = 8
HEAD_SIZE = 64
FE = 1024
E = 3
MB = 2
STEP = 10
CAP = 320


precise = lax.Precision.HIGHEST
epsilon = 1e-06
beta_first = 0.9
beta_second = 0.95
learn_rate = 0.02
weight_decay = 0.1
adam_floor = 1e-08
clip_level = 0.005


def norm_scale(values):
    return lax.rsqrt(jnp.mean(values * values, axis=-1, keepdims=True) + epsilon)


def gather_forward(low_parts):
    return (
        lax.all_gather(low_parts[0], "fsdp", axis=1, tiled=True),
        lax.all_gather(low_parts[1], "fsdp", axis=0, tiled=True),
        lax.all_gather(low_parts[2], "fsdp", axis=0, tiled=True),
        lax.all_gather(low_parts[3], "fsdp", axis=0, tiled=True),
        lax.all_gather(low_parts[4], "fsdp", axis=1, tiled=True),
        lax.all_gather(low_parts[5], "fsdp", axis=1, tiled=True),
    )


def gather_backward(low_parts):
    return (
        lax.all_gather(low_parts[0], "fsdp", axis=1, tiled=True),
        lax.all_gather(low_parts[1], "fsdp", axis=0, tiled=True),
        lax.all_gather(low_parts[2], "fsdp", axis=0, tiled=True),
        lax.all_gather(low_parts[3], "fsdp", axis=0, tiled=True),
        lax.all_gather(low_parts[4], "fsdp", axis=1, tiled=True),
        lax.all_gather(low_parts[5], "fsdp", axis=1, tiled=True),
    )


def reduce_whole(new_grads):
    return (
        lax.psum_scatter(new_grads[0], "fsdp", scatter_dimension=1, tiled=True),
        lax.psum_scatter(new_grads[1], "fsdp", scatter_dimension=0, tiled=True),
        lax.psum_scatter(new_grads[2], "fsdp", scatter_dimension=0, tiled=True),
        lax.psum_scatter(new_grads[3], "fsdp", scatter_dimension=0, tiled=True),
        lax.psum_scatter(new_grads[4], "fsdp", scatter_dimension=1, tiled=True),
        lax.psum_scatter(new_grads[5], "fsdp", scatter_dimension=1, tiled=True),
    )


def softmax_rows(scores):
    highest = jnp.max(scores, axis=-1, keepdims=True)
    raised = jnp.exp(scores - highest)
    return raised / jnp.sum(raised, axis=-1, keepdims=True)


def forward_pass(rows_in, length, route, slot, weights):
    gains, w_in, w_out, w_router, w_up, w_down = weights
    sequence_length = rows_in.shape[0]
    model_dim = rows_in.shape[1]
    query_width = QUERY_HEADS * HEAD_SIZE
    key_value_width = KEY_VALUE_HEADS * HEAD_SIZE
    position = jnp.arange(sequence_length)
    live_mask = (position < length).astype(jnp.float32)
    rows_float = rows_in.astype(jnp.float32)
    gain_one = gains[0].astype(jnp.float32)
    gain_two = gains[1].astype(jnp.float32)
    scale_one = norm_scale(rows_float)
    normed_one = (rows_float * scale_one * gain_one).astype(jnp.bfloat16)
    projected_rows = jnp.dot(normed_one, w_in, preferred_element_type=jnp.float32).astype(
        jnp.bfloat16
    )
    query_rows = projected_rows[:, :query_width].reshape(
        sequence_length, KEY_VALUE_HEADS, QUERY_HEADS // KEY_VALUE_HEADS, HEAD_SIZE
    )
    key_rows_full = projected_rows[:, query_width : query_width + key_value_width].reshape(
        sequence_length, KEY_VALUE_HEADS, HEAD_SIZE
    )
    value_rows_full = projected_rows[:, query_width + key_value_width :].reshape(
        sequence_length, KEY_VALUE_HEADS, HEAD_SIZE
    )
    scores = jnp.einsum(
        "qhgd,khd->hgqk", query_rows, key_rows_full, preferred_element_type=jnp.float32
    ) * HEAD_SIZE ** (-0.5)
    allowed = (position[None, :] <= position[:, None]) & (position[None, :] < length)
    scores = jnp.where(allowed, scores, -1000000000.0)
    highest = jnp.max(scores, axis=-1, keepdims=True)
    raised = jnp.exp(scores - highest)
    totals = jnp.sum(raised, axis=-1, keepdims=True)
    probs = raised / totals
    log_total = highest + jnp.log(totals)
    mixed = jnp.einsum(
        "hgqk,khd->qhgd",
        probs.astype(jnp.bfloat16),
        value_rows_full,
        preferred_element_type=jnp.float32,
    )
    mixed = mixed.reshape(sequence_length, query_width).astype(jnp.bfloat16)
    residual = rows_float + jnp.dot(mixed, w_out, preferred_element_type=jnp.float32)
    scale_two = norm_scale(residual)
    normed_two = (residual * scale_two * gain_two).astype(jnp.bfloat16)
    router_prob = softmax_rows(jnp.dot(normed_two, w_router, preferred_element_type=jnp.float32))
    onehot = (route[:, :, None] == jnp.arange(E)[None, None, :]).astype(jnp.float32)
    gate_weights = jnp.sum(onehot * router_prob[:, None, :], axis=-1)
    keep_mask = ((position[:, None] < length) & (slot < CAP)).astype(jnp.float32)
    target = jnp.where(keep_mask > 0, route * CAP + slot, E * CAP)
    spread_rows = jnp.broadcast_to(normed_two[:, None, :], (sequence_length, 2, model_dim)).reshape(
        -1, model_dim
    )
    buffer = (
        jnp.zeros((E * CAP + 1, model_dim), jnp.bfloat16).at[target.reshape(-1)].set(spread_rows)
    )
    expert_in = buffer[: E * CAP].reshape(E, CAP, model_dim)
    gate_up = jnp.einsum("ecd,edf->ecf", expert_in, w_up, preferred_element_type=jnp.float32)
    act_gate = gate_up[:, :, :FE]
    act_up = gate_up[:, :, FE:]
    hidden = (jax.nn.silu(act_gate) * act_up).astype(jnp.bfloat16)
    expert_out = jnp.einsum("ecf,efd->ecd", hidden, w_down, preferred_element_type=jnp.float32)
    padded = jnp.concatenate(
        [expert_out.reshape(E * CAP, model_dim), jnp.zeros((1, model_dim), jnp.float32)], axis=0
    )
    picked = padded[target]
    mixture = jnp.sum((gate_weights * keep_mask)[:, :, None] * picked, axis=1)
    out_rows = (live_mask[:, None] * (residual + mixture)).astype(jnp.bfloat16)
    saved = (
        rows_float,
        scale_one,
        normed_one,
        query_rows,
        key_rows_full,
        value_rows_full,
        allowed,
        log_total,
        mixed,
        residual,
        scale_two,
        normed_two,
        router_prob,
        onehot,
        gate_weights,
        keep_mask,
        target,
        expert_in,
        act_gate,
        act_up,
        hidden,
        picked,
        live_mask,
    )
    return (out_rows, saved)


def backward_pass(saved, cot_rows, weights):
    (
        rows_float,
        scale_one,
        normed_one,
        query_rows,
        key_rows_full,
        value_rows_full,
        allowed,
        log_total,
        mixed,
        residual,
        scale_two,
        normed_two,
        router_prob,
        onehot,
        gate_weights,
        keep_mask,
        target,
        expert_in,
        act_gate,
        act_up,
        hidden,
        picked,
        live_mask,
    ) = saved
    gains, w_in, w_out, w_router, w_up, w_down = weights
    sequence_length = rows_float.shape[0]
    model_dim = rows_float.shape[1]
    query_width = QUERY_HEADS * HEAD_SIZE
    key_value_width = KEY_VALUE_HEADS * HEAD_SIZE
    gain_one = gains[0].astype(jnp.float32)
    gain_two = gains[1].astype(jnp.float32)
    grad_out = cot_rows.astype(jnp.float32) * live_mask[:, None]
    d_picked = (gate_weights * keep_mask)[:, :, None] * grad_out[:, None, :]
    d_gates = keep_mask * jnp.sum(grad_out[:, None, :] * picked, axis=-1)
    d_padded = (
        jnp.zeros((E * CAP + 1, model_dim), jnp.float32)
        .at[target.reshape(-1)]
        .add(d_picked.reshape(-1, model_dim))
    )
    d_expert = d_padded[: E * CAP].reshape(E, CAP, model_dim).astype(jnp.bfloat16)
    d_hidden = jnp.einsum("ecd,efd->ecf", d_expert, w_down, preferred_element_type=jnp.float32)
    g_down = jnp.einsum("ecf,ecd->efd", hidden, d_expert, preferred_element_type=jnp.float32)
    sigma = jax.nn.sigmoid(act_gate)
    d_gate_part = d_hidden * act_up * sigma * (1.0 + act_gate * (1.0 - sigma))
    d_up_part = d_hidden * act_gate * sigma
    d_gate_up = jnp.concatenate([d_gate_part, d_up_part], axis=-1).astype(jnp.bfloat16)
    d_inputs = jnp.einsum("ecf,edf->ecd", d_gate_up, w_up, preferred_element_type=jnp.float32)
    g_up = jnp.einsum("ecd,ecf->edf", expert_in, d_gate_up, preferred_element_type=jnp.float32)
    d_flat = jnp.concatenate(
        [d_inputs.reshape(E * CAP, model_dim), jnp.zeros((1, model_dim), jnp.float32)], axis=0
    )
    d_normed_two = jnp.sum(d_flat[target] * keep_mask[:, :, None], axis=1)
    d_prob = jnp.sum(d_gates[:, :, None] * onehot, axis=1)
    d_logits = router_prob * (d_prob - jnp.sum(d_prob * router_prob, axis=-1, keepdims=True))
    g_router = jnp.dot(normed_two.astype(jnp.float32).T, d_logits, precision=precise)
    d_normed_two = d_normed_two + jnp.dot(
        d_logits, w_router.astype(jnp.float32).T, precision=precise
    )
    weighted_two = d_normed_two * gain_two
    g_gain_two = jnp.sum(d_normed_two * residual * scale_two, axis=0)
    d_resid = (
        grad_out
        + scale_two * weighted_two
        - residual * scale_two**3 * jnp.mean(weighted_two * residual, axis=-1, keepdims=True)
    )
    d_attn = d_resid.astype(jnp.bfloat16)
    mixed_gradient = jnp.einsum(
        "qd,wd->qw", d_attn, w_out, preferred_element_type=jnp.float32
    ).astype(jnp.bfloat16)
    g_out = jnp.einsum("qw,qd->wd", mixed, d_attn, preferred_element_type=jnp.float32)
    head_gradient = mixed_gradient.reshape(
        sequence_length, KEY_VALUE_HEADS, QUERY_HEADS // KEY_VALUE_HEADS, HEAD_SIZE
    )
    scores = jnp.einsum(
        "qhgd,khd->hgqk", query_rows, key_rows_full, preferred_element_type=jnp.float32
    ) * HEAD_SIZE ** (-0.5)
    scores = jnp.where(allowed, scores, -1000000000.0)
    probs = jnp.exp(scores - log_total)
    d_probs = jnp.einsum(
        "qhgd,khd->hgqk", head_gradient, value_rows_full, preferred_element_type=jnp.float32
    )
    d_scores = (probs * (d_probs - jnp.sum(d_probs * probs, axis=-1, keepdims=True))).astype(
        jnp.bfloat16
    )
    d_queries = jnp.einsum(
        "hgqk,khd->qhgd", d_scores, key_rows_full, preferred_element_type=jnp.float32
    ) * HEAD_SIZE ** (-0.5)
    d_keys = jnp.einsum(
        "hgqk,qhgd->khd", d_scores, query_rows, preferred_element_type=jnp.float32
    ) * HEAD_SIZE ** (-0.5)
    d_values = jnp.einsum(
        "hgqk,qhgd->khd",
        probs.astype(jnp.bfloat16),
        head_gradient,
        preferred_element_type=jnp.float32,
    )
    d_projected = jnp.concatenate(
        [
            d_queries.reshape(sequence_length, query_width),
            d_keys.reshape(sequence_length, key_value_width),
            d_values.reshape(sequence_length, key_value_width),
        ],
        axis=-1,
    ).astype(jnp.bfloat16)
    g_in = jnp.einsum("qc,qw->cw", normed_one, d_projected, preferred_element_type=jnp.float32)
    d_normed_one = jnp.einsum("qw,cw->qc", d_projected, w_in, preferred_element_type=jnp.float32)
    weighted_one = d_normed_one * gain_one
    g_gain_one = jnp.sum(d_normed_one * rows_float * scale_one, axis=0)
    d_rows = (
        d_resid
        + scale_one * weighted_one
        - rows_float * scale_one**3 * jnp.mean(weighted_one * rows_float, axis=-1, keepdims=True)
    )
    g_gains = jnp.stack([g_gain_one, g_gain_two], axis=0)
    return (d_rows.astype(jnp.bfloat16), (g_gains, g_in, g_out, g_router, g_up, g_down))


def adam_step(master, first, second, gradient, rms, decayed):
    clipped = gradient * jnp.minimum(1.0, clip_level / rms)
    first_new = beta_first * first + (1.0 - beta_first) * clipped
    second_new = beta_second * second + (1.0 - beta_second) * clipped * clipped
    first_hat = first_new / (1.0 - beta_first**STEP)
    second_hat = second_new / (1.0 - beta_second**STEP)
    change = first_hat / (jnp.sqrt(second_hat) + adam_floor) + decayed * weight_decay * master
    update = -learn_rate * change
    return (gradient, update, first_new, second_new)


def per_device(
    tokens,
    cotangent,
    lengths,
    routes,
    slot_index,
    norm_gains,
    norm_first,
    norm_second,
    in_proj,
    in_first,
    in_second,
    out_proj,
    out_first,
    out_second,
    router,
    router_first,
    router_second,
    up_proj,
    up_first,
    up_second,
    down_proj,
    down_first,
    down_second,
):
    masters = (norm_gains, in_proj, out_proj, router, up_proj, down_proj)
    low_parts = tuple((master.astype(jnp.bfloat16) for master in masters))
    block_rows = []
    grad_rows = []
    running = None
    for micro_index in range(MB):
        forward_weights = gather_forward(low_parts)
        out_rows, saved = forward_pass(
            tokens[micro_index, 0],
            lengths[micro_index, 0],
            routes[micro_index, 0],
            slot_index[micro_index, 0],
            forward_weights,
        )
        backward_weights = gather_backward(low_parts)
        in_rows, new_grads = backward_pass(saved, cotangent[micro_index, 0], backward_weights)
        block_rows.append(out_rows)
        grad_rows.append(in_rows)
        if running is None:
            running = new_grads
        else:
            running = tuple((earlier + later for earlier, later in zip(running, new_grads)))
    running = reduce_whole(running)
    summed = lax.psum(
        (running[0], running[1], running[2], running[3], running[4], running[5]), "replica"
    )
    group_size = lax.axis_size("fsdp")
    grad_scale = 1.0 / (MB * lax.axis_size("replica") * group_size)
    grads = tuple((total * grad_scale for total in summed))
    local_squares = jnp.stack([jnp.sum(grad * grad) for grad in grads])
    total_squares = lax.psum(local_squares, "fsdp")
    entry_counts = jnp.array([float(grad.size * group_size) for grad in grads], jnp.float32)
    rms = jnp.sqrt(total_squares / entry_counts + epsilon)
    norm_res = adam_step(norm_gains, norm_first, norm_second, grads[0], rms[0], 0.0)
    in_res = adam_step(in_proj, in_first, in_second, grads[1], rms[1], 1.0)
    out_res = adam_step(out_proj, out_first, out_second, grads[2], rms[2], 1.0)
    router_res = adam_step(router, router_first, router_second, grads[3], rms[3], 1.0)
    up_res = adam_step(up_proj, up_first, up_second, grads[4], rms[4], 1.0)
    down_res = adam_step(down_proj, down_first, down_second, grads[5], rms[5], 1.0)
    block_out = jnp.stack(block_rows, axis=0)[:, None]
    input_grad = jnp.stack(grad_rows, axis=0)[:, None]
    return (
        block_out,
        input_grad,
        rms[:5],
        rms[5:6],
        norm_res[0],
        norm_res[1],
        norm_res[2],
        norm_res[3],
        in_res[0],
        in_res[1],
        in_res[2],
        in_res[3],
        out_res[0],
        out_res[1],
        out_res[2],
        out_res[3],
        router_res[0],
        router_res[1],
        router_res[2],
        router_res[3],
        up_res[0],
        up_res[1],
        up_res[2],
        up_res[3],
        down_res[0],
        down_res[1],
        down_res[2],
        down_res[3],
    )


def solution(mesh):
    return jax.shard_map(
        per_device,
        mesh=mesh,
        in_specs=(
            P(None, ("replica", "fsdp"), None, None),
            P(None, ("replica", "fsdp"), None, None),
            P(None, ("replica", "fsdp")),
            P(None, ("replica", "fsdp"), None, None),
            P(None, ("replica", "fsdp"), None, None),
            P(None, "fsdp"),
            P(None, "fsdp"),
            P(None, "fsdp"),
            P("fsdp", None),
            P("fsdp", None),
            P("fsdp", None),
            P("fsdp", None),
            P("fsdp", None),
            P("fsdp", None),
            P("fsdp", None),
            P("fsdp", None),
            P("fsdp", None),
            P(None, "fsdp", None),
            P(None, "fsdp", None),
            P(None, "fsdp", None),
            P(None, "fsdp", None),
            P(None, "fsdp", None),
            P(None, "fsdp", None),
        ),
        out_specs=(
            P(None, ("replica", "fsdp"), None, None),
            P(None, ("replica", "fsdp"), None, None),
            P(),
            P(),
            P(None, "fsdp"),
            P(None, "fsdp"),
            P(None, "fsdp"),
            P(None, "fsdp"),
            P("fsdp", None),
            P("fsdp", None),
            P("fsdp", None),
            P("fsdp", None),
            P("fsdp", None),
            P("fsdp", None),
            P("fsdp", None),
            P("fsdp", None),
            P("fsdp", None),
            P("fsdp", None),
            P("fsdp", None),
            P("fsdp", None),
            P(None, "fsdp", None),
            P(None, "fsdp", None),
            P(None, "fsdp", None),
            P(None, "fsdp", None),
            P(None, "fsdp", None),
            P(None, "fsdp", None),
            P(None, "fsdp", None),
            P(None, "fsdp", None),
        ),
        check_vma=False,
    )
```

profile of v0, /device:TPU:0, one launch (start us, length us, event | category | flops | bytes accessed | tf_op | source)
XLA Modules:
  0.0 1970.3 jit_solution(8968355409564851019)
XLA Ops:
  31.8 13.6 all-gather
  64.6 13.1 all-gather.1
  143.3 13.9 fusion.53
  189.0 15.5 scatter_custom_fusion.2
  224.4 12.0 fusion.52
  245.9 66.9 %all-gather.11.cloned.1.call-done = bf16[3,1536,2048]{2,1,0:T(8,128)(2,1)} async-done(((bf16[3,192,2048]{2,1,0:T(8,128)(2,1)}), bf16[3,1536,2048]{2,1,0:T(8,128)(2,1)}) %all-gather.11.cloned.1.call-update) | async-done | bytes 18874384 | tf_op jit(solution)/shard_map/all_gather | solution.py:36
  312.8 12.1 fusion.137
  325.0 78.8 %all-gather.13.cloned.1.call-done = bf16[3,1024,1536]{2,1,0:T(8,128)(2,1)} async-done(((bf16[3,128,1536]{2,1,0:T(8,128)(2,1)}), bf16[3,1024,1536]{2,1,0:T(8,128)(2,1)}) %all-gather.13.cloned.1.call-update) | async-done | bytes 9437200 | tf_op jit(solution)/shard_map/all_gather | solution.py:37
  414.4 13.2 fusion.49
  479.3 17.2 multiply_reduce_fusion.2
  497.9 32.0 %multiply_reduce_fusion.3 = f32[512,1536]{1,0:T(8,128)S(1)} fusion(f32[512,2,1536]{2,1,0:T(2,128)} %reshape.813, f32[512,2]{1,0:T(8,128)S(1)} %copy-done.79), kind=kLoop, calls=%fused_computation.60 | loop fusion | flops 2359296 | bytes 9441280 | tf_op jit(solution)/shard_map/reduce_sum | solution.py:218
  557.1 15.7 scatter_custom_fusion.3
  587.0 12.1 multiply_convert_fusion.1
  599.1 13.3 fusion.47
  665.3 16.8 multiply_reduce_fusion
  683.3 32.2 %multiply_reduce_fusion.1 = f32[512,1536]{1,0:T(8,128)S(1)} fusion(f32[512,2,1536]{2,1,0:T(2,128)} %reshape.821, f32[512,2]{1,0:T(8,128)S(1)} %copy-done.78), kind=kLoop, calls=%fused_computation.56 | loop fusion | flops 2359296 | bytes 9441280 | tf_op jit(solution)/shard_map/reduce_sum | solution.py:218
  753.0 21.4 %fusion = (f32[8,3,512]{2,1,0:T(4,128)S(1)}, f32[8,512,512,3]{2,1,3,0:T(8,128)}) fusion(f32[8,3,512]{2,1,0:T(4,128)S(1)} %copy-done.80, f32[8,512,512,3]{2,1,3,0:T(8,128)} %copy-done.1, pred[512,512]{0,1:T(8,128)(4,1)S(1)} %copy-done.45, bf16[512,8,64,1]{0,2,3,1:T(8,128)(2,1)S(1)} %bitcast.373, bf16[512,8,3,64]{0,3,2,1:T(8,128)(2,1)S(1)} %bitcast.349), kind=kOutput, calls=%fused_computation.10 | convolution fusion | flops 836751360 | bytes 52789248 | tf_op jit(solution)/shard_map/qhgd,khd->hgqk/dot_general | solution.py:245
  774.4 17.6 fusion.2
  797.6 21.4 %fusion.3 = (f32[8,3,512]{2,1,0:T(4,128)S(1)}, f32[8,512,512,3]{2,1,3,0:T(8,128)}) fusion(f32[8,3,512]{2,1,0:T(4,128)S(1)} %copy-done.81, f32[8,512,512,3]{2,1,3,0:T(8,128)} %copy-done, pred[512,512]{0,1:T(8,128)(4,1)S(1)} %copy-done.43, bf16[512,8,64,1]{0,2,3,1:T(8,128)(2,1)S(1)} %bitcast.371, bf16[512,8,3,64]{0,3,2,1:T(8,128)(2,1)S(1)} %bitcast.351), kind=kOutput, calls=%fused_computation.15 | convolution fusion | flops 836751360 | bytes 52789248 | tf_op jit(solution)/shard_map/qhgd,khd->hgqk/dot_general | solution.py:245
  819.0 17.8 fusion.5
  861.7 11.5 fusion.75
  895.2 12.8 convolution_add_fusion.1
  920.8 13.0 convolution_add_fusion.3
  935.7 18.4 fusion.48
  954.0 27.8 %convolution_add_fusion = f32[3,1536,2048]{2,1,0:T(8,128)} fusion(f32[3,1536,2048]{2,1,0:T(8,128)} %fusion.48, bf16[3,320,1536]{2,1,0:T(8,128)(2,1)} %bitcast.334, bf16[3,320,1024]{2,1,0:T(8,128)(2,1)} %get-tuple-element.205, bf16[3,320,1024]{2,1,0:T(8,128)(2,1)} %copy-done.73), kind=kOutput, calls=%fused_computation.30 | convolution fusion | flops 6057099264 | bytes 82378752 | tf_op jit(solution)/shard_map/ecd,ecf->edf/dot_general | solution.py:214
  1005.8 59.9 %reduce-scatter.11.cloned.1.call-done = f32[192,2560]{1,0:T(8,128)} async-done(((f32[1536,2560]{1,0:T(8,128)}), f32[192,2560]{1,0:T(8,128)}) %reduce-scatter.11.cloned.1.call-update) | async-done | bytes 1966096 | tf_op jit(solution)/shard_map/reduce_scatter | solution.py:55
  1065.7 188.7 %reduce-scatter.17.cloned.1.call-done = f32[3,128,1536]{2,1,0:T(8,128)} async-done(((f32[3,1024,1536]{2,1,0:T(8,128)}), f32[3,128,1536]{2,1,0:T(8,128)}) %reduce-scatter.17.cloned.1.call-update) | async-done | bytes 2359312 | tf_op jit(solution)/shard_map/reduce_scatter | solution.py:59
  1254.4 365.7 %reduce-scatter.15.cloned.1.call-done = f32[3,192,2048]{2,1,0:T(8,128)} async-done(((f32[3,1536,2048]{2,1,0:T(8,128)}), f32[3,192,2048]{2,1,0:T(8,128)}) %reduce-scatter.15.cloned.1.call-update) | async-done | bytes 4718608 | tf_op jit(solution)/shard_map/reduce_scatter | solution.py:58
  1631.0 22.0 %reduce-scatter.19.cloned.1.call-done = f32[192,2]{1,0:T(8,128)} async-done(((f32[1536,2]{1,0:T(8,128)}), f32[192,2]{1,0:T(8,128)}) %reduce-scatter.19.cloned.1.call-update) | async-done | bytes 1552
  1654.0 31.5 %reduce-scatter.21.cloned.1.call-done = f32[192,3]{1,0:T(8,128)} async-done(((f32[1536,3]{1,0:T(8,128)}), f32[192,3]{1,0:T(8,128)}) %reduce-scatter.21.cloned.1.call-update) | async-done | bytes 2320
  1699.1 192.3 %all-reduce.8.cloned.1.call-done = (f32[192,2560]{1,0:T(8,128)}, f32[192,1536]{1,0:T(8,128)}, f32[3,192,2048]{2,1,0:T(8,128)}, f32[3,128,1536]{2,1,0:T(8,128)}) async-done(((f32[192,2560]{1,0:T(8,128)}, f32[192,1536]{1,0:T(8,128)}, f32[3,192,2048]{2,1,0:T(8,128)}, f32[3,128,1536]{2,1,0:T(8,128)}), (f32[192,2560]{1,0:T(8,128)}, f32[192,1536]{1,0:T(8,128)}, f32[3,192,2048]{2,1,0:T(8,128)}, ...) | async-done | bytes 10223632 | tf_op jit(solution)/shard_map/psum | solution.py:343
  1912.2 17.0 psum.55
  (546 shorter events, 532.9 us)
Async XLA Ops:
  7.2 94.5 %all-gather.7.cloned.1.call-start = ((), (), s32[]{:S(2)}) async-start(), calls=%async_computation.6 | async-start | bytes 8847360 | tf_op jit(solution)/shard_map/all_gather | solution.py:33
  10.0 147.2 %all-gather.9.cloned.1.call-start = ((), (), s32[]{:S(2)}) async-start(), calls=%async_computation.7 | async-start | bytes 5308416 | tf_op jit(solution)/shard_map/all_gather | solution.py:34
  10.9 301.9 %all-gather.11.cloned.1.call-start = ((), (), s32[]{:S(2)}) async-start(), calls=%async_computation.8 | async-start | bytes 21233664 | tf_op jit(solution)/shard_map/all_gather | solution.py:36
  15.1 31.0 %copy-start.27 = (bf16[2,1,512,1536]{3,2,1,0:T(8,128)(2,1)S(1)}, bf16[2,1,512,1536]{3,2,1,0:T(8,128)(2,1)}, u32[]{:S(2)}) copy-start(bf16[2,1,512,1536]{3,2,1,0:T(8,128)(2,1)} %param.24) | copy-start | bytes 9437188
  15.1 388.7 %all-gather.13.cloned.1.call-start = ((), (), s32[]{:S(2)}) async-start(), calls=%async_computation.9 | async-start | bytes 10616832 | tf_op jit(solution)/shard_map/all_gather | solution.py:37
  18.2 987.6 %reduce-scatter.13.cloned.1.call-start = ((), (), s32[]{:S(2)}) async-start(), calls=%async_computation.11 | async-start | bytes 10616832 | tf_op jit(solution)/shard_map/reduce_scatter | solution.py:56
  20.1 29.5 %copy-start.119 = (pred[512]{0:T(512)(128)(4,1)}, pred[512]{0:T(512)(128)(4,1)S(1)}, u32[]{:S(2)}) copy-start(pred[512]{0:T(512)(128)(4,1)S(1)} %get-tuple-element.264) | copy-start | bytes 1540
  22.2 121.1 %copy-start.42 = (pred[512,512]{0,1:T(8,128)(4,1)}, pred[512,512]{0,1:T(8,128)(4,1)S(1)}, u32[]{:S(2)}) copy-start(pred[512,512]{0,1:T(8,128)(4,1)S(1)} %fusion.83) | copy-start | bytes 786436
  25.3 183.9 %copy-start.104 = (pred[1,1,512,2]{2,3,1,0:T(4,128)(4,1)}, pred[1,1,512,2]{2,3,1,0:T(4,128)(4,1)S(1)}, u32[]{:S(2)}) copy-start(pred[1,1,512,2]{2,3,1,0:T(4,128)(4,1)S(1)} %get-tuple-element.195) | copy-start | bytes 3076
  46.2 55.5 %copy-start.88 = (f32[1536]{0:T(1024)}, f32[1536]{0:T(1024)S(1)}, u32[]{:S(2)}) copy-start(f32[1536]{0:T(1024)S(1)} %get-tuple-element.157) | copy-start | bytes 18436
  49.7 33.5 %copy-start.10 = (f32[512,1536]{1,0:T(8,128)}, f32[512,1536]{1,0:T(8,128)S(1)}, u32[]{:S(2)}) copy-start(f32[512,1536]{1,0:T(8,128)S(1)} %get-tuple-element.215) | copy-start | bytes 9437188
  77.7 109.8 %copy-start.84 = (bf16[1536,3]{0,1:T(4,128)(2,1)}, bf16[1536,3]{0,1:T(4,128)(2,1)S(1)}, u32[]{:S(2)}) copy-start(bf16[1536,3]{0,1:T(4,128)(2,1)S(1)} %reshape.867) | copy-start | bytes 27652
  236.5 76.3 %copy-start.5 = (bf16[960,1536]{1,0:T(8,128)(2,1)S(1)}, bf16[960,1536]{1,0:T(8,128)(2,1)}, u32[]{:S(2)}) copy-start(bf16[960,1536]{1,0:T(8,128)(2,1)} %slice.154) | copy-start | bytes 8847364
  497.7 32.2 %copy-start.94 = (f32[512,3]{0,1:T(4,128)}, f32[512,3]{0,1:T(4,128)S(1)}, u32[]{:S(2)}) copy-start(f32[512,3]{0,1:T(4,128)S(1)} %select_reduce_fusion.1) | copy-start | bytes 18436
  497.8 32.1 %copy-start.124 = (f32[512]{0:T(512)}, f32[512]{0:T(512)S(1)}, u32[]{:S(2)}) copy-start(f32[512]{0:T(512)S(1)} %multiply_reduce_fusion.17) | copy-start | bytes 6148
  497.8 32.1 %copy-start.17 = (f32[512,1536]{1,0:T(8,128)S(1)}, f32[512,1536]{1,0:T(8,128)}, u32[]{:S(2)}) copy-start(f32[512,1536]{1,0:T(8,128)} %copy-done.16) | copy-start | bytes 9437188
  497.8 32.1 %copy-start.19 = (f32[512,1536]{1,0:T(8,128)S(1)}, f32[512,1536]{1,0:T(8,128)}, u32[]{:S(2)}) copy-start(f32[512,1536]{1,0:T(8,128)} %get-tuple-element.252) | copy-start | bytes 9437188
  497.8 32.1 %copy-start.85 = (bf16[1536,3]{0,1:T(4,128)(2,1)S(1)}, bf16[1536,3]{0,1:T(4,128)(2,1)}, u32[]{:S(2)}) copy-start(bf16[1536,3]{0,1:T(4,128)(2,1)} %copy-done.84) | copy-start | bytes 27652
  497.8 32.1 %copy-start.87 = (f32[1536]{0:T(1024)S(1)}, f32[1536]{0:T(1024)}, u32[]{:S(2)}) copy-start(f32[1536]{0:T(1024)} %get-tuple-element.156) | copy-start | bytes 18436
  497.8 32.1 %copy-start.92 = (f32[512,3]{0,1:T(4,128)S(1)}, f32[512,3]{0,1:T(4,128)}, u32[]{:S(2)}) copy-start(f32[512,3]{0,1:T(4,128)} %copy-done.91) | copy-start | bytes 18436
  497.8 32.1 %copy-start.110 = (f32[512]{0:T(512)S(1)}, f32[512]{0:T(512)}, u32[]{:S(2)}) copy-start(f32[512]{0:T(512)} %copy-done.109) | copy-start | bytes 6148
  535.4 180.2 %copy-start.98 = (f32[512,3]{0,1:T(4,128)}, f32[512,3]{0,1:T(4,128)S(1)}, u32[]{:S(2)}) copy-start(f32[512,3]{0,1:T(4,128)S(1)} %fusion.97) | copy-start | bytes 18436
  683.2 32.3 %copy-start.100 = (f32[512,3]{0,1:T(4,128)}, f32[512,3]{0,1:T(4,128)S(1)}, u32[]{:S(2)}) copy-start(f32[512,3]{0,1:T(4,128)S(1)} %select_reduce_fusion) | copy-start | bytes 18436
  683.3 32.3 %copy-start.133 = (f32[512]{0:T(512)}, f32[512]{0:T(512)S(1)}, u32[]{:S(2)}) copy-start(f32[512]{0:T(512)S(1)} %multiply_reduce_fusion.16) | copy-start | bytes 6148
  683.3 32.3 %copy-start.20 = (f32[512,1536]{1,0:T(8,128)S(1)}, f32[512,1536]{1,0:T(8,128)}, u32[]{:S(2)}) copy-start(f32[512,1536]{1,0:T(8,128)} %get-tuple-element.252) | copy-start | bytes 9437188
  683.3 36.9 %copy-start.38 = (f32[512,1536]{1,0:T(8,128)S(1)}, f32[512,1536]{1,0:T(8,128)}, u32[]{:S(2)}) copy-start(f32[512,1536]{1,0:T(8,128)} %get-tuple-element.253) | copy-start | bytes 9437188
  734.5 331.2 %reduce-scatter.11.cloned.1.call-start = ((), (), s32[]{:S(2)}) async-start(), calls=%async_computation.10 | async-start | bytes 17694720 | tf_op jit(solution)/shard_map/reduce_scatter | solution.py:55
  908.0 346.4 %reduce-scatter.17.cloned.1.call-start = ((), (), s32[]{:S(2)}) async-start(), calls=%async_computation.13 | async-start | bytes 21233664 | tf_op jit(solution)/shard_map/reduce_scatter | solution.py:59
  933.8 686.3 %reduce-scatter.15.cloned.1.call-start = ((), (), s32[]{:S(2)}) async-start(), calls=%async_computation.12 | async-start | bytes 42467328 | tf_op jit(solution)/shard_map/reduce_scatter | solution.py:58
  981.8 671.2 %reduce-scatter.19.cloned.1.call-start = ((), (), s32[]{:S(2)}) async-start(), calls=%async_computation.14 | async-start | bytes 884736
  1003.6 681.9 %reduce-scatter.21.cloned.1.call-start = ((), (), s32[]{:S(2)}) async-start(), calls=%async_computation.15 | async-start | bytes 884736
  1005.7 885.8 %all-reduce.8.cloned.1.call-start = ((), (), s32[]{:S(2)}) async-start(), calls=%async_computation.16 | async-start | bytes 20447232 | tf_op jit(solution)/shard_map/psum | solution.py:343
  (149 other events, 1398.8 us)
Sparse Core Ops, SparseCore 0:
  10.3 80.4 all-gather.6
  93.0 50.4 all-gather.8
  145.7 167.0 all-gather.10
  314.9 88.8 all-gather.12
  734.7 97.9 reduce-scatter.12
  908.1 157.5 reduce-scatter.10
  1068.0 186.3 reduce-scatter.16
  1256.8 363.2 reduce-scatter.14
  1623.1 29.8 reduce-scatter.18
  1655.7 29.7 reduce-scatter.20
  1690.1 201.2 all-reduce.7
where the time goes:
time: 1980 us; the launch traced here: 1970 us
  waiting for transfers between devices  1010 us (51%)
  matrix products  383 us (19%)
  other arithmetic  265 us (13%)
  local copies, waits for them, and re-layouts  242 us (12%)
  blocking collectives  53.9 us (3%)
  between operations  20.2 us (1%)
    reduce_scatter x1, waiting for transfers between devices, reduce_whole(): lax.psum_scatter(new_grads[4], 'fsdp', scatter_dimension=1, tiled=True)  366 us
    psum x1, waiting for transfers between devices, per_device(): lax.psum((running[0], running[1], running[2], running[3], running[4], run...  192 us
    reduce_scatter x1, waiting for transfers between devices, reduce_whole(): lax.psum_scatter(new_grads[5], 'fsdp', scatter_dimension=1, tiled=True)  189 us
    all_gather x1, waiting for transfers between devices, gather_forward(): lax.all_gather(low_parts[5], 'fsdp', axis=1, tiled=True)  78.8 us
    all_gather x1, waiting for transfers between devices, gather_forward(): lax.all_gather(low_parts[4], 'fsdp', axis=1, tiled=True)  66.9 us
    reduce_sum x2, other arithmetic, backward_pass(): d_normed_two = jnp.sum(d_flat[target] * keep_mask[:, :, None], axis=1)  64.2 us
    reduce_scatter x1, waiting for transfers between devices, reduce_whole(): lax.psum_scatter(new_grads[1], 'fsdp', scatter_dimension=0, tiled=True)  59.9 us
    unnamed x13, waiting for transfers between devices  53.8 us
  transfers between devices with their start and end apart: 11, of which 8 were waited for; matrix products, arithmetic and copies ran while one was open for 24% of the time, Pallas kernels for 0%

commit v1 on v0

v1 whole, which is shorter than its diff:
```python
import functools

import jax
import jax.numpy as jnp
from jax import lax
from jax.experimental import pallas as pl
from jax.experimental.pallas import tpu as pltpu
from jax.sharding import PartitionSpec as P

QUERY_HEADS = 24
KEY_VALUE_HEADS = 8
HEAD_SIZE = 64
FE = 1024
E = 3
STEP = 10
CAP = 320
BLK = 512

epsilon = 1e-06
beta_first = 0.9
beta_second = 0.95
learn_rate = 0.02
weight_decay = 0.1
adam_floor = 1e-08
clip_level = 0.005

bf16 = jnp.bfloat16
f32 = jnp.float32

LAST = (((1,), (1,)), ((), ()))
FIRST = (((0,), (0,)), ((), ()))


def dot(a, b):
    return jnp.dot(a, b, preferred_element_type=f32)


def dot_last(a, b):
    return lax.dot_general(a, b, LAST, preferred_element_type=f32)


def dot_first(a, b):
    return lax.dot_general(a, b, FIRST, preferred_element_type=f32)


def params(mib=56):
    return pltpu.CompilerParams(vmem_limit_bytes=mib * 1024 * 1024)


def cost(flops, nbytes):
    return pl.CostEstimate(flops=int(flops), bytes_accessed=int(nbytes), transcendentals=0)


def whole(shape, space=None):
    zeros = (0,) * len(shape)
    return pl.BlockSpec(shape, lambda *_: zeros, pipeline_mode=pl.Buffered(1))


def round_up(n, m):
    return -(-n // m) * m


def shift_core_pairs(x, k):
    size = lax.axis_size("fsdp")
    return lax.ppermute(x, "fsdp", [(i, (i + 2 * k) % size) for i in range(size)])


def swap_core(x):
    size = lax.axis_size("fsdp")
    return lax.ppermute(x, "fsdp", [(i, i ^ 1) for i in range(size)])


def swap_replica(x, bit):
    size = lax.axis_size("replica")
    return lax.ppermute(x, "replica", [(i, i ^ bit) for i in range(size)])


def bit_order(first):
    bits = []
    while (1 << len(bits)) < lax.axis_size("replica"):
        bits.append(1 << len(bits))
    return bits[first % len(bits) :] + bits[: first % len(bits)]


def assemble_kernel(masks, places, idx_ref, *refs):
    n_in = 6
    ins, out, sems = refs[:n_in], refs[n_in], refs[n_in + 1]
    own, low, high, own_c, low_c, high_c = ins
    held = refs[n_in + 2]
    part, z, c = idx_ref[0], idx_ref[1], idx_ref[2]
    half = len(masks) // 2
    rows = low.shape[2]
    n_z = places + 1
    copies = []
    for group, core in (((own, low, high), c), ((own_c, low_c, high_c), 1 - c)):
        copies.append((group[0], held.at[2 * z + core]))
        for j, mask in enumerate(masks):
            source = group[1] if j < half else group[2]
            at = pl.multiple_of((part ^ mask) * rows, 16)
            for k in range(1, n_z):
                zk = lax.rem(z + n_z - k, n_z)
                copies.append((source.at[j % half, k - 1], held.at[2 * zk + core, pl.ds(at, rows)]))
    started = []
    for i, (source, target) in enumerate(copies):
        copy = pltpu.make_async_copy(source, target, sems.at[i])
        copy.start()
        started.append(copy)
    for copy in started:
        copy.wait()
    copy = pltpu.make_async_copy(held, out, sems.at[len(copies)])
    copy.start()
    copy.wait()


def gather_packed(shard, first):
    n_rep, n_f = lax.axis_size("replica"), lax.axis_size("fsdp")
    n_z = n_f // 2
    rows = shard.shape[0] // n_rep
    part, place = lax.axis_index("replica"), lax.axis_index("fsdp")
    own_c = swap_core(shard)
    mine = lax.dynamic_slice_in_dim(shard, part * rows, rows, axis=0)
    stack = jnp.stack([shift_core_pairs(mine, k) for k in range(1, n_z)])[None]
    masks = [0]
    order = bit_order(first)
    for i, bit in enumerate(order):
        received = swap_replica(stack, bit)
        masks = masks + [m ^ bit for m in masks]
        if i < len(order) - 1:
            stack = jnp.concatenate([stack, received])
    low, high = stack, received
    low_c, high_c = swap_core(low), swap_core(high)
    idx = jnp.stack([part, place // 2, place % 2]).astype(jnp.int32)
    anyspec = pl.BlockSpec(memory_space=pl.ANY)
    n_copies = 2 * (1 + n_rep * (n_z - 1))
    return pl.pallas_call(
        functools.partial(assemble_kernel, tuple(masks), n_z - 1),
        out_shape=jax.ShapeDtypeStruct((n_f,) + shard.shape, bf16),
        grid_spec=pltpu.PrefetchScalarGridSpec(
            num_scalar_prefetch=1,
            grid=(1,),
            in_specs=[anyspec] * 6,
            out_specs=anyspec,
            scratch_shapes=[
                pltpu.SemaphoreType.DMA((n_copies + 1,)),
                pltpu.VMEM((n_f,) + shard.shape, bf16),
            ],
        ),
        compiler_params=params(),
        cost_estimate=cost(0, 4 * n_f * shard.size),
        name="assemble",
    )(idx, shard, low, high, own_c, low_c, high_c)


def reduce_packed(keep, send, first):
    n_rep, n_z = lax.axis_size("replica"), lax.axis_size("fsdp") // 2
    part, place = lax.axis_index("replica"), lax.axis_index("fsdp")
    z = place // 2
    rows = keep.shape[1] // n_rep
    order = bit_order(first)
    n_bits = len(order)
    shape = (n_z,) + (2,) * n_bits + (rows, BLK)
    bits = [1 << b for b in range(n_bits)]
    live = list(reversed(bits))
    terms = [keep.reshape(shape), swap_core(send).reshape(shape)]

    def part_sum(index, axis):
        return functools.reduce(
            jnp.add, [lax.dynamic_index_in_dim(t, index, axis, keepdims=False).astype(f32) for t in terms]
        )

    for bit in order:
        axis = 1 + live.index(bit)
        live.remove(bit)
        own = (part // bit) % 2
        got = swap_replica(part_sum(1 - own, axis).astype(bf16), bit)
        terms = [lax.dynamic_index_in_dim(t, own, axis, keepdims=False) for t in terms] + [got]
    gots = [shift_core_pairs(part_sum((z + k) % n_z, 0).astype(bf16), k) for k in range(1, n_z)]
    summed = part_sum(z, 0)
    for got in gots:
        summed = summed + got.astype(f32)
    stack = summed.astype(bf16)
    done = []
    for bit in order:
        got = swap_replica(stack, bit)
        own = (part // bit) % 2
        pair = jnp.stack([stack, got])
        stack = jnp.where(own == 1, pair[::-1], pair)
    names = list(reversed(order))
    stack = jnp.transpose(stack, tuple(names.index(b) for b in reversed(bits)) + (n_bits, n_bits + 1))
    return stack.reshape(n_rep * rows, BLK)


def sum_small(x):
    size = lax.axis_size("fsdp")
    bit = 1
    while bit < size:
        x = x + lax.ppermute(x, "fsdp", [(i, i ^ bit) for i in range(size)])
        bit *= 2
    return x


def sum_all(x):
    x = sum_small(x)
    bit = 1
    while bit < lax.axis_size("replica"):
        x = x + swap_replica(x, bit)
        bit *= 2
    return x


def pack_kernel(counts, *refs):
    out = refs[-1]
    at = 0
    for ref, n in zip(refs, counts):
        value = ref[0] if len(ref.shape) == 3 else ref[...]
        for j in range(n):
            out[at : at + value.shape[0], :] = value[:, j * BLK : (j + 1) * BLK].astype(bf16)
            at += value.shape[0]
    if len(refs) - 1 > len(counts):
        extra = refs[len(counts)][...]
        out[at : at + extra.shape[0], :] = extra
        at += extra.shape[0]
    if at < out.shape[0]:
        out[at:, :] = jnp.zeros((out.shape[0] - at, BLK), bf16)


def pack_call(parts, unit, extra=None):
    specs, counts, total = [], [], 0
    for w, e in parts:
        if e is None:
            specs.append(pl.BlockSpec(w.shape, lambda i: (0, 0)))
        else:
            specs.append(pl.BlockSpec((1,) + w.shape[1:], lambda i, e=e: (e, 0, 0)))
        counts.append(w.shape[-1] // BLK)
        total += counts[-1] * w.shape[-2]
    args = [w for w, _ in parts]
    if extra is not None:
        args.append(extra)
        specs.append(pl.BlockSpec(extra.shape, lambda i: (0, 0)))
        total += extra.shape[0]
    total = round_up(total, unit)
    return pl.pallas_call(
        functools.partial(pack_kernel, tuple(counts)),
        grid=(1,),
        in_specs=specs,
        out_specs=pl.BlockSpec((total, BLK), lambda i: (0, 0)),
        out_shape=jax.ShapeDtypeStruct((total, BLK), bf16),
        compiler_params=params(),
        cost_estimate=cost(0, 6 * total * BLK),
        name="pack",
    )(*args)


def pad_rows(x, rows):
    return jnp.pad(x, ((0, rows - x.shape[0]), (0, 0)))


def qkv_kernel(x_ref, gain_ref, w_ref, qkv_ref, n1_ref):
    tokens, width = x_ref.shape

    @pl.when(pl.program_id(0) == 0)
    def _():
        def body(i, _):
            rows = pl.ds(pl.multiple_of(i * 128, 128), 128)
            xf = x_ref[rows, :].astype(f32)
            scale = lax.rsqrt(jnp.mean(xf * xf, axis=-1, keepdims=True) + epsilon)
            n1_ref[rows, :] = (xf * scale * gain_ref[...]).astype(bf16)
            return 0

        lax.fori_loop(0, tokens // 128, body, 0)

    w = w_ref[...].reshape(width, BLK)

    def body(i, _):
        rows = pl.ds(pl.multiple_of(i * 256, 256), 256)
        qkv_ref[rows, :] = dot(n1_ref[rows, :], w).astype(bf16)
        return 0

    lax.fori_loop(0, tokens // 256, body, 0)


def qkv_call(x, gain, w_in, rows, n):
    tokens, width = x.shape
    n_f = w_in.shape[0]
    return pl.pallas_call(
        qkv_kernel,
        grid=(n,),
        in_specs=[
            whole((tokens, width)),
            whole((1, width)),
            pl.BlockSpec((n_f, rows, BLK), lambda j: (0, j, 0)),
        ],
        out_specs=[
            pl.BlockSpec((tokens, BLK), lambda j: (0, j)),
            pl.BlockSpec((tokens, width), lambda j: (0, 0)),
        ],
        out_shape=[
            jax.ShapeDtypeStruct((tokens, n * BLK), bf16),
            jax.ShapeDtypeStruct((tokens, width), bf16),
        ],
        compiler_params=params(),
        cost_estimate=cost(2 * tokens * width * n * BLK, 2 * width * n * BLK + 4 * tokens * width),
        name="qkv",
    )(x, gain, w_in)


HALF = 256


def attention_kernel(len_ref, q_ref, k_ref, v_ref, p_ref, mix_ref):
    seq = q_ref.shape[0]
    length = len_ref[pl.program_id(0)]
    key = lax.broadcasted_iota(jnp.int32, (seq, seq), 0)
    query = lax.broadcasted_iota(jnp.int32, (seq, seq), 1)
    bias = jnp.where((key <= query) & (key < length), 0.0, -1000000000.0).astype(f32)
    group = QUERY_HEADS // KEY_VALUE_HEADS
    for h in range(2 * group):
        g = h // group
        lanes = slice(h * HEAD_SIZE, (h + 1) * HEAD_SIZE)
        kv = slice(g * HEAD_SIZE, (g + 1) * HEAD_SIZE)
        q = q_ref[:, lanes] * jnp.asarray(HEAD_SIZE ** (-0.5), bf16)
        for start in range(0, seq, HALF):
            stop = start + HALF
            s = dot_last(k_ref[:stop, kv], q[start:stop]) + bias[:stop, start:stop]
            raised = jnp.exp(s - jnp.max(s, axis=0, keepdims=True))
            probs = (raised * (1.0 / jnp.sum(raised, axis=0, keepdims=True))).astype(bf16)
            p_ref[0, h, :stop, start:stop] = probs
            if stop < seq:
                p_ref[0, h, stop:, start:stop] = jnp.zeros((seq - stop, HALF), bf16)
            mixed = dot_first(v_ref[:stop, kv], probs)
            mix_ref[start:stop, lanes] = mixed.T.astype(bf16)


def attention_call(lengths, qkv, n_seq):
    tokens = qkv.shape[0]
    seq = tokens // n_seq
    pairs = KEY_VALUE_HEADS // 2
    heads = QUERY_HEADS // pairs
    qw = heads * HEAD_SIZE
    kw = 2 * HEAD_SIZE
    k_at = QUERY_HEADS * HEAD_SIZE // kw
    v_at = k_at + pairs
    return pl.pallas_call(
        attention_kernel,
        grid_spec=pltpu.PrefetchScalarGridSpec(
            num_scalar_prefetch=1,
            grid=(n_seq, pairs),
            in_specs=[
                pl.BlockSpec((seq, qw), lambda s, j, _: (s, j)),
                pl.BlockSpec((seq, kw), lambda s, j, _: (s, k_at + j)),
                pl.BlockSpec((seq, kw), lambda s, j, _: (s, v_at + j)),
            ],
            out_specs=[
                pl.BlockSpec((1, heads, seq, seq), lambda s, j, _: (s, j, 0, 0)),
                pl.BlockSpec((seq, qw), lambda s, j, _: (s, j)),
            ],
        ),
        out_shape=[
            jax.ShapeDtypeStruct((n_seq, QUERY_HEADS, seq, seq), bf16),
            jax.ShapeDtypeStruct((tokens, QUERY_HEADS * HEAD_SIZE), bf16),
        ],
        compiler_params=params(),
        cost_estimate=cost(16 * n_seq * QUERY_HEADS * seq * seq * HEAD_SIZE, 2 * n_seq * QUERY_HEADS * seq * seq),
        name="attention",
    )(lengths, qkv, qkv, qkv)


def attention_back_kernel(q_ref, k_ref, v_ref, p_ref, mix_ref, dmix_ref, dq_ref, dk_ref, dv_ref):
    seq = q_ref.shape[0]
    group = QUERY_HEADS // KEY_VALUE_HEADS
    scale = HEAD_SIZE ** (-0.5)
    ones = jnp.ones((8, HEAD_SIZE), bf16)
    for g in range(2):
        kv = slice(g * HEAD_SIZE, (g + 1) * HEAD_SIZE)
        k, v = k_ref[:, kv], v_ref[:, kv]
        n_half = seq // HALF
        dk = [jnp.zeros((HALF, HEAD_SIZE), f32) for _ in range(n_half)]
        dv = [jnp.zeros((HALF, HEAD_SIZE), f32) for _ in range(n_half)]
        for i in range(group):
            h = g * group + i
            lanes = slice(h * HEAD_SIZE, (h + 1) * HEAD_SIZE)
            for start in range(0, seq, HALF):
                stop = start + HALF
                dmix = dmix_ref[start:stop, lanes]
                q = q_ref[start:stop, lanes]
                both = dmix.astype(f32) * mix_ref[start:stop, lanes].astype(f32)
                high = both.astype(bf16)
                low = (both - high.astype(f32)).astype(bf16)
                delta = (dot_last(ones, high) + dot_last(ones, low))[:1]
                probs = p_ref[0, h, :stop, start:stop]
                dp = dot_last(v[:stop], dmix)
                ds = (probs.astype(f32) * (dp - delta)).astype(bf16)
                dq = dot_first(k[:stop], ds)
                dq_ref[start:stop, lanes] = (dq.T * scale).astype(bf16)
                dk_part = dot(ds, q)
                dv_part = dot(probs, dmix)
                for m in range(stop // HALF):
                    rows = slice(m * HALF, (m + 1) * HALF)
                    dk[m] += dk_part[rows]
                    dv[m] += dv_part[rows]
        for m in range(n_half):
            rows = slice(m * HALF, (m + 1) * HALF)
            dk_ref[rows, kv] = (dk[m] * scale).astype(bf16)
            dv_ref[rows, kv] = dv[m].astype(bf16)


def attention_back_call(qkv, probs, mixed, dmixed, n_seq):
    tokens = qkv.shape[0]
    seq = tokens // n_seq
    pairs = KEY_VALUE_HEADS // 2
    heads = QUERY_HEADS // pairs
    qw = heads * HEAD_SIZE
    kw = 2 * HEAD_SIZE
    k_at = QUERY_HEADS * HEAD_SIZE // kw
    v_at = k_at + pairs
    qspec = pl.BlockSpec((seq, qw), lambda s, j: (s, j))
    kspec = pl.BlockSpec((seq, kw), lambda s, j: (s, j))
    return pl.pallas_call(
        attention_back_kernel,
        grid=(n_seq, pairs),
        in_specs=[
            qspec,
            pl.BlockSpec((seq, kw), lambda s, j: (s, k_at + j)),
            pl.BlockSpec((seq, kw), lambda s, j: (s, v_at + j)),
            pl.BlockSpec((1, heads, seq, seq), lambda s, j: (s, j, 0, 0)),
            qspec,
            qspec,
        ],
        out_specs=[qspec, kspec, kspec],
        out_shape=[
            jax.ShapeDtypeStruct((tokens, QUERY_HEADS * HEAD_SIZE), bf16),
            jax.ShapeDtypeStruct((tokens, KEY_VALUE_HEADS * HEAD_SIZE), bf16),
            jax.ShapeDtypeStruct((tokens, KEY_VALUE_HEADS * HEAD_SIZE), bf16),
        ],
        compiler_params=params(),
        cost_estimate=cost(32 * n_seq * QUERY_HEADS * seq * seq * HEAD_SIZE, 2 * n_seq * QUERY_HEADS * seq * seq),
        name="attention_back",
    )(qkv, qkv, qkv, probs, mixed, dmixed)


TILE = 256


def resid_kernel(rows, n, mix_ref, w_ref, x_ref, gain_ref, router_ref, resid_ref, n2_ref, prob_ref):
    width = x_ref.shape[1]
    mixed = mix_ref[...]
    squares = jnp.zeros((TILE, 1), f32)
    for j in range(n):
        cols = slice(j * BLK, (j + 1) * BLK)
        w = w_ref[:, j * rows : (j + 1) * rows, :].reshape(-1, BLK)
        part = x_ref[:, cols].astype(f32) + dot(mixed, w)
        resid_ref[:, cols] = part
        squares += jnp.sum(part * part, axis=-1, keepdims=True)
    scale = lax.rsqrt(squares * (1.0 / width) + epsilon)
    n2 = (resid_ref[...] * scale * gain_ref[...]).astype(bf16)
    n2_ref[...] = n2
    logits = dot_last(router_ref[...], n2)
    logits = jnp.where(lax.broadcasted_iota(jnp.int32, logits.shape, 0) < E, logits, -1e30)
    raised = jnp.exp(logits - jnp.max(logits, axis=0, keepdims=True))
    prob_ref[...] = raised / jnp.sum(raised, axis=0, keepdims=True)


def resid_call(mixed, w_out, x, gain, router, rows, n):
    tokens, width = x.shape
    tile = pl.BlockSpec((TILE, width), lambda i: (i, 0))
    return pl.pallas_call(
        functools.partial(resid_kernel, rows, n),
        grid=(tokens // TILE,),
        in_specs=[
            tile,
            whole((w_out.shape[0], n * rows, BLK)),
            tile,
            whole((1, width)),
            whole((8, width)),
        ],
        out_specs=[tile, tile, pl.BlockSpec((8, TILE), lambda i: (0, i))],
        out_shape=[
            jax.ShapeDtypeStruct((tokens, width), f32),
            jax.ShapeDtypeStruct((tokens, width), bf16),
            jax.ShapeDtypeStruct((8, tokens), f32),
        ],
        compiler_params=params(),
        cost_estimate=cost(2 * tokens * width * width, 2 * width * width + 12 * tokens * width),
        name="resid",
    )(mixed, w_out, x, gain, router)


def dispatch_kernel(slot_ref, prob_ref, n2_ref, cot_ref, buf_ref, dys_ref, gate_ref):
    e = pl.program_id(1)
    slots = slot_ref[0, pl.ds(e, 1), :]
    hit = lax.broadcasted_iota(jnp.int32, (CAP, slots.shape[1]), 0) == slots
    gate = jnp.sum(jnp.where(hit, prob_ref[pl.ds(e, 1), :], 0.0), axis=-1, keepdims=True)
    gate_ref[0, 0] = jnp.broadcast_to(gate, (CAP, 128))
    hit = jnp.where(hit, 1.0, 0.0).astype(bf16)
    buf_ref[0, 0] = dot(hit, n2_ref[...]).astype(bf16)
    dys_ref[0, 0] = dot(hit, cot_ref[...]).astype(bf16)


def dispatch_call(slots, prob, n2, cot, n_seq):
    tokens, width = n2.shape
    seq = tokens // n_seq
    out = pl.BlockSpec((1, 1, CAP, width), lambda s, e: (e, s, 0, 0))
    return pl.pallas_call(
        dispatch_kernel,
        grid=(n_seq, E),
        in_specs=[
            pl.BlockSpec((1, 8, seq), lambda s, e: (s, 0, 0)),
            pl.BlockSpec((8, seq), lambda s, e: (0, s)),
            pl.BlockSpec((seq, width), lambda s, e: (s, 0)),
            pl.BlockSpec((seq, width), lambda s, e: (s, 0)),
        ],
        out_specs=[out, out, pl.BlockSpec((1, 1, CAP, 128), lambda s, e: (e, s, 0, 0))],
        out_shape=[
            jax.ShapeDtypeStruct((E, n_seq, CAP, width), bf16),
            jax.ShapeDtypeStruct((E, n_seq, CAP, width), bf16),
            jax.ShapeDtypeStruct((E, n_seq, CAP, 128), f32),
        ],
        compiler_params=params(),
        cost_estimate=cost(4 * E * CAP * tokens * width, 20 * tokens * width),
        name="dispatch",
    )(slots, prob, n2, cot)


def split_cores(block, c, rows):
    parts = block.reshape(-1, 2, rows, block.shape[-1])
    even, odd = parts[:, 0], parts[:, 1]
    return (
        jnp.where(c == 0, even, odd).astype(bf16),
        jnp.where(c == 0, odd, even).astype(bf16),
    )


def expert_kernel(
    e,
    up_rows,
    down_rows,
    idx_ref,
    buf_ref,
    dys_ref,
    gate_ref,
    slot_ref,
    up_a_ref,
    up_b_ref,
    down_ref,
    yg_ref,
    dbuf_ref,
    dgate_ref,
    keep_ref,
    send_ref,
    y_acc,
    d_acc,
    dyexp_ref,
    hid_ref,
    da_ref,
    db_ref,
    dg_acc,
    up_held,
    down_held,
    sems,
):
    h = pl.program_id(0)
    last = pl.num_programs(0) - 1
    c = idx_ref[0]
    n_seq = buf_ref.shape[1]
    width = buf_ref.shape[3]
    n_d = width // BLK
    up_a = up_a_ref[...].reshape(width, BLK)
    up_b = up_b_ref[...].reshape(width, BLK)
    downs = [down_ref[:, j * down_rows : (j + 1) * down_rows, :].reshape(BLK, BLK) for j in range(n_d)]
    for s in range(n_seq):
        rows = slice(s * CAP, (s + 1) * CAP)
        gate = gate_ref[0, s, :, :1]

        @pl.when(h == 0)
        def _():
            dyexp_ref[rows, :] = (gate * dys_ref[0, s].astype(f32)).astype(bf16)

        x = buf_ref[0, s]
        a = dot(x, up_a)
        b = dot(x, up_b)
        sigma = jax.nn.sigmoid(a)
        silu = a * sigma
        hid = (silu * b).astype(bf16)
        hid_ref[rows, :] = hid
        du = dot_last(dys_ref[0, s, :, :BLK], downs[0])
        for j in range(1, n_d):
            du += dot_last(dys_ref[0, s, :, j * BLK : (j + 1) * BLK], downs[j])
        dg = jnp.sum(du * hid.astype(f32), axis=-1, keepdims=True)
        dh = gate * du
        da = (dh * b * sigma * (1.0 + a * (1.0 - sigma))).astype(bf16)
        db = (dh * silu).astype(bf16)
        da_ref[rows, :] = da
        db_ref[rows, :] = db

        @pl.when(h == 0)
        def _():
            dg_acc[rows, :] = jnp.broadcast_to(dg, (CAP, 128))
            for j in range(n_d):
                y_acc[rows, j * BLK : (j + 1) * BLK] = dot(hid, downs[j])
            d_acc[rows, :] = dot_last(da, up_a) + dot_last(db, up_b)

        @pl.when(h > 0)
        def _():
            dg_acc[rows, :] += jnp.broadcast_to(dg, (CAP, 128))
            for j in range(n_d):
                y_acc[rows, j * BLK : (j + 1) * BLK] += dot(hid, downs[j])
            d_acc[rows, :] += dot_last(da, up_a) + dot_last(db, up_b)

        @pl.when(h == last)
        def _():
            yg_ref[s] = (gate * y_acc[rows, :]).astype(bf16)
            dbuf_ref[s] = d_acc[rows, :].astype(bf16)
            slots = slot_ref[s, e : e + 1, :]
            hit = lax.broadcasted_iota(jnp.int32, (CAP, slots.shape[1]), 0) == slots
            row = jnp.sum(jnp.where(hit, dg_acc[rows, :1], 0.0), axis=0, keepdims=True)
            dgate_ref[s] = jnp.broadcast_to(row, (8, slots.shape[1]))

    step = 384
    per = step // (2 * up_rows)

    for m in range(width // step):
        x = jnp.concatenate([buf_ref[0, s, :, m * step : (m + 1) * step] for s in range(n_seq)], axis=0)
        xt = x.T
        for i, d_ref in enumerate((da_ref, db_ref)):
            keep, send = split_cores(dot(xt, d_ref[...]), c, up_rows)
            up_held[h, 0, i, m * per : (m + 1) * per] = keep
            up_held[h, 1, i, m * per : (m + 1) * per] = send
    hid_t = hid_ref[...].T
    for j in range(n_d):
        keep, send = split_cores(dot(hid_t, dyexp_ref[:, j * BLK : (j + 1) * BLK]), c, down_rows)
        down_held[h, 0, :, j * down_rows : (j + 1) * down_rows, :] = keep
        down_held[h, 1, :, j * down_rows : (j + 1) * down_rows, :] = send
    n_h = FE // BLK
    n_zh = keep_ref.shape[0] // n_h

    def copies(step):
        found = []
        for side, ref in enumerate((keep_ref, send_ref)):
            for i in range(2):
                place = pl.ds((i * n_h + step) * up_rows, up_rows)
                found.append((up_held.at[step, side, i], ref.at[:, place, :]))
            place = pl.ds(2 * n_h * up_rows, n_d * down_rows)
            found.append((down_held.at[step, side], ref.at[step * n_zh : (step + 1) * n_zh, place, :]))
        return [pltpu.make_async_copy(a, b, sems.at[step, i]) for i, (a, b) in enumerate(found)]

    for step in range(n_h):

        @pl.when(h == step)
        def _():
            for copy in copies(step):
                copy.start()

    @pl.when(h == last)
    def _():
        for step in range(n_h):
            for copy in copies(step):
                copy.wait()


def expert_call(e, at, core, buf, dys, gates, slots, w, up_rows, down_rows, unit):
    _, n_seq, _, width = buf.shape
    n_f = w.shape[0]
    n_z = n_f // 2
    n_h = FE // BLK
    n_d = width // BLK
    seq = slots.shape[2]
    data = pl.BlockSpec((1, n_seq, CAP, width), lambda h, _: (e, 0, 0, 0), pipeline_mode=pl.Buffered(1))
    out = pl.BlockSpec((n_seq, CAP, width), lambda h, _: (0, 0, 0))
    anyspec = pl.BlockSpec(memory_space=pl.ANY)
    total = round_up(2 * n_h * up_rows + n_d * down_rows, unit)
    grad_shape = jax.ShapeDtypeStruct((n_z, total, BLK), bf16)
    rows = n_seq * CAP
    yg, dbuf, dgate, keep, send = pl.pallas_call(
        functools.partial(expert_kernel, e, up_rows, down_rows),
        grid_spec=pltpu.PrefetchScalarGridSpec(
            num_scalar_prefetch=1,
            grid=(n_h,),
            in_specs=[
                data,
                data,
                pl.BlockSpec((1, n_seq, CAP, 128), lambda h, _: (e, 0, 0, 0)),
                pl.BlockSpec((n_seq, 8, seq), lambda h, _: (0, 0, 0)),
                pl.BlockSpec((n_f, up_rows, BLK), lambda h, _: (0, at // up_rows + h, 0)),
                pl.BlockSpec((n_f, up_rows, BLK), lambda h, _: (0, at // up_rows + n_h + h, 0)),
                pl.BlockSpec(
                    (n_f // n_h, n_d * down_rows, BLK),
                    lambda h, _: (h, (at + 2 * n_h * up_rows) // (n_d * down_rows), 0),
                ),
            ],
            out_specs=[
                out,
                out,
                pl.BlockSpec((n_seq, 8, seq), lambda h, _: (0, 0, 0)),
                anyspec,
                anyspec,
            ],
            scratch_shapes=[
                pltpu.VMEM((rows, width), f32),
                pltpu.VMEM((rows, width), f32),
                pltpu.VMEM((rows, width), bf16),
                pltpu.VMEM((rows, BLK), bf16),
                pltpu.VMEM((rows, BLK), bf16),
                pltpu.VMEM((rows, BLK), bf16),
                pltpu.VMEM((rows, 128), f32),
                pltpu.VMEM((n_h, 2, 2, n_z, up_rows, BLK), bf16),
                pltpu.VMEM((n_h, 2, n_z // n_h, n_d * down_rows, BLK), bf16),
                pltpu.SemaphoreType.DMA((n_h, 6)),
            ],
        ),
        out_shape=[
            jax.ShapeDtypeStruct((n_seq, CAP, width), bf16),
            jax.ShapeDtypeStruct((n_seq, CAP, width), bf16),
            jax.ShapeDtypeStruct((n_seq, 8, seq), f32),
            grad_shape,
            grad_shape,
        ],
        compiler_params=params(60),
        cost_estimate=cost(18 * rows * width * FE, 40 * width * FE),
        name="expert",
    )(core, buf, dys, gates, slots, w, w, w)
    return yg, dbuf, dgate[:, 0], keep, send


def spread(col_ref, e):
    slots = col_ref[:, e : e + 1]
    hit = lax.broadcasted_iota(jnp.int32, (col_ref.shape[0], CAP), 1) == slots
    return jnp.where(hit, 1.0, 0.0).astype(bf16)


def combine_kernel(col_ref, resid_ref, y0_ref, y1_ref, y2_ref, out_ref):
    total = resid_ref[...]
    for e, y_ref in enumerate((y0_ref, y1_ref, y2_ref)):
        total += dot(spread(col_ref, e), y_ref[0])
    out_ref[...] = jnp.where(col_ref[:, E : E + 1] > 0, total, 0.0).astype(bf16)


def combine_call(cols, resid, ys, n_seq):
    tokens, width = resid.shape
    per = tokens // n_seq // TILE
    tile = pl.BlockSpec((TILE, width), lambda i: (i, 0))
    return pl.pallas_call(
        combine_kernel,
        grid=(tokens // TILE,),
        in_specs=[pl.BlockSpec((TILE, 8), lambda i: (i, 0)), tile]
        + [pl.BlockSpec((1, CAP, width), lambda i: (i // per, 0, 0))] * E,
        out_specs=tile,
        out_shape=jax.ShapeDtypeStruct((tokens, width), bf16),
        compiler_params=params(),
        cost_estimate=cost(2 * E * CAP * tokens * width, 12 * tokens * width),
        name="combine",
    )(cols, resid, *ys)


def hi_lo(x):
    high = x.astype(bf16)
    return high, (x - high.astype(f32)).astype(bf16)


def middle_kernel(
    rows,
    n,
    col_ref,
    d0_ref,
    d1_ref,
    d2_ref,
    prob_ref,
    dprob_ref,
    router_ref,
    n2_ref,
    resid_ref,
    cot_ref,
    gain_ref,
    w_ref,
    dresid_ref,
    dattn_ref,
    dmix_ref,
    small_ref,
):
    width = resid_ref.shape[1]

    @pl.when(pl.program_id(0) == 0)
    def _():
        small_ref[...] = jnp.zeros_like(small_ref)

    prob, dprob = prob_ref[...], dprob_ref[...]
    dlogit = prob * (dprob - jnp.sum(dprob * prob, axis=0, keepdims=True))
    high, low = hi_lo(dlogit)
    dn2 = dot_first(high, router_ref[...]) + dot_first(low, router_ref[...])
    for e, d_ref in enumerate((d0_ref, d1_ref, d2_ref)):
        dn2 += dot(spread(col_ref, e), d_ref[0])
    n2 = n2_ref[...]
    small_ref[:8, :] += dot(high, n2) + dot(low, n2)
    resid = resid_ref[...]
    scale = lax.rsqrt(jnp.mean(resid * resid, axis=-1, keepdims=True) + epsilon)
    small_ref[8:, :] += jnp.broadcast_to(jnp.sum(dn2 * resid * scale, axis=0, keepdims=True), (8, width))
    weighted = dn2 * gain_ref[...]
    along = jnp.mean(weighted * resid, axis=-1, keepdims=True)
    dy = jnp.where(col_ref[:, E : E + 1] > 0, cot_ref[...].astype(f32), 0.0)
    dresid = dy + scale * weighted - resid * (scale * scale * scale * along)
    dresid_ref[...] = dresid
    dattn = dresid.astype(bf16)
    dattn_ref[...] = dattn
    dmix = dot_last(dattn[:, :BLK], w_ref[:, :rows, :].reshape(-1, BLK))
    for j in range(1, n):
        w = w_ref[:, j * rows : (j + 1) * rows, :].reshape(-1, BLK)
        dmix += dot_last(dattn[:, j * BLK : (j + 1) * BLK], w)
    dmix_ref[...] = dmix.astype(bf16)


def middle_call(cols, ds, prob, dprob, router, n2, resid, cot, gain, w_out, rows, n, n_seq):
    tokens, width = resid.shape
    per = tokens // n_seq // TILE
    tile = pl.BlockSpec((TILE, width), lambda i: (i, 0))
    row8 = pl.BlockSpec((8, TILE), lambda i: (0, i))
    return pl.pallas_call(
        functools.partial(middle_kernel, rows, n),
        grid=(tokens // TILE,),
        in_specs=[pl.BlockSpec((TILE, 8), lambda i: (i, 0))]
        + [pl.BlockSpec((1, CAP, width), lambda i: (i // per, 0, 0))] * E
        + [
            row8,
            row8,
            whole((8, width)),
            tile,
            tile,
            tile,
            whole((1, width)),
            whole((w_out.shape[0], n * rows, BLK)),
        ],
        out_specs=[tile, tile, tile, pl.BlockSpec((16, width), lambda i: (0, 0))],
        out_shape=[
            jax.ShapeDtypeStruct((tokens, width), f32),
            jax.ShapeDtypeStruct((tokens, width), bf16),
            jax.ShapeDtypeStruct((tokens, width), bf16),
            jax.ShapeDtypeStruct((16, width), f32),
        ],
        compiler_params=params(),
        cost_estimate=cost(2 * tokens * width * (width + E * CAP), 20 * tokens * width),
        name="middle",
    )(cols, *ds, prob, dprob, router, n2, resid, cot, gain, w_out)


def weight_grad_kernel(rows, idx_ref, left_ref, right_ref, keep_ref, send_ref, turned_ref):
    c = idx_ref[0]
    width = left_ref.shape[1]
    step = 384
    per = step // (2 * rows)

    @pl.when(pl.program_id(0) == 0)
    def _():
        for m in range(width // step):
            turned_ref[m * step : (m + 1) * step, :] = left_ref[:, m * step : (m + 1) * step].T

    right = right_ref[...]
    for m in range(width // step):
        keep, send = split_cores(dot(turned_ref[m * step : (m + 1) * step, :], right), c, rows)
        keep_ref[m * per : (m + 1) * per] = keep
        send_ref[m * per : (m + 1) * per] = send


def weight_grad_call(core, left, right, rows, n_z, name):
    tokens, width = left.shape
    n = right.shape[1] // BLK
    out = pl.BlockSpec((n_z, rows, BLK), lambda j, _: (0, j, 0))
    shape = jax.ShapeDtypeStruct((n_z, n * rows, BLK), bf16)
    return pl.pallas_call(
        functools.partial(weight_grad_kernel, rows),
        grid_spec=pltpu.PrefetchScalarGridSpec(
            num_scalar_prefetch=1,
            grid=(n,),
            in_specs=[
                pl.BlockSpec((tokens, width), lambda j, _: (0, 0), pipeline_mode=pl.Buffered(1)),
                pl.BlockSpec((tokens, BLK), lambda j, _: (0, j)),
            ],
            out_specs=[out, out],
            scratch_shapes=[pltpu.VMEM((width, tokens), bf16)],
        ),
        out_shape=[shape, shape],
        compiler_params=params(),
        cost_estimate=cost(2 * tokens * width * n * BLK, 2 * width * n * BLK + 4 * tokens * width),
        name=name,
    )(core, left, right)


def input_grad_kernel(rows, n, d_ref, w_ref, x_ref, dresid_ref, gain_ref, out_ref, small_ref):
    width = x_ref.shape[1]

    @pl.when(pl.program_id(0) == 0)
    def _():
        small_ref[...] = jnp.zeros_like(small_ref)

    dn1 = dot_last(d_ref[:, :BLK], w_ref[:, :rows, :].reshape(-1, BLK))
    for j in range(1, n):
        w = w_ref[:, j * rows : (j + 1) * rows, :].reshape(-1, BLK)
        dn1 += dot_last(d_ref[:, j * BLK : (j + 1) * BLK], w)
    x = x_ref[...].astype(f32)
    scale = lax.rsqrt(jnp.mean(x * x, axis=-1, keepdims=True) + epsilon)
    small_ref[...] += jnp.broadcast_to(jnp.sum(dn1 * x * scale, axis=0, keepdims=True), (8, width))
    weighted = dn1 * gain_ref[...]
    along = jnp.mean(weighted * x, axis=-1, keepdims=True)
    out = dresid_ref[...] + scale * weighted - x * (scale * scale * scale * along)
    out_ref[...] = out.astype(bf16)


def input_grad_call(dqkv, w_in, x, dresid, gain, rows, n):
    tokens, width = x.shape
    tile = pl.BlockSpec((TILE, width), lambda i: (i, 0))
    return pl.pallas_call(
        functools.partial(input_grad_kernel, rows, n),
        grid=(tokens // TILE,),
        in_specs=[
            pl.BlockSpec((TILE, n * BLK), lambda i: (i, 0)),
            whole((w_in.shape[0], n * rows, BLK)),
            tile,
            tile,
            whole((1, width)),
        ],
        out_specs=[tile, pl.BlockSpec((8, width), lambda i: (0, 0))],
        out_shape=[
            jax.ShapeDtypeStruct((tokens, width), bf16),
            jax.ShapeDtypeStruct((8, width), f32),
        ],
        compiler_params=params(),
        cost_estimate=cost(2 * tokens * width * n * BLK, 2 * width * n * BLK + 12 * tokens * width),
        name="input_grad",
    )(dqkv, w_in, x, dresid, gain)


def adam_step(master, first, second, gradient, clip, decayed):
    clipped = gradient * clip
    first_new = beta_first * first + (1.0 - beta_first) * clipped
    second_new = beta_second * second + (1.0 - beta_second) * clipped * clipped
    first_hat = first_new * (1.0 / (1.0 - beta_first**STEP))
    second_hat = second_new * (1.0 / (1.0 - beta_second**STEP))
    change = first_hat / (jnp.sqrt(second_hat) + adam_floor) + decayed * weight_decay * master
    update = -learn_rate * change
    return (gradient, update, first_new, second_new)


def adam_kernel(scale, clip_ref, g_ref, master_ref, first_ref, second_ref, *outs):
    gradient = g_ref[...].astype(f32) * scale
    results = adam_step(master_ref[...], first_ref[...], second_ref[...], gradient, clip_ref[0], 1.0)
    for out, result in zip(outs, results):
        out[...] = result


def adam_call(clip, packed, at, master, first, second, scale, name):
    rows, cols = master.shape
    natural = pl.BlockSpec((rows, BLK), lambda j, _: (0, j))
    shape = jax.ShapeDtypeStruct(master.shape, f32)
    return pl.pallas_call(
        functools.partial(adam_kernel, scale),
        grid_spec=pltpu.PrefetchScalarGridSpec(
            num_scalar_prefetch=1,
            grid=(cols // BLK,),
            in_specs=[pl.BlockSpec((rows, BLK), lambda j, _: (at // rows + j, 0)), natural, natural, natural],
            out_specs=[natural] * 4,
        ),
        out_shape=[shape] * 4,
        compiler_params=params(),
        cost_estimate=cost(20 * master.size, 30 * master.size),
        name=name,
    )(clip, packed, master, first, second)


def adam_experts_kernel(scale, clip_ref, g0_ref, g1_ref, g2_ref, master_ref, first_ref, second_ref, *outs):
    for e, g_ref in enumerate((g0_ref, g1_ref, g2_ref)):

        @pl.when(pl.program_id(0) == e)
        def _():
            gradient = g_ref[...].astype(f32) * scale
            results = adam_step(master_ref[0], first_ref[0], second_ref[0], gradient, clip_ref[0], 1.0)
            for out, result in zip(outs, results):
                out[0] = result


def adam_experts_call(clip, packed, at, master, first, second, scale, name):
    _, rows, cols = master.shape
    n = cols // BLK
    natural = pl.BlockSpec((1, rows, BLK), lambda e, j, _: (e, 0, j))
    shape = jax.ShapeDtypeStruct(master.shape, f32)

    def g_spec(own):
        return pl.BlockSpec(
            (rows, BLK), lambda e, j, _: (at // rows + jnp.where(e < own, 0, jnp.where(e > own, n - 1, j)), 0)
        )

    return pl.pallas_call(
        functools.partial(adam_experts_kernel, scale),
        grid_spec=pltpu.PrefetchScalarGridSpec(
            num_scalar_prefetch=1,
            grid=(E, n),
            in_specs=[g_spec(e) for e in range(E)] + [natural] * 3,
            out_specs=[natural] * 4,
        ),
        out_shape=[shape] * 4,
        compiler_params=params(),
        cost_estimate=cost(20 * master.size, 30 * master.size),
        name=name,
    )(clip, *packed, master, first, second)


def per_device(
    tokens,
    cotangent,
    lengths,
    routes,
    slot_index,
    norm_gains,
    norm_first,
    norm_second,
    in_proj,
    in_first,
    in_second,
    out_proj,
    out_first,
    out_second,
    router,
    router_first,
    router_second,
    up_proj,
    up_first,
    up_second,
    down_proj,
    down_first,
    down_second,
):
    n_rep, n_f = lax.axis_size("replica"), lax.axis_size("fsdp")
    n_z = n_f // 2
    n_mb, n_local, seq, width = tokens.shape
    n_seq = n_mb * n_local
    total_tokens = n_seq * seq
    unit = 16 * n_rep
    rows = in_proj.shape[0]
    down_rows = down_proj.shape[1]
    n_in, n_out, n_up, n_down = (w.shape[-1] // BLK for w in (in_proj, out_proj, up_proj, down_proj))
    core = (lax.axis_index("fsdp") % 2).astype(jnp.int32)[None]

    smalls = jnp.concatenate([norm_gains.astype(bf16), router.astype(bf16).T], axis=0)
    n_small = round_up(smalls.size, BLK) // BLK
    smalls = jnp.pad(smalls.reshape(-1), (0, 16 * BLK - smalls.size)).reshape(16, BLK)
    in_shard = pack_call([(in_proj, None)], unit, smalls)
    out_shard = pack_call([(out_proj, None)], unit)
    early_shard = pack_call([(up_proj, 0), (down_proj, 0)], unit)
    late_shard = pack_call([(w, e) for e in range(1, E) for w in (up_proj, down_proj)], unit)
    e_rows = n_up * rows + n_down * down_rows

    w_in = gather_packed(in_shard, 0)
    w_out = gather_packed(out_shard, 1)
    w_early = gather_packed(early_shard, 0)
    w_late = gather_packed(late_shard, 1)

    small_all = w_in[:, n_in * rows : n_in * rows + n_small, :].reshape(n_f, n_small * BLK)[:, : 5 * rows]
    small_all = small_all.reshape(n_f, 5, rows).transpose(1, 0, 2).reshape(5, width)
    gain_one = small_all[0:1].astype(f32)
    gain_two = small_all[1:2].astype(f32)
    router8 = pad_rows(small_all[2:5], 8)

    length = lengths.reshape(n_seq).astype(jnp.int32)
    route = routes.reshape(n_seq, seq, 2)
    slot = slot_index.reshape(n_seq, seq, 2)
    live = jnp.arange(seq)[None, :] < length[:, None]
    kept = live[:, :, None] & (slot < CAP)
    slot_of = [
        jnp.max(jnp.where(kept & (route == e), slot, -1), axis=-1) for e in range(E)
    ]
    slot_rows = jnp.stack(slot_of + [live.astype(jnp.int32)] + [jnp.full_like(slot_of[0], -1)] * 4, axis=1)
    slot_cols = slot_rows.transpose(0, 2, 1).reshape(total_tokens, 8)

    x = tokens.reshape(total_tokens, width)
    cot = cotangent.reshape(total_tokens, width)

    qkv, n1 = qkv_call(x, gain_one, w_in, rows, n_in)
    probs, mixed = attention_call(length, qkv, n_seq)
    resid, n2, prob = resid_call(mixed, w_out, x, gain_two, router8, rows, n_out)
    buf, dys, gates = dispatch_call(slot_rows, prob, n2, cot, n_seq)

    ys, dbufs, dgates, sums = [], [], [], []
    for e in range(E):
        w, at = (w_early, 0) if e == 0 else (w_late, (e - 1) * e_rows)
        y, dbuf, dgate, keep, send = expert_call(
            e, at, core, buf, dys, gates, slot_rows, w, rows, down_rows, unit
        )
        ys.append(y)
        dbufs.append(dbuf)
        dgates.append(dgate.reshape(1, total_tokens))
        sums.append(reduce_packed(keep, send, e))
    dprob = pad_rows(jnp.concatenate(dgates, axis=0), 8)
    block_out = combine_call(slot_cols, resid, ys, n_seq)

    dresid, dattn, dmixed, small_two = middle_call(
        slot_cols, dbufs, prob, dprob, router8, n2, resid, cot, gain_two, w_out, rows, n_out, n_seq
    )

    def reduce_one(keep, send, first):
        n = keep.shape[1]
        extra = round_up(n, unit) - n
        if extra:
            keep = jnp.pad(keep, ((0, 0), (0, extra), (0, 0)))
            send = jnp.pad(send, ((0, 0), (0, extra), (0, 0)))
        return reduce_packed(keep, send, first)

    out_sum = reduce_one(*weight_grad_call(core, mixed, dattn, rows, n_z, "out_grad"), 1)
    dq, dk, dv = attention_back_call(qkv, probs, mixed, dmixed, n_seq)
    dqkv = jnp.concatenate([dq, dk, dv], axis=1)
    in_sum = reduce_one(*weight_grad_call(core, n1, dqkv, rows, n_z, "in_grad"), 0)
    input_grad, small_one = input_grad_call(dqkv, w_in, x, dresid, gain_one, rows, n_in)

    grad_scale = 1.0 / (n_seq * n_rep * n_f)
    small_sum = sum_all(jnp.concatenate([small_one[:1], small_two[8:9], small_two[:E]], axis=0)) * grad_scale
    at = lax.axis_index("fsdp") * rows
    small_mine = lax.dynamic_slice_in_dim(small_sum, at, rows, axis=1)
    def square(packed):
        values = packed.astype(f32) * grad_scale
        return jnp.sum(values * values)

    at_down = n_up * rows
    late = sum_small(jnp.stack([square(in_sum[: n_in * rows])]))
    early = sum_small(
        jnp.stack(
            [
                square(out_sum[: n_out * rows]),
                sum(square(s[:at_down]) for s in sums),
                sum(square(s[at_down:e_rows]) for s in sums),
            ]
        )
    )
    totals = (
        jnp.sum(small_sum[:2] * small_sum[:2]),
        late[0],
        early[0],
        jnp.sum(small_sum[2:] * small_sum[2:]),
        early[1],
        early[2],
    )
    weights = (norm_gains, in_proj, out_proj, router, up_proj, down_proj)
    counts = (2 * width,) + tuple(w.size * n_f for w in weights[1:])
    rms = [jnp.sqrt(t / float(n) + epsilon) for t, n in zip(totals, counts)]
    clips = [jnp.minimum(1.0, clip_level / r)[None] for r in rms]
    norm_res = adam_step(norm_gains, norm_first, norm_second, small_mine[:2], clips[0], 0.0)
    in_res = adam_call(clips[1], in_sum, 0, in_proj, in_first, in_second, grad_scale, "in_adam")
    out_res = adam_call(clips[2], out_sum, 0, out_proj, out_first, out_second, grad_scale, "out_adam")
    router_res = adam_step(router, router_first, router_second, small_mine[2:].T, clips[3], 1.0)
    up_res = adam_experts_call(clips[4], sums, 0, up_proj, up_first, up_second, grad_scale, "up_adam")
    down_res = adam_experts_call(
        clips[5], sums, at_down, down_proj, down_first, down_second, grad_scale, "down_adam"
    )
    return (
        block_out.reshape(tokens.shape),
        input_grad.reshape(tokens.shape),
        jnp.stack(rms[:5]),
        jnp.stack(rms[5:]),
        *norm_res,
        *in_res,
        *out_res,
        *router_res,
        *up_res,
        *down_res,
    )


def solution(mesh):
    data = P(None, ("replica", "fsdp"), None, None)
    gains = P(None, "fsdp")
    flat = P("fsdp", None)
    experts = P(None, "fsdp", None)
    return jax.shard_map(
        per_device,
        mesh=mesh,
        in_specs=(data, data, P(None, ("replica", "fsdp")), data, data)
        + (gains,) * 3
        + (flat,) * 9
        + (experts,) * 6,
        out_specs=(data, data, P(), P()) + (gains,) * 4 + (flat,) * 12 + (experts,) * 8,
        check_vma=False,
    )
```

time: 1980 us -> 955 us (0.48)
  waiting for transfers between devices: 1010 us -> 352 us
  matrix products: 383 us -> 0 us
  Pallas kernels: 0 us -> 379 us
  local copies, waits for them, and re-layouts: 242 us -> 30.4 us
  other arithmetic: 265 us -> 72.6 us
  starting transfers between devices: 0.46 us -> 103 us
  blocking collectives: 53.9 us -> 0 us
    reduce_scatter x4 -> x0, waiting for transfers between devices: 614 us -> none  [the longest x1 366 us: reduce_whole(): lax.psum_scatter(new_grads[4], 'fsdp', scatter_dimension=1, tiled=True)]
    dot_general x42 -> x0, matrix products: 383 us -> none  [the longest x2 46.1 us: backward_pass(): jnp.einsum('ecd,ecf->edf', expert_in, d_gate_up, preferred_element_type=j...]
    pallas_call x0 -> x25, Pallas kernels: none -> 379 us  [the longest x3 98.3 us: expert_call(): pl.pallas_call(functools.partial(expert_kernel, e, up_rows, down_rows), g...]
    ppermute x0 -> x83, waiting for transfers between devices: none -> 352 us  [the longest x30 234 us: swap_replica(): return lax.ppermute(x, 'replica', [(i, i ^ bit) for i in range(size)])]
    psum x1 -> x0, waiting for transfers between devices: 192 us -> none  [per_device(): lax.psum((running[0], running[1], running[2], running[3], running[4], run...]
    all_gather x4 -> x0, waiting for transfers between devices: 146 us -> none  [the longest x1 78.8 us: gather_forward(): lax.all_gather(low_parts[5], 'fsdp', axis=1, tiled=True)]
    reduce_sum x21 -> x8, other arithmetic: 125 us -> 8.69 us  [the longest x6 7.46 us: square(): return jnp.sum(values * values)]
    ppermute x0 -> x83, starting transfers between devices: none -> 103 us  [the longest x27 51.2 us: shift_core_pairs(): lax.ppermute(x, 'fsdp', [(i, (i + 2 * k) % size) for i in range(size)])]
  transfers between devices with their start and end apart: 11 -> 83, of which waited for: 8 -> 34; matrix products, arithmetic and copies ran while one was open for 24% -> 10% of each run, Pallas kernels for 0% -> 36%
where the time goes in v1:
time: 955 us; the launch traced here: 949 us
  Pallas kernels  379 us (40%)
  waiting for transfers between devices  352 us (37%)
  starting transfers between devices  103 us (11%)
  other arithmetic  72.6 us (8%)
  local copies, waits for them, and re-layouts  30.4 us (3%)
  between operations  12.9 us (1%)
    ppermute x30, waiting for transfers between devices, swap_replica(): return lax.ppermute(x, 'replica', [(i, i ^ bit) for i in range(size)])  234 us
    pallas_call x3, Pallas kernels, expert_call(): pl.pallas_call(functools.partial(expert_kernel, e, up_rows, down_rows), g...  98.3 us
    ppermute x27, waiting for transfers between devices, shift_core_pairs(): lax.ppermute(x, 'fsdp', [(i, (i + 2 * k) % size) for i in range(size)])  98 us
    ppermute x27, starting transfers between devices, shift_core_pairs(): lax.ppermute(x, 'fsdp', [(i, (i + 2 * k) % size) for i in range(size)])  51.2 us
    pallas_call x1, Pallas kernels, attention_back_call(): pl.pallas_call(attention_back_kernel, grid=(n_seq, pairs), in_specs=[qspe...  42 us
    pallas_call x1, Pallas kernels, attention_call(): pl.pallas_call(attention_kernel, grid_spec=pltpu.PrefetchScalarGridSpec(n...  37.8 us
    pallas_call x4, Pallas kernels, gather_packed(): pl.pallas_call(functools.partial(assemble_kernel, tuple(masks), n_z - 1),...  34.7 us
    ppermute x30, starting transfers between devices, swap_replica(): return lax.ppermute(x, 'replica', [(i, i ^ bit) for i in range(size)])  32 us
  transfers between devices with their start and end apart: 83, of which 34 were waited for; matrix products, arithmetic and copies ran while one was open for 10% of the time, Pallas kernels for 36%

profile of v1, /device:TPU:0, one launch (start us, length us, event | category | flops | bytes accessed | tf_op | source)
XLA Modules:
  0.0 949.5 jit_solution(10608569657001620075)
XLA Ops:
  27.7 22.8 %collective-permute-done.25 = bf16[576,512]{1,0:T(8,128)(2,1)S(1)} collective-permute-done((bf16[576,512]{1,0:T(8,128)(2,1)S(1)}, bf16[576,512]{1,0:T(8,128)(2,1)S(1)}, u32[]{:S(2)}, u32[]{:S(2)}) %collective-permute-start.25) | collective-permute-done | bytes 589856 | tf_op jit(solution)/shard_map/ppermute | solution.py:65
  56.1 23.0 %collective-permute-done.1 = bf16[256,512]{1,0:T(8,128)(2,1)S(1)} collective-permute-done((bf16[256,512]{1,0:T(8,128)(2,1)S(1)}, bf16[256,512]{1,0:T(8,128)(2,1)S(1)}, u32[]{:S(2)}, u32[]{:S(2)}) %collective-permute-start.1) | collective-permute-done | bytes 262176 | tf_op jit(solution)/shard_map/ppermute | solution.py:65
  110.6 12.9 %collective-permute-done.17 = bf16[288,512]{1,0:T(8,128)(2,1)S(1)} collective-permute-done((bf16[288,512]{1,0:T(8,128)(2,1)S(1)}, bf16[288,512]{1,0:T(8,128)(2,1)S(1)}, u32[]{:S(2)}, u32[]{:S(2)}) %collective-permute-start.17) | collective-permute-done | bytes 294944 | tf_op jit(solution)/shard_map/ppermute | solution.py:65
  137.3 15.0 %collective-permute-done.19 = bf16[1,3,288,512]{3,2,1,0:T(8,128)(2,1)S(1)} collective-permute-done((bf16[1,3,288,512]{3,2,1,0:T(8,128)(2,1)S(1)}, bf16[1,3,288,512]{3,2,1,0:T(8,128)(2,1)S(1)}, u32[]{:S(2)}, u32[]{:S(2)}) %collective-permute-start.19) | collective-permute-done | bytes 884768 | tf_op jit(solution)/shard_map/ppermute | solution.py:75
  152.4 19.0 %collective-permute-done.12.refs_2_ = bf16[2,3,144,512]{3,2,1,0:T(8,128)(2,1)S(1)} collective-permute-done((bf16[2,3,144,512]{3,2,1,0:T(8,128)(2,1)S(1)}, bf16[2,3,144,512]{3,2,1,0:T(8,128)(2,1)S(1)}, u32[]{:S(2)}, u32[]{:S(2)}) %collective-permute-start.12) | collective-permute-done | bytes 884768 | tf_op jit(solution)/shard_map/ppermute | solution.py:75
  188.2 25.9 %collective-permute-done.20.refs_2_ = bf16[2,3,288,512]{3,2,1,0:T(8,128)(2,1)} collective-permute-done((bf16[2,3,288,512]{3,2,1,0:T(8,128)(2,1)}, bf16[2,3,288,512]{3,2,1,0:T(8,128)(2,1)}, u32[]{:S(2)}, u32[]{:S(2)}) %collective-permute-start.20) | collective-permute-done | bytes 1769504 | tf_op jit(solution)/shard_map/ppermute | solution.py:75
  225.8 18.1 %qkv.1 = (bf16[1024,2560]{1,0:T(8,128)(2,1)}, bf16[1024,1536]{1,0:T(8,128)(2,1)}) custom-call(bf16[1024,1536]{1,0:T(8,128)(2,1)} %bitcast.421, f32[1,1536]{1,0:T(1,128)} %reshape.633.gain_ref, bf16[8,1024,512]{2,1,0:T(8,128)(2,1)} %assemble.4.w_ref), custom_call_target="tpu_custom_call" | custom-call | flops 8053063680 | bytes 14155776 | tf_op jit(solution)/shard_map/qkv/pallas_call | solution.py:285
  246.4 37.8 %attention.1 = (bf16[2,24,512,512]{3,2,1,0:T(8,128)(2,1)}, bf16[1024,1536]{1,0:T(8,128)(2,1)}) custom-call(s32[2]{0:T(128)} %bitcast.418, bf16[1024,2560]{1,0:T(8,128)(2,1)} %get-tuple-element.82.q_ref.k_ref.v_ref, bf16[1024,2560]{1,0:T(8,128)(2,1)} %get-tuple-element.82.q_ref.k_ref.v_ref, bf16[1024,2560]{1,0:T(8,128)(2,1)} %get-tuple-element.82.q_ref.k_ref.v_ref), custom_call_target="tpu_custom_call" | custom-call | flops 12884901888 | bytes 25165824 | tf_op jit(solution)/shard_map/attention/pallas_call | solution.py:343
  287.5 12.0 %resid.1 = (f32[1024,1536]{1,0:T(8,128)}, bf16[1024,1536]{1,0:T(8,128)(2,1)}, f32[8,1024]{1,0:T(8,128)}) custom-call(bf16[1024,1536]{1,0:T(8,128)(2,1)} %get-tuple-element.83.mix_ref.left_ref, bf16[8,576,512]{2,1,0:T(8,128)(2,1)} %assemble.5.w_ref, bf16[1024,1536]{1,0:T(8,128)(2,1)} %bitcast.422, f32[1,1536]{1,0:T(1,128)} %reshape.634.gain_ref, ...), custom_call_target="tpu_custom_call" | custom-call | flops 4831838208 | bytes 23592960 | tf_op jit(solution)/shard_map/resid/pallas_call | solution.py:466
  300.1 12.1 %dispatch.1 = (bf16[3,2,320,1536]{3,2,1,0:T(8,128)(2,1)}, bf16[3,2,320,1536]{3,2,1,0:T(8,128)(2,1)}, f32[3,2,320,128]{3,2,1,0:T(8,128)}) custom-call(s32[2,8,512]{2,1,0:T(8,128)} %stack.210.slot_ref, f32[8,1024]{1,0:T(8,128)} %get-tuple-element.85.prob_ref, bf16[1024,1536]{1,0:T(8,128)(2,1)} %get-tuple-element.86.n2_ref, bf16[1024,1536]{1,0:T(8,128)(2,1)} %bitcast.419), custom_call_target="tpu_custom_call" | custom-call | flops 6039797760 | bytes 31457280 | tf_op jit(solution)/shard_map/dispatch/pallas_call | solution.py:503
  312.2 8.1 assemble.6.up_a_ref.up_b_ref.down_ref
  320.4 32.6 %expert.3 = (bf16[2,320,1536]{2,1,0:T(8,128)(2,1)}, bf16[2,320,1536]{2,1,0:T(8,128)(2,1)}, f32[2,8,512]{2,1,0:T(8,128)}, bf16[4,1152,512]{2,1,0:T(8,128)(2,1)}, bf16[4,1152,512]{2,1,0:T(8,128)(2,1)}) custom-call(s32[1]{0:T(128)} %bitcast.11.idx_ref, bf16[3,2,320,1536]{3,2,1,0:T(8,128)(2,1)} %get-tuple-element.87.buf_ref, ...), custom_call_target="tpu_custom_call" | custom-call | flops 18119393280 | bytes 62914560 | tf_op jit(solution)/shard_map/expert/pallas_call | solution.py:673
  355.7 13.6 %assemble.7.up_a_ref.up_b_ref.down_ref = bf16[8,2304,512]{2,1,0:T(8,128)(2,1)} custom-call(s32[3]{0:T(128)} %pad_add_fusion.idx_ref, bf16[2304,512]{1,0:T(8,128)(2,1)} %pack.7.refs_0_, bf16[2,3,576,512]{3,2,1,0:T(8,128)(2,1)} %copy-done.3, bf16[2,3,576,512]{3,2,1,0:T(8,128)(2,1)} %collective-permute-done.28.refs_2_, ...), custom_call_target="tpu_custom_call" | custom-call | bytes 37748736 | tf_op jit(solution)/shard_map/assemble/pallas_call | solution.py:135
  369.3 33.0 %expert.5 = (bf16[2,320,1536]{2,1,0:T(8,128)(2,1)}, bf16[2,320,1536]{2,1,0:T(8,128)(2,1)}, f32[2,8,512]{2,1,0:T(8,128)}, bf16[4,1152,512]{2,1,0:T(8,128)(2,1)}, bf16[4,1152,512]{2,1,0:T(8,128)(2,1)}) custom-call(s32[1]{0:T(128)} %bitcast.11.idx_ref, bf16[3,2,320,1536]{3,2,1,0:T(8,128)(2,1)} %get-tuple-element.87.buf_ref, ...), custom_call_target="tpu_custom_call" | custom-call | flops 18119393280 | bytes 62914560 | tf_op jit(solution)/shard_map/expert/pallas_call | solution.py:673
  403.0 32.7 %expert.4 = (bf16[2,320,1536]{2,1,0:T(8,128)(2,1)}, bf16[2,320,1536]{2,1,0:T(8,128)(2,1)}, f32[2,8,512]{2,1,0:T(8,128)}, bf16[4,1152,512]{2,1,0:T(8,128)(2,1)}, bf16[4,1152,512]{2,1,0:T(8,128)(2,1)}) custom-call(s32[1]{0:T(128)} %bitcast.11.idx_ref, bf16[3,2,320,1536]{3,2,1,0:T(8,128)(2,1)} %get-tuple-element.87.buf_ref, ...), custom_call_target="tpu_custom_call" | custom-call | flops 18119393280 | bytes 62914560 | tf_op jit(solution)/shard_map/expert/pallas_call | solution.py:673
  437.1 20.3 %middle.1 = (f32[1024,1536]{1,0:T(8,128)}, bf16[1024,1536]{1,0:T(8,128)(2,1)}, bf16[1024,1536]{1,0:T(8,128)(2,1)}, f32[16,1536]{1,0:T(8,128)}) custom-call(s32[1024,8]{1,0:T(8,128)} %bitcast.384, bf16[2,320,1536]{2,1,0:T(8,128)(2,1)} %get-tuple-element.94.d0_ref, bf16[2,320,1536]{2,1,0:T(8,128)(2,1)} %get-tuple-element.95.d1_ref, ...), custom_call_target="tpu_custom_call" | custom-call | flops 7851737088 | bytes 31457280 | tf_op jit(solution)/shard_map/middle/pallas_call | solution.py:815
  463.0 42.0 %attention_back.1 = (bf16[1024,1536]{1,0:T(8,128)(2,1)}, bf16[1024,512]{1,0:T(8,128)(2,1)}, bf16[1024,512]{1,0:T(8,128)(2,1)}) custom-call(bf16[1024,2560]{1,0:T(8,128)(2,1)} %get-tuple-element.82.q_ref.k_ref.v_ref, bf16[1024,2560]{1,0:T(8,128)(2,1)} %get-tuple-element.82.q_ref.k_ref.v_ref, bf16[1024,2560]{1,0:T(8,128)(2,1)} %get-tuple-element.82.q_ref.k_ref.v_ref, ...), custom_call_target="tpu_custom_call" | custom-call | flops 25769803776 | bytes 25165824 | tf_op jit(solution)/shard_map/attention_back/pallas_call | solution.py:418
  511.6 15.3 %input_grad.1 = (bf16[1024,1536]{1,0:T(8,128)(2,1)}, f32[8,1536]{1,0:T(8,128)}) custom-call(bf16[1024,2560]{1,0:T(8,128)(2,1)} %constant_dynamic-update-slice_fusion.d_ref.right_ref, bf16[8,1024,512]{2,1,0:T(8,128)(2,1)} %assemble.4.w_ref, bf16[1024,1536]{1,0:T(8,128)(2,1)} %bitcast.423, f32[1024,1536]{1,0:T(8,128)} %get-tuple-element.104.dresid_ref, ...), custom_call_target="tpu_custom_call" | custom-call | flops 8053063680 | bytes 26738688 | tf_op jit(solution)/shard_map/input_grad/pallas_call | solution.py:908
  528.1 13.8 %in_grad.1 = (bf16[4,960,512]{2,1,0:T(8,128)(2,1)}, bf16[4,960,512]{2,1,0:T(8,128)(2,1)}) custom-call(s32[1]{0:T(128)} %bitcast.11.idx_ref, bf16[1024,1536]{1,0:T(8,128)(2,1)} %get-tuple-element.108.left_ref, bf16[1024,2560]{1,0:T(8,128)(2,1)} %constant_dynamic-update-slice_fusion.d_ref.right_ref), custom_call_target="tpu_custom_call" | custom-call | flops 8053063680 | bytes 14155776 | tf_op jit(solution)/shard_map/in_grad/pallas_call | solution.py:866
  542.1 9.7 %out_grad.1 = (bf16[4,576,512]{2,1,0:T(8,128)(2,1)}, bf16[4,576,512]{2,1,0:T(8,128)(2,1)}) custom-call(s32[1]{0:T(128)} %bitcast.11.idx_ref, bf16[1024,1536]{1,0:T(8,128)(2,1)} %get-tuple-element.83.mix_ref.left_ref, bf16[1024,1536]{1,0:T(8,128)(2,1)} %get-tuple-element.111.right_ref), custom_call_target="tpu_custom_call" | custom-call | flops 4831838208 | bytes 11010048 | tf_op jit(solution)/shard_map/out_grad/pallas_call | solution.py:866
  573.1 23.8 %collective-permute-done.36 = f32[5,1536]{1,0:T(8,128)S(1)} collective-permute-done((f32[5,1536]{1,0:T(8,128)S(1)}, f32[5,1536]{1,0:T(8,128)S(1)}, u32[]{:S(2)}, u32[]{:S(2)}) %collective-permute-start.36) | collective-permute-done | bytes 30752 | tf_op jit(solution)/shard_map/ppermute | solution.py:75
  598.5 10.4 %combine.1 = bf16[1024,1536]{1,0:T(8,128)(2,1)} custom-call(s32[1024,8]{1,0:T(8,128)} %bitcast.385, f32[1024,1536]{1,0:T(8,128)} %get-tuple-element.84.resid_ref, bf16[2,320,1536]{2,1,0:T(8,128)(2,1)} %get-tuple-element.90.y0_ref, bf16[2,320,1536]{2,1,0:T(8,128)(2,1)} %get-tuple-element.91.y1_ref, bf16[2,320,1536]{2,1,0:T(8,128)(2,1)} %get-tuple-element.92.y2_ref), custom_call_target="tpu_custom_call" | custom-call | flops 3019898880 | bytes 18874368 | tf_op jit(solution)/shard_map/combine/pallas_call | solution.py:741
  630.0 9.1 collective-permute-done.60
  648.3 26.6 %collective-permute-done.50 = bf16[4,144,512]{2,1,0:T(8,128)(2,1)S(1)} collective-permute-done((bf16[4,144,512]{2,1,0:T(8,128)(2,1)S(1)}, bf16[4,144,512]{2,1,0:T(8,128)(2,1)S(1)}, u32[]{:S(2)}, u32[]{:S(2)}) %collective-permute-start.50) | collective-permute-done | bytes 589856 | tf_op jit(solution)/shard_map/ppermute | solution.py:75
  696.1 61.7 %collective-permute-done.54 = bf16[144,512]{1,0:T(8,128)(2,1)S(1)} collective-permute-done((bf16[144,512]{1,0:T(8,128)(2,1)S(1)}, bf16[144,512]{1,0:T(8,128)(2,1)S(1)}, u32[]{:S(2)}, u32[]{:S(2)}) %collective-permute-start.54) | collective-permute-done | bytes 147488 | tf_op jit(solution)/shard_map/ppermute | solution.py:75
  758.1 15.2 %collective-permute-done.39 = bf16[4,240,512]{2,1,0:T(8,128)(2,1)S(1)} collective-permute-done((bf16[4,240,512]{2,1,0:T(8,128)(2,1)S(1)}, bf16[4,240,512]{2,1,0:T(8,128)(2,1)S(1)}, u32[]{:S(2)}, u32[]{:S(2)}) %collective-permute-start.39) | collective-permute-done | bytes 983072 | tf_op jit(solution)/shard_map/ppermute | solution.py:75
  814.1 8.7 collective-permute-done.66
  843.1 10.8 %collective-permute-start.46 = (f32[1]{0:T(128)}, f32[1]{0:T(128)}, u32[]{:S(2)}, u32[]{:S(2)}) collective-permute-start(f32[1]{0:T(128)} %add.1133), channel_id=1, source_target_pairs={{0,2},{1,3},{2,0},{3,1},{4,6},{5,7},{6,4},{7,5},{8,10},{9,11},{10,... | collective-permute-start | bytes 20 | tf_op jit(solution)/shard_map/ppermute | solution.py:197
  860.1 8.6 in_adam.1
  881.7 8.9 collective-permute-done.79
  913.8 11.2 %down_adam.1 = (f32[3,128,1536]{2,1,0:T(8,128)}, f32[3,128,1536]{2,1,0:T(8,128)}, f32[3,128,1536]{2,1,0:T(8,128)}, f32[3,128,1536]{2,1,0:T(8,128)}) custom-call(f32[1]{0:T(128)S(6)} %min.27.clip_ref, bf16[1152,512]{1,0:T(8,128)(2,1)} %bitcast.351, bf16[1152,512]{1,0:T(8,128)(2,1)} %bitcast.355, bf16[1152,512]{1,0:T(8,128)(2,1)} %bitcast.347, ...), custom_call_target="tpu_custom_call" | custom-call | flops 11796480 | bytes 17694720 | tf_op jit(solution)/shard_map/down_adam/pallas_call | solution.py:988
  925.0 17.3 %up_adam.1 = (f32[3,192,2048]{2,1,0:T(8,128)}, f32[3,192,2048]{2,1,0:T(8,128)}, f32[3,192,2048]{2,1,0:T(8,128)}, f32[3,192,2048]{2,1,0:T(8,128)}) custom-call(f32[1]{0:T(128)S(6)} %min.26.clip_ref, bf16[1152,512]{1,0:T(8,128)(2,1)} %bitcast.352, bf16[1152,512]{1,0:T(8,128)(2,1)} %bitcast.356, bf16[1152,512]{1,0:T(8,128)(2,1)} %bitcast.348, ...), custom_call_target="tpu_custom_call" | custom-call | flops 23592960 | bytes 35389440 | tf_op jit(solution)/shard_map/up_adam/pallas_call | solution.py:988
  (346 shorter events, 304.4 us)
Async XLA Ops:
  8.8 41.7 %collective-permute-start.25 = (bf16[576,512]{1,0:T(8,128)(2,1)S(1)}, bf16[576,512]{1,0:T(8,128)(2,1)S(1)}, u32[]{:S(2)}, u32[]{:S(2)}) collective-permute-start(bf16[576,512]{1,0:T(8,128)(2,1)S(1)} %constant_dynamic-slice_fusion.1), channel_id=1, source_target_pairs={{0,4},{1,5},{2,6},{3,7},{4,0},{5,1},{6,2},{7,3},{8,12},{9,13},{10,... | collective-permute-start | bytes 1769480 | tf_op jit(solution)/shard_map/ppermute | solution.py:65
  11.4 39.1 %collective-permute-start.26 = (bf16[576,512]{1,0:T(8,128)(2,1)S(1)}, bf16[576,512]{1,0:T(8,128)(2,1)S(1)}, u32[]{:S(2)}, u32[]{:S(2)}) collective-permute-start(bf16[576,512]{1,0:T(8,128)(2,1)S(1)} %constant_dynamic-slice_fusion.1), channel_id=1, source_target_pairs={{0,6},{1,7},{2,0},{3,1},{4,2},{5,3},{6,4},{7,5},{8,14},{9,15},{10,... | collective-permute-start | bytes 1769480 | tf_op jit(solution)/shard_map/ppermute | solution.py:65
  17.1 39.0 %collective-permute-start = (bf16[256,512]{1,0:T(8,128)(2,1)S(1)}, bf16[256,512]{1,0:T(8,128)(2,1)S(1)}, u32[]{:S(2)}, u32[]{:S(2)}) collective-permute-start(bf16[256,512]{1,0:T(8,128)(2,1)S(1)} %constant_dynamic-slice_fusion.4), channel_id=1, source_target_pairs={{0,2},{1,3},{2,4},{3,5},{4,6},{5,7},{6,0},{7,1},{8,10},{9,11},{10,... | collective-permute-start | bytes 786440 | tf_op jit(solution)/shard_map/ppermute | solution.py:65
  17.9 61.3 %collective-permute-start.1 = (bf16[256,512]{1,0:T(8,128)(2,1)S(1)}, bf16[256,512]{1,0:T(8,128)(2,1)S(1)}, u32[]{:S(2)}, u32[]{:S(2)}) collective-permute-start(bf16[256,512]{1,0:T(8,128)(2,1)S(1)} %constant_dynamic-slice_fusion.4), channel_id=1, source_target_pairs={{0,4},{1,5},{2,6},{3,7},{4,0},{5,1},{6,2},{7,3},{8,12},{9,13},{10,... | collective-permute-start | bytes 786440 | tf_op jit(solution)/shard_map/ppermute | solution.py:65
  25.2 54.0 %collective-permute-start.2 = (bf16[256,512]{1,0:T(8,128)(2,1)S(1)}, bf16[256,512]{1,0:T(8,128)(2,1)S(1)}, u32[]{:S(2)}, u32[]{:S(2)}) collective-permute-start(bf16[256,512]{1,0:T(8,128)(2,1)S(1)} %constant_dynamic-slice_fusion.4), channel_id=1, source_target_pairs={{0,6},{1,7},{2,0},{3,1},{4,2},{5,3},{6,4},{7,5},{8,14},{9,15},{10,... | collective-permute-start | bytes 786440 | tf_op jit(solution)/shard_map/ppermute | solution.py:65
  50.7 84.2 %collective-permute-start.27 = (bf16[1,3,576,512]{3,2,1,0:T(8,128)(2,1)S(1)}, bf16[1,3,576,512]{3,2,1,0:T(8,128)(2,1)}, u32[]{:S(2)}, u32[]{:S(2)}) collective-permute-start(bf16[1,3,576,512]{3,2,1,0:T(8,128)(2,1)S(1)} %maximum_bitcast_fusion), channel_id=1, source_target_pairs={{0,16},{8,24},{16,0},{24,8},{1,17},{9,25},{17,1},{25,9},{2,18},{10... | collective-permute-start | bytes 5308424 | tf_op jit(solution)/shard_map/ppermute | solution.py:75
  79.2 51.2 %collective-permute-start.3 = (bf16[1,3,256,512]{3,2,1,0:T(8,128)(2,1)S(1)}, bf16[1,3,256,512]{3,2,1,0:T(8,128)(2,1)S(1)}, u32[]{:S(2)}, u32[]{:S(2)}) collective-permute-start(bf16[1,3,256,512]{3,2,1,0:T(8,128)(2,1)S(1)} %maximum_bitcast_fusion.2), channel_id=1, source_target_pairs={{0,8},{8,0},{16,24},{24,16},{1,9},{9,1},{17,25},{25,17},{2,10},{10... | collective-permute-start | bytes 2359304 | tf_op jit(solution)/shard_map/ppermute | solution.py:75
  131.7 42.8 %collective-permute-start.4 = (bf16[2,3,256,512]{3,2,1,0:T(8,128)(2,1)}, bf16[2,3,256,512]{3,2,1,0:T(8,128)(2,1)}, u32[]{:S(2)}, u32[]{:S(2)}) collective-permute-start(bf16[2,3,256,512]{3,2,1,0:T(8,128)(2,1)} %pad_maximum_fusion.2.refs_1_), channel_id=1, source_target_pairs={{0,16},{8,24},{16,0},{24,8},{1,17},{9,25},{17,1},{25,9},{2,18},{10... | collective-permute-start | bytes 4718600 | tf_op jit(solution)/shard_map/ppermute | solution.py:75
  134.9 39.5 %collective-permute-start.14 = (bf16[2,3,144,512]{3,2,1,0:T(8,128)(2,1)S(1)}, bf16[2,3,144,512]{3,2,1,0:T(8,128)(2,1)S(1)}, u32[]{:S(2)}, u32[]{:S(2)}) collective-permute-start(bf16[2,3,144,512]{3,2,1,0:T(8,128)(2,1)S(1)} %pad_maximum_fusion.7.refs_1_), channel_id=1, source_target_pairs={{0,1},{1,0},{2,3},{3,2},{4,5},{5,4},{6,7},{7,6},{8,9},{9,8},{10,11... | collective-permute-start | bytes 2654216 | tf_op jit(solution)/shard_map/ppermute | solution.py:70
  136.7 109.6 %collective-permute-start.28 = (bf16[2,3,576,512]{3,2,1,0:T(8,128)(2,1)S(1)}, bf16[2,3,576,512]{3,2,1,0:T(8,128)(2,1)}, u32[]{:S(2)}, u32[]{:S(2)}) collective-permute-start(bf16[2,3,576,512]{3,2,1,0:T(8,128)(2,1)S(1)} %pad_maximum_fusion.refs_1_), channel_id=1, source_target_pairs={{0,8},{8,0},{16,24},{24,16},{1,9},{9,1},{17,25},{25,17},{2,10},{10... | collective-permute-start | bytes 10616840 | tf_op jit(solution)/shard_map/ppermute | solution.py:75
  172.8 41.2 %collective-permute-start.20 = (bf16[2,3,288,512]{3,2,1,0:T(8,128)(2,1)}, bf16[2,3,288,512]{3,2,1,0:T(8,128)(2,1)}, u32[]{:S(2)}, u32[]{:S(2)}) collective-permute-start(bf16[2,3,288,512]{3,2,1,0:T(8,128)(2,1)} %pad_maximum_fusion.1.refs_1_), channel_id=1, source_target_pairs={{0,16},{8,24},{16,0},{24,8},{1,17},{9,25},{17,1},{25,9},{2,18},{10... | collective-permute-start | bytes 5308424 | tf_op jit(solution)/shard_map/ppermute | solution.py:75
  174.5 39.5 %collective-permute-start.7 = (bf16[2,3,256,512]{3,2,1,0:T(8,128)(2,1)}, bf16[2,3,256,512]{3,2,1,0:T(8,128)(2,1)}, u32[]{:S(2)}, u32[]{:S(2)}) collective-permute-start(bf16[2,3,256,512]{3,2,1,0:T(8,128)(2,1)} %collective-permute-done.4.refs_2_), channel_id=1, source_target_pairs={{0,1},{1,0},{2,3},{3,2},{4,5},{5,4},{6,7},{7,6},{8,9},{9,8},{10,11... | collective-permute-start | bytes 4718600 | tf_op jit(solution)/shard_map/ppermute | solution.py:70
  187.6 112.0 %collective-permute-start.21 = (bf16[1152,512]{1,0:T(8,128)(2,1)}, bf16[1152,512]{1,0:T(8,128)(2,1)}, u32[]{:S(2)}, u32[]{:S(2)}) collective-permute-start(bf16[1152,512]{1,0:T(8,128)(2,1)} %pack.6.refs_0_), channel_id=1, source_target_pairs={{0,1},{1,0},{2,3},{3,2},{4,5},{5,4},{6,7},{7,6},{8,9},{9,8},{10,11... | collective-permute-start | bytes 3538952 | tf_op jit(solution)/shard_map/ppermute | solution.py:70
  188.1 124.1 %collective-permute-start.22 = (bf16[2,3,288,512]{3,2,1,0:T(8,128)(2,1)}, bf16[2,3,288,512]{3,2,1,0:T(8,128)(2,1)}, u32[]{:S(2)}, u32[]{:S(2)}) collective-permute-start(bf16[2,3,288,512]{3,2,1,0:T(8,128)(2,1)} %pad_maximum_fusion.1.refs_1_), channel_id=1, source_target_pairs={{0,1},{1,0},{2,3},{3,2},{4,5},{5,4},{6,7},{7,6},{8,9},{9,8},{10,11... | collective-permute-start | bytes 5308424 | tf_op jit(solution)/shard_map/ppermute | solution.py:70
  214.0 141.6 %collective-permute-start.30 = (bf16[2,3,576,512]{3,2,1,0:T(8,128)(2,1)S(1)}, bf16[2,3,576,512]{3,2,1,0:T(8,128)(2,1)}, u32[]{:S(2)}, u32[]{:S(2)}) collective-permute-start(bf16[2,3,576,512]{3,2,1,0:T(8,128)(2,1)S(1)} %pad_maximum_fusion.refs_1_), channel_id=1, source_target_pairs={{0,1},{1,0},{2,3},{3,2},{4,5},{5,4},{6,7},{7,6},{8,9},{9,8},{10,11... | collective-permute-start | bytes 10616840 | tf_op jit(solution)/shard_map/ppermute | solution.py:70
  214.0 98.2 %collective-permute-start.23 = (bf16[2,3,288,512]{3,2,1,0:T(8,128)(2,1)}, bf16[2,3,288,512]{3,2,1,0:T(8,128)(2,1)}, u32[]{:S(2)}, u32[]{:S(2)}) collective-permute-start(bf16[2,3,288,512]{3,2,1,0:T(8,128)(2,1)} %collective-permute-done.20.refs_2_), channel_id=1, source_target_pairs={{0,1},{1,0},{2,3},{3,2},{4,5},{5,4},{6,7},{7,6},{8,9},{9,8},{10,11... | collective-permute-start | bytes 5308424 | tf_op jit(solution)/shard_map/ppermute | solution.py:70
  246.4 109.3 %collective-permute-start.31 = (bf16[2,3,576,512]{3,2,1,0:T(8,128)(2,1)}, bf16[2,3,576,512]{3,2,1,0:T(8,128)(2,1)}, u32[]{:S(2)}, u32[]{:S(2)}) collective-permute-start(bf16[2,3,576,512]{3,2,1,0:T(8,128)(2,1)} %collective-permute-done.28.refs_2_), channel_id=1, source_target_pairs={{0,1},{1,0},{2,3},{3,2},{4,5},{5,4},{6,7},{7,6},{8,9},{9,8},{10,11... | collective-permute-start | bytes 10616840 | tf_op jit(solution)/shard_map/ppermute | solution.py:70
  299.5 56.1 %collective-permute-start.29 = (bf16[2304,512]{1,0:T(8,128)(2,1)}, bf16[2304,512]{1,0:T(8,128)(2,1)}, u32[]{:S(2)}, u32[]{:S(2)}) collective-permute-start(bf16[2304,512]{1,0:T(8,128)(2,1)} %pack.7.refs_0_), channel_id=1, source_target_pairs={{0,1},{1,0},{2,3},{3,2},{4,5},{5,4},{6,7},{7,6},{8,9},{9,8},{10,11... | collective-permute-start | bytes 7077896 | tf_op jit(solution)/shard_map/ppermute | solution.py:70
  353.0 106.0 %collective-permute-start.56 = (bf16[4,1152,512]{2,1,0:T(8,128)(2,1)}, bf16[4,1152,512]{2,1,0:T(8,128)(2,1)}, u32[]{:S(2)}, u32[]{:S(2)}) collective-permute-start(bf16[4,1152,512]{2,1,0:T(8,128)(2,1)} %get-tuple-element.115), channel_id=1, source_target_pairs={{0,1},{1,0},{2,3},{3,2},{4,5},{5,4},{6,7},{7,6},{8,9},{9,8},{10,11... | collective-permute-start | bytes 14155784 | tf_op jit(solution)/shard_map/ppermute | solution.py:70
  462.2 99.8 %collective-permute-start.57 = (bf16[4,2,288,512]{3,2,1,0:T(8,128)(2,1)S(1)}, bf16[4,2,288,512]{3,2,1,0:T(8,128)(2,1)}, u32[]{:S(2)}, u32[]{:S(2)}) collective-permute-start(bf16[4,2,288,512]{3,2,1,0:T(8,128)(2,1)S(1)} %fusion), channel_id=1, source_target_pairs={{0,8},{8,0},{16,24},{24,16},{1,9},{9,1},{17,25},{25,17},{2,10},{10... | collective-permute-start | bytes 7077896 | tf_op jit(solution)/shard_map/ppermute | solution.py:75
  462.8 179.9 %collective-permute-start.72 = (bf16[4,1152,512]{2,1,0:T(8,128)(2,1)}, bf16[4,1152,512]{2,1,0:T(8,128)(2,1)}, u32[]{:S(2)}, u32[]{:S(2)}) collective-permute-start(bf16[4,1152,512]{2,1,0:T(8,128)(2,1)} %get-tuple-element.119), channel_id=1, source_target_pairs={{0,1},{1,0},{2,3},{3,2},{4,5},{5,4},{6,7},{7,6},{8,9},{9,8},{10,11... | collective-permute-start | bytes 14155784 | tf_op jit(solution)/shard_map/ppermute | solution.py:70
  541.9 70.9 %collective-permute-start.37 = (bf16[4,960,512]{2,1,0:T(8,128)(2,1)}, bf16[4,960,512]{2,1,0:T(8,128)(2,1)}, u32[]{:S(2)}, u32[]{:S(2)}) collective-permute-start(bf16[4,960,512]{2,1,0:T(8,128)(2,1)} %get-tuple-element.110), channel_id=1, source_target_pairs={{0,1},{1,0},{2,3},{3,2},{4,5},{5,4},{6,7},{7,6},{8,9},{9,8},{10,11... | collective-permute-start | bytes 11796488 | tf_op jit(solution)/shard_map/ppermute | solution.py:70
  561.9 120.7 %collective-permute-start.64 = (bf16[4,1152,512]{2,1,0:T(8,128)(2,1)}, bf16[4,1152,512]{2,1,0:T(8,128)(2,1)}, u32[]{:S(2)}, u32[]{:S(2)}) collective-permute-start(bf16[4,1152,512]{2,1,0:T(8,128)(2,1)} %get-tuple-element.117), channel_id=1, source_target_pairs={{0,1},{1,0},{2,3},{3,2},{4,5},{5,4},{6,7},{7,6},{8,9},{9,8},{10,11... | collective-permute-start | bytes 14155784 | tf_op jit(solution)/shard_map/ppermute | solution.py:70
  567.6 41.3 %collective-permute-start.58 = (bf16[4,288,512]{2,1,0:T(8,128)(2,1)}, bf16[4,288,512]{2,1,0:T(8,128)(2,1)S(1)}, u32[]{:S(2)}, u32[]{:S(2)}) collective-permute-start(bf16[4,288,512]{2,1,0:T(8,128)(2,1)} %fusion.5), channel_id=1, source_target_pairs={{0,16},{8,24},{16,0},{24,8},{1,17},{9,25},{17,1},{25,9},{2,18},{10... | collective-permute-start | bytes 3538952 | tf_op jit(solution)/shard_map/ppermute | solution.py:75
  616.3 77.2 %collective-permute-start.38 = (bf16[4,2,240,512]{3,2,1,0:T(8,128)(2,1)}, bf16[4,2,240,512]{3,2,1,0:T(8,128)(2,1)}, u32[]{:S(2)}, u32[]{:S(2)}) collective-permute-start(bf16[4,2,240,512]{3,2,1,0:T(8,128)(2,1)} %fusion.6), channel_id=1, source_target_pairs={{0,8},{8,0},{16,24},{24,16},{1,9},{9,1},{17,25},{25,17},{2,10},{10... | collective-permute-start | bytes 5898248 | tf_op jit(solution)/shard_map/ppermute | solution.py:75
  641.4 39.8 %collective-permute-start.62 = (bf16[288,512]{1,0:T(8,128)(2,1)S(1)}, bf16[288,512]{1,0:T(8,128)(2,1)S(1)}, u32[]{:S(2)}, u32[]{:S(2)}) collective-permute-start(bf16[288,512]{1,0:T(8,128)(2,1)S(1)} %fusion.30), channel_id=1, source_target_pairs={{0,8},{8,0},{16,24},{24,16},{1,9},{9,1},{17,25},{25,17},{2,10},{10... | collective-permute-start | bytes 884744 | tf_op jit(solution)/shard_map/ppermute | solution.py:75
  646.0 133.9 %collective-permute-start.73 = (bf16[4,2,288,512]{3,2,1,0:T(8,128)(2,1)S(1)}, bf16[4,2,288,512]{3,2,1,0:T(8,128)(2,1)S(1)}, u32[]{:S(2)}, u32[]{:S(2)}) collective-permute-start(bf16[4,2,288,512]{3,2,1,0:T(8,128)(2,1)S(1)} %fusion.2), channel_id=1, source_target_pairs={{0,8},{8,0},{16,24},{24,16},{1,9},{9,1},{17,25},{25,17},{2,10},{10... | collective-permute-start | bytes 7077896 | tf_op jit(solution)/shard_map/ppermute | solution.py:75
  687.8 105.4 %collective-permute-start.65 = (bf16[4,2,288,512]{3,2,1,0:T(8,128)(2,1)S(1)}, bf16[4,2,288,512]{3,2,1,0:T(8,128)(2,1)S(1)}, u32[]{:S(2)}, u32[]{:S(2)}) collective-permute-start(bf16[4,2,288,512]{3,2,1,0:T(8,128)(2,1)S(1)} %fusion.1), channel_id=1, source_target_pairs={{0,16},{8,24},{16,0},{24,8},{1,17},{9,25},{17,1},{25,9},{2,18},{10... | collective-permute-start | bytes 7077896 | tf_op jit(solution)/shard_map/ppermute | solution.py:75
  690.2 67.8 %collective-permute-start.63 = (bf16[2,288,512]{2,1,0:T(8,128)(2,1)S(1)}, bf16[2,288,512]{2,1,0:T(8,128)(2,1)S(1)}, u32[]{:S(2)}, u32[]{:S(2)}) collective-permute-start(bf16[2,288,512]{2,1,0:T(8,128)(2,1)S(1)} %reverse_select_fusion.6), channel_id=1, source_target_pairs={{0,16},{8,24},{16,0},{24,8},{1,17},{9,25},{17,1},{25,9},{2,18},{10... | collective-permute-start | bytes 1769480 | tf_op jit(solution)/shard_map/ppermute | solution.py:75
  691.9 65.9 %collective-permute-start.54 = (bf16[144,512]{1,0:T(8,128)(2,1)S(1)}, bf16[144,512]{1,0:T(8,128)(2,1)S(1)}, u32[]{:S(2)}, u32[]{:S(2)}) collective-permute-start(bf16[144,512]{1,0:T(8,128)(2,1)S(1)} %fusion.44), channel_id=1, source_target_pairs={{0,16},{8,24},{16,0},{24,8},{1,17},{9,25},{17,1},{25,9},{2,18},{10... | collective-permute-start | bytes 442376 | tf_op jit(solution)/shard_map/ppermute | solution.py:75
  695.4 77.9 %collective-permute-start.39 = (bf16[4,240,512]{2,1,0:T(8,128)(2,1)S(1)}, bf16[4,240,512]{2,1,0:T(8,128)(2,1)S(1)}, u32[]{:S(2)}, u32[]{:S(2)}) collective-permute-start(bf16[4,240,512]{2,1,0:T(8,128)(2,1)S(1)} %fusion.7), channel_id=1, source_target_pairs={{0,16},{8,24},{16,0},{24,8},{1,17},{9,25},{17,1},{25,9},{2,18},{10... | collective-permute-start | bytes 2949128 | tf_op jit(solution)/shard_map/ppermute | solution.py:75
  825.6 43.2 %collective-permute-start.67 = (bf16[288,512]{1,0:T(8,128)(2,1)}, bf16[288,512]{1,0:T(8,128)(2,1)}, u32[]{:S(2)}, u32[]{:S(2)}) collective-permute-start(bf16[288,512]{1,0:T(8,128)(2,1)} %get-tuple-element.212), channel_id=1, source_target_pairs={{0,2},{1,3},{2,4},{3,5},{4,6},{5,7},{6,0},{7,1},{8,10},{9,11},{10,... | collective-permute-start | bytes 884744 | tf_op jit(solution)/shard_map/ppermute | solution.py:65
  (87 other events, 1652.3 us)

commit v2 on v1

--- a/solution.py
+++ b/solution.py
@@ -48,7 +48,7 @@
 
 
 def cost(flops, nbytes):
-    return pl.CostEstimate(flops=int(flops), bytes_accessed=int(nbytes), transcendentals=0)
+    return pl.CostEstimate(flops=int(flops) // 1000000000, bytes_accessed=int(nbytes) // 1000000, transcendentals=0)
 
 
 def whole(shape, space=None):
@@ -56,6 +56,34 @@
     return pl.BlockSpec(shape, lambda *_: zeros, pipeline_mode=pl.Buffered(1))
 
 
+def hold(values, after):
+    if not after:
+        return values
+    return lax.optimization_barrier((values, list(after)))[0]
+
+
+def kernel_call(
+    kernel, args, *, grid, in_specs, out_specs, out_shape, name, cost_estimate, prefetch=0, scratch=(), after=(), mib=56, aliases=None
+):
+    args = list(args)
+    args[0] = hold(args[0], after)
+    return pl.pallas_call(
+        kernel,
+        grid_spec=pltpu.PrefetchScalarGridSpec(
+            num_scalar_prefetch=prefetch,
+            grid=grid,
+            in_specs=list(in_specs),
+            out_specs=out_specs,
+            scratch_shapes=list(scratch),
+        ),
+        out_shape=out_shape,
+        compiler_params=params(mib),
+        cost_estimate=cost_estimate,
+        input_output_aliases=aliases or {},
+        name=name,
+    )(*args)
+
+
 def round_up(n, m):
     return -(-n // m) * m
 
@@ -63,6 +91,11 @@
 def shift_core_pairs(x, k):
     size = lax.axis_size("fsdp")
     return lax.ppermute(x, "fsdp", [(i, (i + 2 * k) % size) for i in range(size)])
+
+
+def core_groups():
+    size = lax.axis_size("fsdp")
+    return [list(range(c, size, 2)) for c in range(2)]
 
 
 def swap_core(x):
@@ -82,112 +115,222 @@
     return bits[first % len(bits) :] + bits[: first % len(bits)]
 
 
-def assemble_kernel(masks, places, idx_ref, *refs):
-    n_in = 6
-    ins, out, sems = refs[:n_in], refs[n_in], refs[n_in + 1]
-    own, low, high, own_c, low_c, high_c = ins
-    held = refs[n_in + 2]
+def stack_kernel(cuts, n_z, z_ref, *refs):
+    pieces, outs = refs[: -len(cuts)], refs[-len(cuts) :]
+    for (at, size), out in zip(cuts, outs):
+        for k in range(1, n_z):
+            if len(pieces) > 1:
+                out[0, k - 1] = pieces[k - 1][at : at + size, :]
+            else:
+                out[0, k - 1] = pieces[0][lax.rem(z_ref[0] + n_z - k, n_z), at : at + size, :]
+
+
+def assemble_kernel(masks, n_z, cuts, rows, idx_ref, *refs):
+    n_in = 2 * (1 + 2 * len(cuts))
+    out, sems, held = refs[n_in:]
     part, z, c = idx_ref[0], idx_ref[1], idx_ref[2]
-    half = len(masks) // 2
-    rows = low.shape[2]
-    n_z = places + 1
-    copies = []
-    for group, core in (((own, low, high), c), ((own_c, low_c, high_c), 1 - c)):
-        copies.append((group[0], held.at[2 * z + core]))
-        for j, mask in enumerate(masks):
-            source = group[1] if j < half else group[2]
-            at = pl.multiple_of((part ^ mask) * rows, 16)
-            for k in range(1, n_z):
-                zk = lax.rem(z + n_z - k, n_z)
-                copies.append((source.at[j % half, k - 1], held.at[2 * zk + core, pl.ds(at, rows)]))
-    started = []
-    for i, (source, target) in enumerate(copies):
-        copy = pltpu.make_async_copy(source, target, sems.at[i])
+    half = len(masks[0]) // 2
+    blocks, count = [], 0
+    for ins, core in ((refs[: n_in // 2], c), (refs[n_in // 2 : n_in], 1 - c)):
+        for k in range(n_z):
+            at_block = 2 * lax.rem(z + n_z - k, n_z) + core
+            found = []
+            if k == 0:
+                found.append((ins[0], held.at[at_block]))
+            else:
+                for i, (offset, size) in enumerate(cuts):
+                    for j, mask in enumerate(masks[i]):
+                        at = pl.multiple_of((part ^ mask) * rows + offset, 16)
+                        found.append(
+                            (ins[1 + 2 * i + j // half].at[j % half, k - 1], held.at[at_block, pl.ds(at, size)])
+                        )
+            copies = [pltpu.make_async_copy(a, b, sems.at[count + i]) for i, (a, b) in enumerate(found)]
+            count += len(copies)
+            for copy in copies:
+                copy.start()
+            blocks.append((at_block, copies))
+    written = []
+    for i, (at_block, copies) in enumerate(blocks):
+        for copy in copies:
+            copy.wait()
+        copy = pltpu.make_async_copy(held.at[at_block], out.at[at_block], sems.at[count + i])
         copy.start()
-        started.append(copy)
-    for copy in started:
+        written.append(copy)
+    for copy in written:
         copy.wait()
-    copy = pltpu.make_async_copy(held, out, sems.at[len(copies)])
-    copy.start()
-    copy.wait()
-
-
-def gather_packed(shard, first):
-    n_rep, n_f = lax.axis_size("replica"), lax.axis_size("fsdp")
-    n_z = n_f // 2
-    rows = shard.shape[0] // n_rep
-    part, place = lax.axis_index("replica"), lax.axis_index("fsdp")
-    own_c = swap_core(shard)
-    mine = lax.dynamic_slice_in_dim(shard, part * rows, rows, axis=0)
-    stack = jnp.stack([shift_core_pairs(mine, k) for k in range(1, n_z)])[None]
-    masks = [0]
-    order = bit_order(first)
-    for i, bit in enumerate(order):
-        received = swap_replica(stack, bit)
-        masks = masks + [m ^ bit for m in masks]
-        if i < len(order) - 1:
-            stack = jnp.concatenate([stack, received])
-    low, high = stack, received
-    low_c, high_c = swap_core(low), swap_core(high)
-    idx = jnp.stack([part, place // 2, place % 2]).astype(jnp.int32)
-    anyspec = pl.BlockSpec(memory_space=pl.ANY)
-    n_copies = 2 * (1 + n_rep * (n_z - 1))
-    return pl.pallas_call(
-        functools.partial(assemble_kernel, tuple(masks), n_z - 1),
-        out_shape=jax.ShapeDtypeStruct((n_f,) + shard.shape, bf16),
-        grid_spec=pltpu.PrefetchScalarGridSpec(
-            num_scalar_prefetch=1,
+
+
+class Gather:
+    def __init__(self, shard):
+        self.shard = shard
+        self.n_z = lax.axis_size("fsdp") // 2
+        self.rows = shard.shape[0] // lax.axis_size("replica")
+        half = round_up(self.rows // 2, 16)
+        self.cuts = ((0, half), (half, self.rows - half))
+        self.orders = [bit_order(i) for i in range(len(self.cuts))]
+        self.masks = [[0] for _ in self.cuts]
+
+    def start(self, mine, direct):
+        if direct:
+            self.pieces = [shift_core_pairs(mine, k) for k in range(1, self.n_z)]
+        else:
+            self.pieces = [lax.all_gather(mine, "fsdp", axis_index_groups=core_groups())]
+
+    def stack(self, after=()):
+        in_specs = [pl.BlockSpec(p.shape, (lambda i, _: (0, 0, 0)) if p.ndim == 3 else (lambda i, _: (0, 0))) for p in self.pieces]
+        shapes = [(1, self.n_z - 1, size, BLK) for _, size in self.cuts]
+        self.stacks = kernel_call(
+            functools.partial(stack_kernel, self.cuts, self.n_z),
+            [(lax.axis_index("fsdp") // 2).astype(jnp.int32)[None], *self.pieces],
+            prefetch=1,
             grid=(1,),
-            in_specs=[anyspec] * 6,
+            in_specs=in_specs,
+            out_specs=[pl.BlockSpec(shape, lambda i, _: (0, 0, 0, 0)) for shape in shapes],
+            out_shape=[jax.ShapeDtypeStruct(shape, bf16) for shape in shapes],
+            name="stack",
+            cost_estimate=cost(0, 4 * self.rows * BLK * (self.n_z - 1)),
+            after=after,
+        )
+        self.swap(0)
+
+    def swap(self, step):
+        self.received = [swap_replica(x, order[step]) for x, order in zip(self.stacks, self.orders)]
+        self.masks = [m + [v ^ order[step] for v in m] for m, order in zip(self.masks, self.orders)]
+
+    def double(self, after=()):
+        for step in range(1, len(self.orders[0])):
+            arrived = hold(self.received, after)
+            self.stacks = [jnp.concatenate(pair) for pair in zip(self.stacks, arrived)]
+            self.swap(step)
+
+    def swap_early(self):
+        self.own_c = swap_core(self.shard)
+        self.low_c = [swap_core(x) for x in self.stacks]
+
+    def settle(self, after):
+        self.received, self.own_c, self.low_c = hold((self.received, self.own_c, self.low_c), after)
+
+    def assemble(self, after=()):
+        place = lax.axis_index("fsdp")
+        idx = jnp.stack([lax.axis_index("replica"), place // 2, place % 2]).astype(jnp.int32)
+        ins = [self.shard]
+        other = [self.own_c]
+        high_c = [swap_core(x) for x in self.received]
+        for pair in zip(self.stacks, self.received):
+            ins += pair
+        for pair in zip(self.low_c, high_c):
+            other += pair
+        n_f = lax.axis_size("fsdp")
+        n_copies = 2 * (1 + len(self.cuts) * len(self.masks[0]) * (self.n_z - 1))
+        anyspec = pl.BlockSpec(memory_space=pl.ANY)
+        return kernel_call(
+            functools.partial(assemble_kernel, self.masks, self.n_z, self.cuts, self.rows),
+            [idx, *ins, *other],
+            prefetch=1,
+            grid=(1,),
+            in_specs=[anyspec] * (2 * len(ins)),
             out_specs=anyspec,
-            scratch_shapes=[
-                pltpu.SemaphoreType.DMA((n_copies + 1,)),
-                pltpu.VMEM((n_f,) + shard.shape, bf16),
+            out_shape=jax.ShapeDtypeStruct((n_f,) + self.shard.shape, bf16),
+            scratch=[
+                pltpu.SemaphoreType.DMA((n_copies + n_f,)),
+                pltpu.VMEM((n_f,) + self.shard.shape, bf16),
             ],
-        ),
-        compiler_params=params(),
-        cost_estimate=cost(0, 4 * n_f * shard.size),
-        name="assemble",
-    )(idx, shard, low, high, own_c, low_c, high_c)
-
-
-def reduce_packed(keep, send, first):
-    n_rep, n_z = lax.axis_size("replica"), lax.axis_size("fsdp") // 2
-    part, place = lax.axis_index("replica"), lax.axis_index("fsdp")
-    z = place // 2
-    rows = keep.shape[1] // n_rep
-    order = bit_order(first)
-    n_bits = len(order)
-    shape = (n_z,) + (2,) * n_bits + (rows, BLK)
-    bits = [1 << b for b in range(n_bits)]
-    live = list(reversed(bits))
-    terms = [keep.reshape(shape), swap_core(send).reshape(shape)]
-
-    def part_sum(index, axis):
-        return functools.reduce(
-            jnp.add, [lax.dynamic_index_in_dim(t, index, axis, keepdims=False).astype(f32) for t in terms]
+            name="assemble",
+            cost_estimate=cost(0, 4 * n_f * self.shard.size),
+            after=after,
         )
 
-    for bit in order:
-        axis = 1 + live.index(bit)
-        live.remove(bit)
-        own = (part // bit) % 2
-        got = swap_replica(part_sum(1 - own, axis).astype(bf16), bit)
-        terms = [lax.dynamic_index_in_dim(t, own, axis, keepdims=False) for t in terms] + [got]
-    gots = [shift_core_pairs(part_sum((z + k) % n_z, 0).astype(bf16), k) for k in range(1, n_z)]
-    summed = part_sum(z, 0)
-    for got in gots:
-        summed = summed + got.astype(f32)
-    stack = summed.astype(bf16)
-    done = []
-    for bit in order:
-        got = swap_replica(stack, bit)
-        own = (part // bit) % 2
-        pair = jnp.stack([stack, got])
-        stack = jnp.where(own == 1, pair[::-1], pair)
-    names = list(reversed(order))
-    stack = jnp.transpose(stack, tuple(names.index(b) for b in reversed(bits)) + (n_bits, n_bits + 1))
-    return stack.reshape(n_rep * rows, BLK)
+
+class Reduce:
+    def __init__(self, keep, received, first=0):
+        n_rep, self.n_z = lax.axis_size("replica"), lax.axis_size("fsdp") // 2
+        self.part, self.z = lax.axis_index("replica"), lax.axis_index("fsdp") // 2
+        self.rows = keep.shape[1] // n_rep
+        n_bits = len(bit_order(0))
+        self.bits = [1 << b for b in range(n_bits)]
+        self.order = bit_order(first)
+        shape = (self.n_z,) + (2,) * n_bits + (self.rows, BLK)
+        half = round_up(self.rows // 2, 16)
+        self.cuts = ((0, half), (half, self.rows - half))
+        self.orders = [bit_order(i) for i in range(len(self.cuts))]
+        self.live = [list(reversed(self.bits)) for _ in self.cuts]
+        self.terms = [[keep.reshape(shape)] for _ in self.cuts]
+        self.newest = [received.reshape(shape)]
+        halves = [functools.partial(self.halve, i) for i in range(n_bits)]
+        gathers = [functools.partial(self.gather, i, bit) for i, bit in enumerate(self.order)]
+        self.todo = [halves[:1], halves[1:], [self.along], gathers[:1], gathers[1:]]
+
+    def step(self, after=()):
+        self.newest = hold(self.newest, after)
+        for action in self.todo.pop(0):
+            sent = action()
+        return sent
+
+    def part_sum(self, terms):
+        return functools.reduce(jnp.add, [t.astype(f32) for t in terms])
+
+    def halve(self, i):
+        news, marks = [], []
+        for p, (at, size) in enumerate(self.cuts):
+            self.terms[p] = self.terms[p] + [self.newest[p % len(self.newest)]]
+            bit = self.orders[p][i]
+            axis = 1 + self.live[p].index(bit)
+            self.live[p].remove(bit)
+            own = (self.part // bit) % 2
+
+            def take(t, index):
+                starts, sizes = [0] * t.ndim, list(t.shape)
+                starts[axis], sizes[axis] = index, 1
+                if i == 0:
+                    starts[-2], sizes[-2] = at, size
+                out = lax.dynamic_slice(t, starts, sizes)
+                return out.reshape(out.shape[:axis] + out.shape[axis + 1 :])
+
+            away = self.part_sum([take(t, 1 - own) for t in self.terms[p]]).astype(bf16)
+            self.terms[p] = [take(t, own) for t in self.terms[p]]
+            news.append(swap_replica(away, bit))
+            marks.append(away)
+        self.newest = news
+        return marks
+
+    def at_place(self, z):
+        parts = [
+            self.part_sum([lax.dynamic_index_in_dim(t, z, 0, keepdims=False) for t in terms]) for terms in self.terms
+        ]
+        return jnp.concatenate(parts)
+
+    def along(self):
+        self.terms = [terms + [new] for terms, new in zip(self.terms, self.newest)]
+        aways = [self.at_place((self.z + k) % self.n_z).astype(bf16) for k in range(1, self.n_z)]
+        self.newest = [shift_core_pairs(away, k) for k, away in enumerate(aways, 1)]
+        return aways
+
+    def gather(self, i, bit):
+        if i == 0:
+            summed = self.at_place(self.z)
+            for got in self.newest:
+                summed = summed + got.astype(f32)
+            self.have = summed.astype(bf16)
+        else:
+            self.have = self.joined()
+        self.newest, self.bit = [swap_replica(self.have, bit)], bit
+        return [self.have]
+
+    def joined(self):
+        pair = jnp.stack([self.have, self.newest[0]])
+        return jnp.where((self.part // self.bit) % 2 == 1, pair[::-1], pair)
+
+    def result(self, after=()):
+        self.newest = hold(self.newest, after)
+        stack = self.joined()
+        names = list(reversed(self.order))
+        n_bits = len(names)
+        stack = jnp.transpose(stack, tuple(names.index(b) for b in reversed(self.bits)) + (n_bits, n_bits + 1))
+        return stack.reshape(-1, BLK)
+
+
+def pair_sum(keep, got):
+    return (keep.astype(f32) + got.astype(f32)).astype(bf16)
 
 
 def sum_small(x):
@@ -199,56 +342,62 @@
     return x
 
 
-def sum_all(x):
-    x = sum_small(x)
-    bit = 1
-    while bit < lax.axis_size("replica"):
-        x = x + swap_replica(x, bit)
-        bit *= 2
-    return x
-
-
-def pack_kernel(counts, *refs):
-    out = refs[-1]
+def pack_kernel(counts, has_extra, has_before, prefix_ref, *refs):
+    n = len(counts) + has_extra + has_before
+    out = refs[n]
     at = 0
-    for ref, n in zip(refs, counts):
+    for ref, count in zip(refs, counts):
         value = ref[0] if len(ref.shape) == 3 else ref[...]
-        for j in range(n):
+        for j in range(count):
             out[at : at + value.shape[0], :] = value[:, j * BLK : (j + 1) * BLK].astype(bf16)
             at += value.shape[0]
-    if len(refs) - 1 > len(counts):
+    if has_extra:
         extra = refs[len(counts)][...]
         out[at : at + extra.shape[0], :] = extra
         at += extra.shape[0]
     if at < out.shape[0]:
         out[at:, :] = jnp.zeros((out.shape[0] - at, BLK), bf16)
-
-
-def pack_call(parts, unit, extra=None):
+    mine = refs[n + 1]
+    rows = mine.shape[0]
+    mine[...] = out[pl.ds(pl.multiple_of(prefix_ref[0] * rows, 16), rows), :]
+    if has_before:
+        refs[n + 2][...] = refs[n - 1][...]
+
+
+def pack_call(parts, unit, extra=None, before=None, after=()):
     specs, counts, total = [], [], 0
     for w, e in parts:
         if e is None:
-            specs.append(pl.BlockSpec(w.shape, lambda i: (0, 0)))
+            specs.append(pl.BlockSpec(w.shape, lambda i, _: (0, 0)))
         else:
-            specs.append(pl.BlockSpec((1,) + w.shape[1:], lambda i, e=e: (e, 0, 0)))
+            specs.append(pl.BlockSpec((1,) + w.shape[1:], lambda i, _, e=e: (e, 0, 0)))
         counts.append(w.shape[-1] // BLK)
         total += counts[-1] * w.shape[-2]
-    args = [w for w, _ in parts]
+    part = lax.axis_index("replica").astype(jnp.int32)[None]
+    args = [part] + [w for w, _ in parts]
     if extra is not None:
         args.append(extra)
-        specs.append(pl.BlockSpec(extra.shape, lambda i: (0, 0)))
+        specs.append(pl.BlockSpec(extra.shape, lambda i, _: (0, 0)))
         total += extra.shape[0]
     total = round_up(total, unit)
-    return pl.pallas_call(
-        functools.partial(pack_kernel, tuple(counts)),
+    n_rep = lax.axis_size("replica")
+    shapes = [(total, BLK), (total // n_rep, BLK)]
+    if before is not None:
+        shapes.append((before.shape[0] // n_rep, BLK))
+        args.append(before)
+        specs.append(pl.BlockSpec(shapes[-1], lambda i, part: (part[0], 0)))
+    return kernel_call(
+        functools.partial(pack_kernel, tuple(counts), extra is not None, before is not None),
+        args,
+        prefetch=1,
         grid=(1,),
         in_specs=specs,
-        out_specs=pl.BlockSpec((total, BLK), lambda i: (0, 0)),
-        out_shape=jax.ShapeDtypeStruct((total, BLK), bf16),
-        compiler_params=params(),
+        out_specs=[pl.BlockSpec(shape, lambda i, _: (0, 0)) for shape in shapes],
+        out_shape=[jax.ShapeDtypeStruct(shape, bf16) for shape in shapes],
         cost_estimate=cost(0, 6 * total * BLK),
         name="pack",
-    )(*args)
+        after=after,
+    )
 
 
 def pad_rows(x, rows):
@@ -279,11 +428,12 @@
     lax.fori_loop(0, tokens // 256, body, 0)
 
 
-def qkv_call(x, gain, w_in, rows, n):
+def qkv_call(x, gain, w_in, rows, n, after=()):
     tokens, width = x.shape
     n_f = w_in.shape[0]
-    return pl.pallas_call(
+    return kernel_call(
         qkv_kernel,
+        [x, gain, w_in],
         grid=(n,),
         in_specs=[
             whole((tokens, width)),
@@ -298,10 +448,10 @@
             jax.ShapeDtypeStruct((tokens, n * BLK), bf16),
             jax.ShapeDtypeStruct((tokens, width), bf16),
         ],
-        compiler_params=params(),
         cost_estimate=cost(2 * tokens * width * n * BLK, 2 * width * n * BLK + 4 * tokens * width),
         name="qkv",
-    )(x, gain, w_in)
+        after=after,
+    )
 
 
 HALF = 256
@@ -331,7 +481,7 @@
             mix_ref[start:stop, lanes] = mixed.T.astype(bf16)
 
 
-def attention_call(lengths, qkv, n_seq):
+def attention_call(lengths, qkv, n_seq, after=()):
     tokens = qkv.shape[0]
     seq = tokens // n_seq
     pairs = KEY_VALUE_HEADS // 2
@@ -340,10 +490,10 @@
     kw = 2 * HEAD_SIZE
     k_at = QUERY_HEADS * HEAD_SIZE // kw
     v_at = k_at + pairs
-    return pl.pallas_call(
+    return kernel_call(
         attention_kernel,
-        grid_spec=pltpu.PrefetchScalarGridSpec(
-            num_scalar_prefetch=1,
+        [lengths, qkv, qkv, qkv],
+            prefetch=1,
             grid=(n_seq, pairs),
             in_specs=[
                 pl.BlockSpec((seq, qw), lambda s, j, _: (s, j)),
@@ -354,15 +504,14 @@
                 pl.BlockSpec((1, heads, seq, seq), lambda s, j, _: (s, j, 0, 0)),
                 pl.BlockSpec((seq, qw), lambda s, j, _: (s, j)),
             ],
-        ),
         out_shape=[
             jax.ShapeDtypeStruct((n_seq, QUERY_HEADS, seq, seq), bf16),
             jax.ShapeDtypeStruct((tokens, QUERY_HEADS * HEAD_SIZE), bf16),
         ],
-        compiler_params=params(),
         cost_estimate=cost(16 * n_seq * QUERY_HEADS * seq * seq * HEAD_SIZE, 2 * n_seq * QUERY_HEADS * seq * seq),
         name="attention",
-    )(lengths, qkv, qkv, qkv)
+        after=after,
+    )
 
 
 def attention_back_kernel(q_ref, k_ref, v_ref, p_ref, mix_ref, dmix_ref, dq_ref, dk_ref, dv_ref):
@@ -404,7 +553,7 @@
             dv_ref[rows, kv] = dv[m].astype(bf16)
 
 
-def attention_back_call(qkv, probs, mixed, dmixed, n_seq):
+def attention_back_call(qkv, probs, mixed, dmixed, n_seq, after=()):
     tokens = qkv.shape[0]
     seq = tokens // n_seq
     pairs = KEY_VALUE_HEADS // 2
@@ -415,8 +564,9 @@
     v_at = k_at + pairs
     qspec = pl.BlockSpec((seq, qw), lambda s, j: (s, j))
     kspec = pl.BlockSpec((seq, kw), lambda s, j: (s, j))
-    return pl.pallas_call(
+    return kernel_call(
         attention_back_kernel,
+        [qkv, qkv, qkv, probs, mixed, dmixed],
         grid=(n_seq, pairs),
         in_specs=[
             qspec,
@@ -432,10 +582,10 @@
             jax.ShapeDtypeStruct((tokens, KEY_VALUE_HEADS * HEAD_SIZE), bf16),
             jax.ShapeDtypeStruct((tokens, KEY_VALUE_HEADS * HEAD_SIZE), bf16),
         ],
-        compiler_params=params(),
         cost_estimate=cost(32 * n_seq * QUERY_HEADS * seq * seq * HEAD_SIZE, 2 * n_seq * QUERY_HEADS * seq * seq),
         name="attention_back",
-    )(qkv, qkv, qkv, probs, mixed, dmixed)
+        after=after,
+    )
 
 
 TILE = 256
@@ -460,15 +610,16 @@
     prob_ref[...] = raised / jnp.sum(raised, axis=0, keepdims=True)
 
 
-def resid_call(mixed, w_out, x, gain, router, rows, n):
+def resid_call(mixed, w_out, at, x, gain, router, rows, n, after=()):
     tokens, width = x.shape
     tile = pl.BlockSpec((TILE, width), lambda i: (i, 0))
-    return pl.pallas_call(
+    return kernel_call(
         functools.partial(resid_kernel, rows, n),
+        [mixed, w_out, x, gain, router],
         grid=(tokens // TILE,),
         in_specs=[
             tile,
-            whole((w_out.shape[0], n * rows, BLK)),
+            pl.BlockSpec((w_out.shape[0], n * rows, BLK), lambda i: (0, at, 0), pipeline_mode=pl.Buffered(1)),
             tile,
             whole((1, width)),
             whole((8, width)),
@@ -479,10 +630,10 @@
             jax.ShapeDtypeStruct((tokens, width), bf16),
             jax.ShapeDtypeStruct((8, tokens), f32),
         ],
-        compiler_params=params(),
         cost_estimate=cost(2 * tokens * width * width, 2 * width * width + 12 * tokens * width),
         name="resid",
-    )(mixed, w_out, x, gain, router)
+        after=after,
+    )
 
 
 def dispatch_kernel(slot_ref, prob_ref, n2_ref, cot_ref, buf_ref, dys_ref, gate_ref):
@@ -496,12 +647,13 @@
     dys_ref[0, 0] = dot(hit, cot_ref[...]).astype(bf16)
 
 
-def dispatch_call(slots, prob, n2, cot, n_seq):
+def dispatch_call(slots, prob, n2, cot, n_seq, after=()):
     tokens, width = n2.shape
     seq = tokens // n_seq
     out = pl.BlockSpec((1, 1, CAP, width), lambda s, e: (e, s, 0, 0))
-    return pl.pallas_call(
+    return kernel_call(
         dispatch_kernel,
+        [slots, prob, n2, cot],
         grid=(n_seq, E),
         in_specs=[
             pl.BlockSpec((1, 8, seq), lambda s, e: (s, 0, 0)),
@@ -515,10 +667,10 @@
             jax.ShapeDtypeStruct((E, n_seq, CAP, width), bf16),
             jax.ShapeDtypeStruct((E, n_seq, CAP, 128), f32),
         ],
-        compiler_params=params(),
         cost_estimate=cost(4 * E * CAP * tokens * width, 20 * tokens * width),
         name="dispatch",
-    )(slots, prob, n2, cot)
+        after=after,
+    )
 
 
 def split_cores(block, c, rows):
@@ -657,7 +809,7 @@
                 copy.wait()
 
 
-def expert_call(e, at, core, buf, dys, gates, slots, w, up_rows, down_rows, unit):
+def expert_call(e, at, core, buf, dys, gates, slots, w, up_rows, down_rows, unit, after=()):
     _, n_seq, _, width = buf.shape
     n_f = w.shape[0]
     n_z = n_f // 2
@@ -670,10 +822,10 @@
     total = round_up(2 * n_h * up_rows + n_d * down_rows, unit)
     grad_shape = jax.ShapeDtypeStruct((n_z, total, BLK), bf16)
     rows = n_seq * CAP
-    yg, dbuf, dgate, keep, send = pl.pallas_call(
+    yg, dbuf, dgate, keep, send = kernel_call(
         functools.partial(expert_kernel, e, up_rows, down_rows),
-        grid_spec=pltpu.PrefetchScalarGridSpec(
-            num_scalar_prefetch=1,
+        [core, buf, dys, gates, slots, w, w, w],
+            prefetch=1,
             grid=(n_h,),
             in_specs=[
                 data,
@@ -694,7 +846,7 @@
                 anyspec,
                 anyspec,
             ],
-            scratch_shapes=[
+            scratch=[
                 pltpu.VMEM((rows, width), f32),
                 pltpu.VMEM((rows, width), f32),
                 pltpu.VMEM((rows, width), bf16),
@@ -706,7 +858,6 @@
                 pltpu.VMEM((n_h, 2, n_z // n_h, n_d * down_rows, BLK), bf16),
                 pltpu.SemaphoreType.DMA((n_h, 6)),
             ],
-        ),
         out_shape=[
             jax.ShapeDtypeStruct((n_seq, CAP, width), bf16),
             jax.ShapeDtypeStruct((n_seq, CAP, width), bf16),
@@ -714,11 +865,12 @@
             grad_shape,
             grad_shape,
         ],
-        compiler_params=params(60),
+        mib=60,
         cost_estimate=cost(18 * rows * width * FE, 40 * width * FE),
         name="expert",
-    )(core, buf, dys, gates, slots, w, w, w)
-    return yg, dbuf, dgate[:, 0], keep, send
+        after=after,
+    )
+    return yg, dbuf, dgate, keep, send
 
 
 def spread(col_ref, e):
@@ -734,21 +886,22 @@
     out_ref[...] = jnp.where(col_ref[:, E : E + 1] > 0, total, 0.0).astype(bf16)
 
 
-def combine_call(cols, resid, ys, n_seq):
+def combine_call(cols, resid, ys, n_seq, after=()):
     tokens, width = resid.shape
     per = tokens // n_seq // TILE
     tile = pl.BlockSpec((TILE, width), lambda i: (i, 0))
-    return pl.pallas_call(
+    return kernel_call(
         combine_kernel,
+        [cols, resid, *ys],
         grid=(tokens // TILE,),
         in_specs=[pl.BlockSpec((TILE, 8), lambda i: (i, 0)), tile]
         + [pl.BlockSpec((1, CAP, width), lambda i: (i // per, 0, 0))] * E,
         out_specs=tile,
         out_shape=jax.ShapeDtypeStruct((tokens, width), bf16),
-        compiler_params=params(),
         cost_estimate=cost(2 * E * CAP * tokens * width, 12 * tokens * width),
         name="combine",
-    )(cols, resid, *ys)
+        after=after,
+    )
 
 
 def hi_lo(x):
@@ -763,8 +916,10 @@
     d0_ref,
     d1_ref,
     d2_ref,
+    g0_ref,
+    g1_ref,
+    g2_ref,
     prob_ref,
-    dprob_ref,
     router_ref,
     n2_ref,
     resid_ref,
@@ -776,23 +931,25 @@
     dmix_ref,
     small_ref,
 ):
-    width = resid_ref.shape[1]
 
     @pl.when(pl.program_id(0) == 0)
     def _():
         small_ref[...] = jnp.zeros_like(small_ref)
 
-    prob, dprob = prob_ref[...], dprob_ref[...]
+    prob = prob_ref[...]
+    expert = lax.broadcasted_iota(jnp.int32, prob.shape, 0)
+    dprob = jnp.zeros_like(prob)
+    for e, g_ref in enumerate((g0_ref, g1_ref, g2_ref)):
+        dprob = jnp.where(expert == e, g_ref[0], dprob)
     dlogit = prob * (dprob - jnp.sum(dprob * prob, axis=0, keepdims=True))
     high, low = hi_lo(dlogit)
     dn2 = dot_first(high, router_ref[...]) + dot_first(low, router_ref[...])
     for e, d_ref in enumerate((d0_ref, d1_ref, d2_ref)):
         dn2 += dot(spread(col_ref, e), d_ref[0])
     n2 = n2_ref[...]
-    small_ref[:8, :] += dot(high, n2) + dot(low, n2)
+    small_ref[...] += dot(high, n2) + dot(low, n2)
     resid = resid_ref[...]
     scale = lax.rsqrt(jnp.mean(resid * resid, axis=-1, keepdims=True) + epsilon)
-    small_ref[8:, :] += jnp.broadcast_to(jnp.sum(dn2 * resid * scale, axis=0, keepdims=True), (8, width))
     weighted = dn2 * gain_ref[...]
     along = jnp.mean(weighted * resid, axis=-1, keepdims=True)
     dy = jnp.where(col_ref[:, E : E + 1] > 0, cot_ref[...].astype(f32), 0.0)
@@ -807,40 +964,42 @@
     dmix_ref[...] = dmix.astype(bf16)
 
 
-def middle_call(cols, ds, prob, dprob, router, n2, resid, cot, gain, w_out, rows, n, n_seq):
+def middle_call(cols, ds, dgates, prob, router, n2, resid, cot, gain, w_out, at, rows, n, n_seq, after=()):
     tokens, width = resid.shape
     per = tokens // n_seq // TILE
     tile = pl.BlockSpec((TILE, width), lambda i: (i, 0))
     row8 = pl.BlockSpec((8, TILE), lambda i: (0, i))
-    return pl.pallas_call(
+    return kernel_call(
         functools.partial(middle_kernel, rows, n),
+        [cols, *ds, *dgates, prob, router, n2, resid, cot, gain, w_out],
         grid=(tokens // TILE,),
         in_specs=[pl.BlockSpec((TILE, 8), lambda i: (i, 0))]
         + [pl.BlockSpec((1, CAP, width), lambda i: (i // per, 0, 0))] * E
+        + [pl.BlockSpec((1, 8, TILE), lambda i: (i // per, 0, i % per))] * E
         + [
-            row8,
             row8,
             whole((8, width)),
             tile,
             tile,
             tile,
             whole((1, width)),
-            whole((w_out.shape[0], n * rows, BLK)),
+            pl.BlockSpec((w_out.shape[0], n * rows, BLK), lambda i: (0, at, 0), pipeline_mode=pl.Buffered(1)),
         ],
-        out_specs=[tile, tile, tile, pl.BlockSpec((16, width), lambda i: (0, 0))],
+        out_specs=[tile, tile, tile, pl.BlockSpec((8, width), lambda i: (0, 0))],
         out_shape=[
             jax.ShapeDtypeStruct((tokens, width), f32),
             jax.ShapeDtypeStruct((tokens, width), bf16),
             jax.ShapeDtypeStruct((tokens, width), bf16),
-            jax.ShapeDtypeStruct((16, width), f32),
+            jax.ShapeDtypeStruct((8, width), f32),
         ],
-        compiler_params=params(),
         cost_estimate=cost(2 * tokens * width * (width + E * CAP), 20 * tokens * width),
         name="middle",
-    )(cols, *ds, prob, dprob, router, n2, resid, cot, gain, w_out)
-
-
-def weight_grad_kernel(rows, idx_ref, left_ref, right_ref, keep_ref, send_ref, turned_ref):
+        after=after,
+    )
+
+
+def weight_grad_kernel(rows, n_old, idx_ref, left_ref, right_ref, *refs):
+    keep_ref, send_ref, turned_ref = refs[n_old:]
     c = idx_ref[0]
     width = left_ref.shape[1]
     step = 384
@@ -858,55 +1017,50 @@
         send_ref[m * per : (m + 1) * per] = send
 
 
-def weight_grad_call(core, left, right, rows, n_z, name):
+def weight_grad_call(core, left, right, rows, n_z, total, at, name, old=(), after=()):
     tokens, width = left.shape
     n = right.shape[1] // BLK
-    out = pl.BlockSpec((n_z, rows, BLK), lambda j, _: (0, j, 0))
-    shape = jax.ShapeDtypeStruct((n_z, n * rows, BLK), bf16)
-    return pl.pallas_call(
-        functools.partial(weight_grad_kernel, rows),
-        grid_spec=pltpu.PrefetchScalarGridSpec(
-            num_scalar_prefetch=1,
-            grid=(n,),
-            in_specs=[
-                pl.BlockSpec((tokens, width), lambda j, _: (0, 0), pipeline_mode=pl.Buffered(1)),
-                pl.BlockSpec((tokens, BLK), lambda j, _: (0, j)),
-            ],
-            out_specs=[out, out],
-            scratch_shapes=[pltpu.VMEM((width, tokens), bf16)],
-        ),
+    out = pl.BlockSpec((n_z, rows, BLK), lambda j, _: (0, at + j, 0))
+    shape = jax.ShapeDtypeStruct((n_z, total, BLK), bf16)
+    return kernel_call(
+        functools.partial(weight_grad_kernel, rows, len(old)),
+        [core, left, right, *old],
+        prefetch=1,
+        grid=(n,),
+        in_specs=[
+            pl.BlockSpec((tokens, width), lambda j, _: (0, 0), pipeline_mode=pl.Buffered(1)),
+            pl.BlockSpec((tokens, BLK), lambda j, _: (0, j)),
+        ]
+        + [pl.BlockSpec(memory_space=pl.ANY)] * len(old),
+        out_specs=[out, out],
+        scratch=[pltpu.VMEM((width, tokens), bf16)],
         out_shape=[shape, shape],
-        compiler_params=params(),
         cost_estimate=cost(2 * tokens * width * n * BLK, 2 * width * n * BLK + 4 * tokens * width),
+        aliases={3 + i: i for i in range(len(old))},
         name=name,
-    )(core, left, right)
-
-
-def input_grad_kernel(rows, n, d_ref, w_ref, x_ref, dresid_ref, gain_ref, out_ref, small_ref):
-    width = x_ref.shape[1]
-
-    @pl.when(pl.program_id(0) == 0)
-    def _():
-        small_ref[...] = jnp.zeros_like(small_ref)
-
+        after=after,
+    )
+
+
+def input_grad_kernel(rows, n, d_ref, w_ref, x_ref, dresid_ref, gain_ref, out_ref):
     dn1 = dot_last(d_ref[:, :BLK], w_ref[:, :rows, :].reshape(-1, BLK))
     for j in range(1, n):
         w = w_ref[:, j * rows : (j + 1) * rows, :].reshape(-1, BLK)
         dn1 += dot_last(d_ref[:, j * BLK : (j + 1) * BLK], w)
     x = x_ref[...].astype(f32)
     scale = lax.rsqrt(jnp.mean(x * x, axis=-1, keepdims=True) + epsilon)
-    small_ref[...] += jnp.broadcast_to(jnp.sum(dn1 * x * scale, axis=0, keepdims=True), (8, width))
     weighted = dn1 * gain_ref[...]
     along = jnp.mean(weighted * x, axis=-1, keepdims=True)
     out = dresid_ref[...] + scale * weighted - x * (scale * scale * scale * along)
     out_ref[...] = out.astype(bf16)
 
 
-def input_grad_call(dqkv, w_in, x, dresid, gain, rows, n):
+def input_grad_call(dqkv, w_in, x, dresid, gain, rows, n, after=()):
     tokens, width = x.shape
     tile = pl.BlockSpec((TILE, width), lambda i: (i, 0))
-    return pl.pallas_call(
+    return kernel_call(
         functools.partial(input_grad_kernel, rows, n),
+        [dqkv, w_in, x, dresid, gain],
         grid=(tokens // TILE,),
         in_specs=[
             pl.BlockSpec((TILE, n * BLK), lambda i: (i, 0)),
@@ -915,15 +1069,12 @@
             tile,
             whole((1, width)),
         ],
-        out_specs=[tile, pl.BlockSpec((8, width), lambda i: (0, 0))],
-        out_shape=[
-            jax.ShapeDtypeStruct((tokens, width), bf16),
-            jax.ShapeDtypeStruct((8, width), f32),
-        ],
-        compiler_params=params(),
+        out_specs=tile,
+        out_shape=jax.ShapeDtypeStruct((tokens, width), bf16),
         cost_estimate=cost(2 * tokens * width * n * BLK, 2 * width * n * BLK + 12 * tokens * width),
         name="input_grad",
-    )(dqkv, w_in, x, dresid, gain)
+        after=after,
+    )
 
 
 def adam_step(master, first, second, gradient, clip, decayed):
@@ -937,44 +1088,43 @@
     return (gradient, update, first_new, second_new)
 
 
-def adam_kernel(scale, clip_ref, g_ref, master_ref, first_ref, second_ref, *outs):
+def adam_kernel(scale, which, clip_ref, g_ref, master_ref, first_ref, second_ref, *outs):
     gradient = g_ref[...].astype(f32) * scale
-    results = adam_step(master_ref[...], first_ref[...], second_ref[...], gradient, clip_ref[0], 1.0)
+    results = adam_step(master_ref[...], first_ref[...], second_ref[...], gradient, clip_ref[0, which], 1.0)
     for out, result in zip(outs, results):
         out[...] = result
 
 
-def adam_call(clip, packed, at, master, first, second, scale, name):
+def adam_call(clip, which, packed, at, master, first, second, scale, name, after=()):
     rows, cols = master.shape
     natural = pl.BlockSpec((rows, BLK), lambda j, _: (0, j))
     shape = jax.ShapeDtypeStruct(master.shape, f32)
-    return pl.pallas_call(
-        functools.partial(adam_kernel, scale),
-        grid_spec=pltpu.PrefetchScalarGridSpec(
-            num_scalar_prefetch=1,
+    return kernel_call(
+        functools.partial(adam_kernel, scale, which),
+        [clip, packed, master, first, second],
+            prefetch=1,
             grid=(cols // BLK,),
             in_specs=[pl.BlockSpec((rows, BLK), lambda j, _: (at // rows + j, 0)), natural, natural, natural],
             out_specs=[natural] * 4,
-        ),
         out_shape=[shape] * 4,
-        compiler_params=params(),
         cost_estimate=cost(20 * master.size, 30 * master.size),
         name=name,
-    )(clip, packed, master, first, second)
-
-
-def adam_experts_kernel(scale, clip_ref, g0_ref, g1_ref, g2_ref, master_ref, first_ref, second_ref, *outs):
+        after=after,
+    )
+
+
+def adam_experts_kernel(scale, which, clip_ref, g0_ref, g1_ref, g2_ref, master_ref, first_ref, second_ref, *outs):
     for e, g_ref in enumerate((g0_ref, g1_ref, g2_ref)):
 
         @pl.when(pl.program_id(0) == e)
         def _():
             gradient = g_ref[...].astype(f32) * scale
-            results = adam_step(master_ref[0], first_ref[0], second_ref[0], gradient, clip_ref[0], 1.0)
+            results = adam_step(master_ref[0], first_ref[0], second_ref[0], gradient, clip_ref[0, which], 1.0)
             for out, result in zip(outs, results):
                 out[0] = result
 
 
-def adam_experts_call(clip, packed, at, master, first, second, scale, name):
+def adam_experts_call(clip, which, packed, at, master, first, second, scale, name, after=()):
     _, rows, cols = master.shape
     n = cols // BLK
     natural = pl.BlockSpec((1, rows, BLK), lambda e, j, _: (e, 0, j))
@@ -985,19 +1135,18 @@
             (rows, BLK), lambda e, j, _: (at // rows + jnp.where(e < own, 0, jnp.where(e > own, n - 1, j)), 0)
         )
 
-    return pl.pallas_call(
-        functools.partial(adam_experts_kernel, scale),
-        grid_spec=pltpu.PrefetchScalarGridSpec(
-            num_scalar_prefetch=1,
+    return kernel_call(
+        functools.partial(adam_experts_kernel, scale, which),
+        [clip, *packed, master, first, second],
+            prefetch=1,
             grid=(E, n),
             in_specs=[g_spec(e) for e in range(E)] + [natural] * 3,
             out_specs=[natural] * 4,
-        ),
         out_shape=[shape] * 4,
-        compiler_params=params(),
         cost_estimate=cost(20 * master.size, 30 * master.size),
         name=name,
-    )(clip, *packed, master, first, second)
+        after=after,
+    )
 
 
 def per_device(
@@ -1039,16 +1188,21 @@
     smalls = jnp.concatenate([norm_gains.astype(bf16), router.astype(bf16).T], axis=0)
     n_small = round_up(smalls.size, BLK) // BLK
     smalls = jnp.pad(smalls.reshape(-1), (0, 16 * BLK - smalls.size)).reshape(16, BLK)
-    in_shard = pack_call([(in_proj, None)], unit, smalls)
-    out_shard = pack_call([(out_proj, None)], unit)
-    early_shard = pack_call([(up_proj, 0), (down_proj, 0)], unit)
-    late_shard = pack_call([(w, e) for e in range(1, E) for w in (up_proj, down_proj)], unit)
     e_rows = n_up * rows + n_down * down_rows
-
-    w_in = gather_packed(in_shard, 0)
-    w_out = gather_packed(out_shard, 1)
-    w_early = gather_packed(early_shard, 0)
-    w_late = gather_packed(late_shard, 1)
+    in_shard, in_mine = pack_call([(in_proj, None)], unit, smalls)
+    mid_shard, _ = pack_call([(up_proj, 0), (down_proj, 0), (out_proj, None)], unit, after=[in_shard])
+    late_shard, late_mine, mid_mine = pack_call(
+        [(w, e) for e in range(1, E) for w in (up_proj, down_proj)], unit, before=mid_shard
+    )
+    g_in, g_mid, g_late = Gather(in_shard), Gather(mid_shard), Gather(late_shard)
+    g_in.start(in_mine, True)
+    g_in.own_c = swap_core(in_shard)
+    g_in.stack(after=[late_shard, g_in.own_c])
+    g_mid.start(hold(mid_mine, g_in.stacks), False)
+    g_in.double(after=[late_shard])
+    g_in.low_c = [swap_core(x) for x in hold(g_in.stacks, g_in.received)]
+    w_in = g_in.assemble()
+    g_late.start(hold(late_mine, g_mid.pieces), False)
 
     small_all = w_in[:, n_in * rows : n_in * rows + n_small, :].reshape(n_f, n_small * BLK)[:, : 5 * rows]
     small_all = small_all.reshape(n_f, 5, rows).transpose(1, 0, 2).reshape(5, width)
@@ -1071,85 +1225,134 @@
     cot = cotangent.reshape(total_tokens, width)
 
     qkv, n1 = qkv_call(x, gain_one, w_in, rows, n_in)
-    probs, mixed = attention_call(length, qkv, n_seq)
-    resid, n2, prob = resid_call(mixed, w_out, x, gain_two, router8, rows, n_out)
-    buf, dys, gates = dispatch_call(slot_rows, prob, n2, cot, n_seq)
-
-    ys, dbufs, dgates, sums = [], [], [], []
-    for e in range(E):
-        w, at = (w_early, 0) if e == 0 else (w_late, (e - 1) * e_rows)
-        y, dbuf, dgate, keep, send = expert_call(
-            e, at, core, buf, dys, gates, slot_rows, w, rows, down_rows, unit
-        )
-        ys.append(y)
-        dbufs.append(dbuf)
-        dgates.append(dgate.reshape(1, total_tokens))
-        sums.append(reduce_packed(keep, send, e))
-    dprob = pad_rows(jnp.concatenate(dgates, axis=0), 8)
-    block_out = combine_call(slot_cols, resid, ys, n_seq)
-
-    dresid, dattn, dmixed, small_two = middle_call(
-        slot_cols, dbufs, prob, dprob, router8, n2, resid, cot, gain_two, w_out, rows, n_out, n_seq
-    )
-
-    def reduce_one(keep, send, first):
-        n = keep.shape[1]
-        extra = round_up(n, unit) - n
-        if extra:
-            keep = jnp.pad(keep, ((0, 0), (0, extra), (0, 0)))
-            send = jnp.pad(send, ((0, 0), (0, extra), (0, 0)))
-        return reduce_packed(keep, send, first)
-
-    out_sum = reduce_one(*weight_grad_call(core, mixed, dattn, rows, n_z, "out_grad"), 1)
-    dq, dk, dv = attention_back_call(qkv, probs, mixed, dmixed, n_seq)
+    g_mid.stack(after=[qkv])
+    g_mid.double(after=[qkv])
+    g_mid.swap_early()
+    probs, mixed = attention_call(length, qkv, n_seq, after=g_mid.stacks)
+    g_mid.settle([mixed])
+    g_late.stack(after=[mixed, *g_mid.received])
+    w_mid = g_mid.assemble(after=g_late.stacks)
+    w_at = e_rows // (n_out * rows)
+    resid, n2, prob = resid_call(mixed, w_mid, w_at, x, gain_two, router8, rows, n_out)
+    g_late.double(after=[resid])
+    g_late.swap_early()
+    buf, dys, gates = dispatch_call(slot_rows, prob, n2, cot, n_seq, after=g_late.stacks)
+
+    def expert(e, w, at, after):
+        return expert_call(e, at, core, buf, dys, gates, slot_rows, w, rows, down_rows, unit, after)
+
+    y0, dbuf0, dgate0, keep0, send0 = expert(0, w_mid, 0, ())
+    g_late.settle([y0])
+    got0 = swap_core(hold(send0, g_late.received))
+    w_late = g_late.assemble(after=[y0])
+    total0 = pair_sum(keep0, hold(got0, [w_late]))
+    part0 = lax.psum_scatter(total0, "fsdp", axis_index_groups=core_groups())
+    y1, dbuf1, dgate1, keep1, send1 = expert(1, w_late, 0, [total0])
+    got1 = swap_core(send1)
+    y2, dbuf2, dgate2, keep2, send2 = expert(2, w_late, e_rows, [y1])
+    sum1 = Reduce(keep1, got1, 0)
+    sent = sum1.step([y2])
+    got2 = swap_core(hold(send2, sent))
+
+    dresid, dattn, dmixed, router_part = middle_call(
+        slot_cols,
+        (dbuf0, dbuf1, dbuf2),
+        (dgate0, dgate1, dgate2),
+        prob,
+        router8,
+        n2,
+        resid,
+        cot,
+        gain_two,
+        w_mid,
+        w_at,
+        rows,
+        n_out,
+        n_seq,
+        after=sent,
+    )
+    io_rows = round_up((n_in + n_out) * rows + 16, unit)
+    keep, send = weight_grad_call(core, mixed, dattn, rows, n_z, io_rows, n_in, "out_grad")
+    router_part = router_part[:E].astype(bf16).reshape(E, n_z, 2, rows).transpose(2, 1, 0, 3)
+    router_part = jnp.pad(router_part, ((0, 0), (0, 0), (0, 16 - E), (0, BLK - rows)))
+    at = (0, (n_in + n_out) * rows, 0)
+    keep = lax.dynamic_update_slice(keep, lax.dynamic_index_in_dim(router_part, core[0], keepdims=False), at)
+    send = lax.dynamic_update_slice(send, lax.dynamic_index_in_dim(router_part, 1 - core[0], keepdims=False), at)
+    sum2 = Reduce(keep2, got2, 1)
+    sent = sum1.step([send]) + sum2.step([send])
+    dq, dk, dv = attention_back_call(qkv, probs, mixed, dmixed, n_seq, sent + [part0])
+    sent = sum1.step([dq]) + sum2.step([dq])
     dqkv = jnp.concatenate([dq, dk, dv], axis=1)
-    in_sum = reduce_one(*weight_grad_call(core, n1, dqkv, rows, n_z, "in_grad"), 0)
-    input_grad, small_one = input_grad_call(dqkv, w_in, x, dresid, gain_one, rows, n_in)
+    keep, send = weight_grad_call(core, n1, dqkv, rows, n_z, io_rows, 0, "in_grad", (keep, send), sent)
+    sum2.newest = hold(sum2.newest, [send])
+    got = swap_core(hold(send, sum2.newest))
+    sum0 = lax.psum(part0, "replica")
+    input_grad = input_grad_call(dqkv, w_in, x, dresid, gain_one, rows, n_in, [send])
+    got = hold(got, [input_grad])
+    sum1.newest = hold(sum1.newest, [input_grad])
+    io_sum = Reduce(keep, got, 0)
+    sent = io_sum.step(sum1.newest) + sum2.step(sum1.newest)
+    block_out = combine_call(slot_cols, resid, (y0, y1, y2), n_seq, sent)
+    sum2.newest = hold(sum2.newest, [block_out])
+    sent = sum1.step(sum2.newest) + sum2.step()
+    sent = io_sum.step(sent)
+    sent = sum1.step(sent) + sum2.step(sent)
+    sent = io_sum.step(sent)
+    sums = [hold(sum0, sent), sum1.result(sent), sum2.result(sent)]
 
     grad_scale = 1.0 / (n_seq * n_rep * n_f)
-    small_sum = sum_all(jnp.concatenate([small_one[:1], small_two[8:9], small_two[:E]], axis=0)) * grad_scale
-    at = lax.axis_index("fsdp") * rows
-    small_mine = lax.dynamic_slice_in_dim(small_sum, at, rows, axis=1)
+    weights = (norm_gains, in_proj, out_proj, router, up_proj, down_proj)
+    counts = (2 * width,) + tuple(w.size * n_f for w in weights[1:])
+
     def square(packed):
         values = packed.astype(f32) * grad_scale
         return jnp.sum(values * values)
 
+    def along_rows(shard, packed, n):
+        both = shard[: n * rows].astype(f32) * packed[: n * rows].astype(f32)
+        return jnp.sum(both.reshape(n, rows, BLK), axis=(0, 2)) * grad_scale
+
+    def rms_of(squares, which):
+        lane = lax.broadcasted_iota(jnp.int32, (8, 128), 1)
+        values = sum(jnp.where(lane == i, value, 0.0) for i, value in enumerate(squares))
+        sizes = sum(jnp.where(lane == i, 1.0 / counts[w], 0.0) for i, w in enumerate(which))
+        rms = jnp.sqrt(sum_small(values) * sizes + epsilon)
+        return rms, jnp.minimum(1.0, clip_level / rms)
+
     at_down = n_up * rows
-    late = sum_small(jnp.stack([square(in_sum[: n_in * rows])]))
-    early = sum_small(
-        jnp.stack(
-            [
-                square(out_sum[: n_out * rows]),
-                sum(square(s[:at_down]) for s in sums),
-                sum(square(s[at_down:e_rows]) for s in sums),
-            ]
-        )
-    )
-    totals = (
-        jnp.sum(small_sum[:2] * small_sum[:2]),
-        late[0],
-        early[0],
-        jnp.sum(small_sum[2:] * small_sum[2:]),
-        early[1],
-        early[2],
-    )
-    weights = (norm_gains, in_proj, out_proj, router, up_proj, down_proj)
-    counts = (2 * width,) + tuple(w.size * n_f for w in weights[1:])
-    rms = [jnp.sqrt(t / float(n) + epsilon) for t, n in zip(totals, counts)]
-    clips = [jnp.minimum(1.0, clip_level / r)[None] for r in rms]
-    norm_res = adam_step(norm_gains, norm_first, norm_second, small_mine[:2], clips[0], 0.0)
-    in_res = adam_call(clips[1], in_sum, 0, in_proj, in_first, in_second, grad_scale, "in_adam")
-    out_res = adam_call(clips[2], out_sum, 0, out_proj, out_first, out_second, grad_scale, "out_adam")
-    router_res = adam_step(router, router_first, router_second, small_mine[2:].T, clips[3], 1.0)
-    up_res = adam_experts_call(clips[4], sums, 0, up_proj, up_first, up_second, grad_scale, "up_adam")
+    early_rms, early_clip = rms_of([sum(square(s[:at_down]) for s in sums), sum(square(s[at_down:e_rows]) for s in sums)], (4, 5))
+    sent = io_sum.step([early_clip])
     down_res = adam_experts_call(
-        clips[5], sums, at_down, down_proj, down_first, down_second, grad_scale, "down_adam"
-    )
+        hold(early_clip, sent), 1, sums, at_down, down_proj, down_first, down_second, grad_scale, "down_adam"
+    )
+    sent = io_sum.step([down_res[1]])
+    up_res = adam_experts_call(
+        hold(early_clip, sent), 0, sums, 0, up_proj, up_first, up_second, grad_scale, "up_adam"
+    )
+    gains_low = norm_gains.astype(bf16).astype(f32)
+    shards = (mid_shard, late_shard, late_shard[e_rows:])
+    gain_two_grad = sum(along_rows(shard, packed, n_up) for shard, packed in zip(shards, sums))
+
+    total = io_sum.result([up_res[1], gain_two_grad])
+    in_sum, out_sum = total[: n_in * rows], total[n_in * rows : (n_in + n_out) * rows]
+    at = (n_in + n_out) * rows
+    router_grad = total[at : at + E, :rows].astype(f32) * grad_scale
+    gain_one_grad = along_rows(in_shard, in_sum, n_in) / gains_low[0]
+    gain_two_grad = gain_two_grad + jnp.sum(router.astype(bf16).astype(f32).T * router_grad, axis=0)
+    gain_two_grad = gain_two_grad / gains_low[1]
+    gain_grad = jnp.stack([gain_one_grad, gain_two_grad])
+    late = [jnp.sum(gain_grad * gain_grad), square(in_sum), square(out_sum), jnp.sum(router_grad * router_grad)]
+    late_rms, late_clip = rms_of(late, (0, 1, 2, 3))
+    in_res = adam_call(late_clip, 1, total, 0, in_proj, in_first, in_second, grad_scale, "in_adam")
+    out_res = adam_call(late_clip, 2, total, n_in * rows, out_proj, out_first, out_second, grad_scale, "out_adam")
+    norm_res = adam_step(norm_gains, norm_first, norm_second, gain_grad, late_clip[0, 0], 0.0)
+    router_res = adam_step(router, router_first, router_second, router_grad.T, late_clip[0, 3], 1.0)
+    rms = jnp.concatenate([late_rms[0, :4], early_rms[0, :2]])
     return (
         block_out.reshape(tokens.shape),
         input_grad.reshape(tokens.shape),
-        jnp.stack(rms[:5]),
-        jnp.stack(rms[5:]),
+        rms[:5],
+        rms[5:],
         *norm_res,
         *in_res,
         *out_res,

time: 955 us -> 751 us (0.79)
  waiting for transfers between devices: 352 us -> 165 us
  starting transfers between devices: 103 us -> 69.3 us
  Pallas kernels: 379 us -> 389 us
    ppermute x30, waiting for transfers between devices: 234 us -> 77.9 us  [swap_replica(): return lax.ppermute(x, 'replica', [(i, i ^ bit) for i in range(size)])]
    ppermute x27 -> x12, waiting for transfers between devices: 98 us -> 23.9 us  [shift_core_pairs(): lax.ppermute(x, 'fsdp', [(i, (i + 2 * k) % size) for i in range(size)])]
    ppermute x27 -> x12, starting transfers between devices: 51.2 us -> 22.9 us  [shift_core_pairs(): lax.ppermute(x, 'fsdp', [(i, (i + 2 * k) % size) for i in range(size)])]
    ppermute x9 -> x6, waiting for transfers between devices: 19.6 us -> 42.7 us  [sum_small(): x = x + lax.ppermute(x, 'fsdp', [(i, i ^ bit) for i in range(size)])]
    ppermute x17 -> x19, waiting for transfers between devices: 0.04 us -> 12.5 us  [swap_core(): return lax.ppermute(x, 'fsdp', [(i, i ^ 1) for i in range(size)])]
    add x1 -> x9, other arithmetic: 0.83 us -> 12.5 us  [the longest x4 9.92 us: part_sum(): return functools.reduce(jnp.add, [t.astype(f32) for t in terms])]
    pallas_call x25 -> x26, Pallas kernels: 379 us -> 389 us  [kernel_call(): pl.pallas_call(kernel, grid_spec=pltpu.PrefetchScalarGridSpec(num_scalar_...]
    convert_element_type x21 -> x14, other arithmetic: 43.8 us -> 37.5 us  [the longest x10 28.3 us: halve(): away = self.part_sum([take(t, 1 - own) for t in self.terms[p]]).astype(bf16)]
  transfers between devices with their start and end apart: 83 -> 71, of which waited for: 34 -> 22; matrix products, arithmetic and copies ran while one was open for 10% -> 8% of each run, Pallas kernels for 36% -> 45%
where the time goes in v2:
time: 751 us; the launch traced here: 746 us
  Pallas kernels  389 us (52%)
  waiting for transfers between devices  165 us (22%)
  other arithmetic  75.9 us (10%)
  starting transfers between devices  69.3 us (9%)
  local copies, waits for them, and re-layouts  27.4 us (4%)
  between operations  19.3 us (3%)
    pallas_call x26, Pallas kernels, kernel_call(): pl.pallas_call(kernel, grid_spec=pltpu.PrefetchScalarGridSpec(num_scalar_...  389 us
    ppermute x30, waiting for transfers between devices, swap_replica(): return lax.ppermute(x, 'replica', [(i, i ^ bit) for i in range(size)])  77.9 us
    ppermute x6, waiting for transfers between devices, sum_small(): x = x + lax.ppermute(x, 'fsdp', [(i, i ^ bit) for i in range(size)])  42.7 us
    ppermute x30, starting transfers between devices, swap_replica(): return lax.ppermute(x, 'replica', [(i, i ^ bit) for i in range(size)])  33.5 us
    convert_element_type x10, other arithmetic, halve(): away = self.part_sum([take(t, 1 - own) for t in self.terms[p]]).astype(bf16)  28.3 us
    ppermute x12, waiting for transfers between devices, shift_core_pairs(): lax.ppermute(x, 'fsdp', [(i, (i + 2 * k) % size) for i in range(size)])  23.9 us
    ppermute x12, starting transfers between devices, shift_core_pairs(): lax.ppermute(x, 'fsdp', [(i, (i + 2 * k) % size) for i in range(size)])  22.9 us
    unnamed x128, local copies, waits for them, and re-layouts  16.4 us
  transfers between devices with their start and end apart: 71, of which 22 were waited for; matrix products, arithmetic and copies ran while one was open for 8% of the time, Pallas kernels for 45%

profile of v2, /device:TPU:0, one launch (start us, length us, event | category | flops | bytes accessed | tf_op | source)
XLA Modules:
  0.0 746.3 jit_solution(11021650542473447449)
XLA Ops:
  26.6 14.3 %collective-permute-done.2.refs_1_ = bf16[256,512]{1,0:T(8,128)(2,1)S(1)} collective-permute-done((bf16[256,512]{1,0:T(8,128)(2,1)}, bf16[256,512]{1,0:T(8,128)(2,1)S(1)}, u32[]{:S(2)}, u32[]{:S(2)}) %collective-permute-start.2) | collective-permute-done | bytes 262176 | tf_op jit(solution)/shard_map/ppermute | solution.py:93
  58.9 15.8 %collective-permute-done.7.refs_4_ = bf16[2,3,128,512]{3,2,1,0:T(8,128)(2,1)S(1)} collective-permute-done((bf16[2,3,128,512]{3,2,1,0:T(8,128)(2,1)S(1)}, bf16[2,3,128,512]{3,2,1,0:T(8,128)(2,1)S(1)}, u32[]{:S(2)}, u32[]{:S(2)}) %collective-permute-start.7) | collective-permute-done | bytes 786464 | tf_op jit(solution)/shard_map/ppermute | solution.py:108
  76.2 8.4 %all-gather.5.cloned.1.call-done = bf16[1728,512]{1,0:T(8,128)(2,1)} async-done(((bf16[432,512]{1,0:T(8,128)(2,1)}), bf16[1728,512]{1,0:T(8,128)(2,1)}) %all-gather.5.cloned.1.call-update) | async-done | bytes 1769488 | tf_op jit(solution)/shard_map/all_gather | solution.py:177
  85.5 7.5 %assemble.3.w_ref = bf16[8,1024,512]{2,1,0:T(8,128)(2,1)} custom-call(s32[3]{0:T(128)} %pad_add_fusion.idx_ref, bf16[1024,512]{1,0:T(8,128)(2,1)} %get-tuple-element.170.refs_0_, bf16[2,3,128,512]{3,2,1,0:T(8,128)(2,1)} %copy-done.13, bf16[2,3,128,512]{3,2,1,0:T(8,128)(2,1)} %copy-done.35, bf16[2,3,128,512]{3,2,1,0:T(8,128)(2,1)} %copy-done.14, ...), custom_call_target="tpu_custom_call" | custom-call | bytes 16 | tf_op jit(solution)/shard_map/assemble/pallas_call | solution.py:70
  94.7 18.1 %qkv.1 = (bf16[1024,2560]{1,0:T(8,128)(2,1)}, bf16[1024,1536]{1,0:T(8,128)(2,1)}) custom-call(bf16[1024,1536]{1,0:T(8,128)(2,1)} %bitcast.354, f32[1,1536]{1,0:T(1,128)} %reshape.762.gain_ref, bf16[8,1024,512]{2,1,0:T(8,128)(2,1)} %assemble.3.w_ref), custom_call_target="tpu_custom_call" | custom-call | flops 8 | bytes 14 | tf_op jit(solution)/shard_map/qkv/pallas_call | solution.py:70
  119.7 13.4 %collective-permute-done.13 = bf16[1,3,208,512]{3,2,1,0:T(8,128)(2,1)S(1)} collective-permute-done((bf16[1,3,208,512]{3,2,1,0:T(8,128)(2,1)}, bf16[1,3,208,512]{3,2,1,0:T(8,128)(2,1)S(1)}, u32[]{:S(2)}, u32[]{:S(2)}) %collective-permute-start.13) | collective-permute-done | bytes 639008 | tf_op jit(solution)/shard_map/ppermute | solution.py:108
  136.5 37.6 %attention.1 = (bf16[2,24,512,512]{3,2,1,0:T(8,128)(2,1)}, bf16[1024,1536]{1,0:T(8,128)(2,1)}) custom-call(s32[2]{0:T(128)} %bitcast.410, bf16[1024,2560]{1,0:T(8,128)(2,1)} %get-tuple-element.246.q_ref.k_ref.v_ref, bf16[1024,2560]{1,0:T(8,128)(2,1)} %get-tuple-element.246.q_ref.k_ref.v_ref, bf16[1024,2560]{1,0:T(8,128)(2,1)} %get-tuple-element.246.q_ref.k_ref.v_ref), custom_call_target="tpu_custom_call" | custom-call | flops 12 | bytes 25 | tf_op jit(solution)/shard_map/attention/pallas_call | solution.py:70
  181.5 11.5 %assemble.4.w_ref.up_a_ref.up_b_ref.down_ref = bf16[8,1728,512]{2,1,0:T(8,128)(2,1)} custom-call(s32[3]{0:T(128)} %pad_add_fusion.idx_ref, bf16[1728,512]{1,0:T(8,128)(2,1)} %get-tuple-element.172.refs_4_.refs_0_, bf16[2,3,224,512]{3,2,1,0:T(8,128)(2,1)} %copy-done.11, bf16[2,3,224,512]{3,2,1,0:T(8,128)(2,1)} %collective-permute-done.14.refs_2_, ...), custom_call_target="tpu_custom_call" | custom-call | bytes 28 | tf_op jit(solution)/shard_map/assemble/pallas_call | solution.py:70
  192.9 12.1 %resid.1 = (f32[1024,1536]{1,0:T(8,128)}, bf16[1024,1536]{1,0:T(8,128)(2,1)}, f32[8,1024]{1,0:T(8,128)}) custom-call(bf16[1024,1536]{1,0:T(8,128)(2,1)} %get-tuple-element.191.mix_ref.left_ref, bf16[8,1728,512]{2,1,0:T(8,128)(2,1)} %assemble.4.w_ref.up_a_ref.up_b_ref.down_ref, bf16[1024,1536]{1,0:T(8,128)(2,1)} %bitcast.355, f32[1,1536]{1,0:T(1,128)} %reshape.763.gain_ref, ...), custom_call_target="tpu_custom_call" | custom-call | flops 4 | bytes 23 | tf_op jit(solution)/shard_map/resid/pallas_call | solution.py:70
  214.9 12.1 %dispatch.1 = (bf16[3,2,320,1536]{3,2,1,0:T(8,128)(2,1)}, bf16[3,2,320,1536]{3,2,1,0:T(8,128)(2,1)}, f32[3,2,320,128]{3,2,1,0:T(8,128)}) custom-call(s32[2,8,512]{2,1,0:T(8,128)} %stack.98.slot_ref, f32[8,1024]{1,0:T(8,128)} %get-tuple-element.207.prob_ref, bf16[1024,1536]{1,0:T(8,128)(2,1)} %get-tuple-element.208.n2_ref, bf16[1024,1536]{1,0:T(8,128)(2,1)} %bitcast.379), custom_call_target="tpu_custom_call" | custom-call | flops 6 | bytes 31 | tf_op jit(solution)/shard_map/dispatch/pallas_call | solution.py:70
  227.0 32.9 %expert.3 = (bf16[2,320,1536]{2,1,0:T(8,128)(2,1)}, bf16[2,320,1536]{2,1,0:T(8,128)(2,1)}, f32[2,8,512]{2,1,0:T(8,128)}, bf16[4,1152,512]{2,1,0:T(8,128)(2,1)}, bf16[4,1152,512]{2,1,0:T(8,128)(2,1)}) custom-call(s32[1]{0:T(128)} %bitcast.8.idx_ref, bf16[3,2,320,1536]{3,2,1,0:T(8,128)(2,1)} %get-tuple-element.209.buf_ref, ...), custom_call_target="tpu_custom_call" | custom-call | flops 18 | bytes 62 | tf_op jit(solution)/shard_map/expert/pallas_call | solution.py:70
  260.8 8.3 %collective-permute-done.29.refs_7_ = bf16[2,3,288,512]{3,2,1,0:T(8,128)(2,1)S(1)} collective-permute-done((bf16[2,3,288,512]{3,2,1,0:T(8,128)(2,1)}, bf16[2,3,288,512]{3,2,1,0:T(8,128)(2,1)S(1)}, u32[]{:S(2)}, u32[]{:S(2)}) %collective-permute-start.29) | collective-permute-done | bytes 1769504 | tf_op jit(solution)/shard_map/ppermute | solution.py:103
  274.4 14.6 %assemble.5.up_a_ref.up_b_ref.down_ref = bf16[8,2304,512]{2,1,0:T(8,128)(2,1)} custom-call(s32[3]{0:T(128)} %pad_add_fusion.idx_ref, bf16[2304,512]{1,0:T(8,128)(2,1)} %get-tuple-element.173.refs_0_, bf16[2,3,288,512]{3,2,1,0:T(8,128)(2,1)} %constant_dynamic-update-slice_fusion.8.refs_1_, bf16[2,3,288,512]{3,2,1,0:T(8,128)(2,1)} %collective-permute-done.23.refs_2_, ...), custom_call_target="tpu_custom_call" | custom-call | bytes 37 | tf_op jit(solution)/shard_map/assemble/pallas_call | solution.py:70
  289.1 5.9 add_convert_fusion
  295.0 32.6 %expert.4 = (bf16[2,320,1536]{2,1,0:T(8,128)(2,1)}, bf16[2,320,1536]{2,1,0:T(8,128)(2,1)}, f32[2,8,512]{2,1,0:T(8,128)}, bf16[4,1152,512]{2,1,0:T(8,128)(2,1)}, bf16[4,1152,512]{2,1,0:T(8,128)(2,1)}) custom-call(s32[1]{0:T(128)} %bitcast.8.idx_ref, bf16[3,2,320,1536]{3,2,1,0:T(8,128)(2,1)} %get-tuple-element.209.buf_ref, ...), custom_call_target="tpu_custom_call" | custom-call | flops 18 | bytes 62 | tf_op jit(solution)/shard_map/expert/pallas_call | solution.py:70
  328.1 33.4 %expert.5 = (bf16[2,320,1536]{2,1,0:T(8,128)(2,1)}, bf16[2,320,1536]{2,1,0:T(8,128)(2,1)}, f32[2,8,512]{2,1,0:T(8,128)}, bf16[4,1152,512]{2,1,0:T(8,128)(2,1)}, bf16[4,1152,512]{2,1,0:T(8,128)(2,1)}) custom-call(s32[1]{0:T(128)} %bitcast.8.idx_ref, bf16[3,2,320,1536]{3,2,1,0:T(8,128)(2,1)} %get-tuple-element.209.buf_ref, ...), custom_call_target="tpu_custom_call" | custom-call | flops 18 | bytes 62 | tf_op jit(solution)/shard_map/expert/pallas_call | solution.py:70
  369.7 20.0 %middle.1 = (f32[1024,1536]{1,0:T(8,128)}, bf16[1024,1536]{1,0:T(8,128)(2,1)}, bf16[1024,1536]{1,0:T(8,128)(2,1)}, f32[8,1536]{1,0:T(8,128)}) custom-call(s32[1024,8]{1,0:T(8,128)} %bitcast.381, bf16[2,320,1536]{2,1,0:T(8,128)(2,1)} %get-tuple-element.231.d0_ref, bf16[2,320,1536]{2,1,0:T(8,128)(2,1)} %get-tuple-element.232.d1_ref, ...), custom_call_target="tpu_custom_call" | custom-call | flops 7 | bytes 31 | tf_op jit(solution)/shard_map/middle/pallas_call | solution.py:70
  389.6 9.8 %out_grad.1 = (bf16[4,1600,512]{2,1,0:T(8,128)(2,1)}, bf16[4,1600,512]{2,1,0:T(8,128)(2,1)}) custom-call(s32[1]{0:T(128)} %bitcast.8.idx_ref, bf16[1024,1536]{1,0:T(8,128)(2,1)} %get-tuple-element.191.mix_ref.left_ref, bf16[1024,1536]{1,0:T(8,128)(2,1)} %get-tuple-element.237.right_ref), custom_call_target="tpu_custom_call" | custom-call | flops 4 | bytes 11 | tf_op jit(solution)/shard_map/out_grad/pallas_call | solution.py:70
  415.4 42.4 %attention_back.1 = (bf16[1024,1536]{1,0:T(8,128)(2,1)}, bf16[1024,512]{1,0:T(8,128)(2,1)}, bf16[1024,512]{1,0:T(8,128)(2,1)}) custom-call(bf16[1024,2560]{1,0:T(8,128)(2,1)} %get-tuple-element.246.q_ref.k_ref.v_ref, bf16[1024,2560]{1,0:T(8,128)(2,1)} %get-tuple-element.246.q_ref.k_ref.v_ref, bf16[1024,2560]{1,0:T(8,128)(2,1)} %get-tuple-element.246.q_ref.k_ref.v_ref, ...), custom_call_target="tpu_custom_call" | custom-call | flops 25 | bytes 25 | tf_op jit(solution)/shard_map/attention_back/pallas_call | solution.py:70
  473.8 13.4 %in_grad.1 = (bf16[4,1600,512]{2,1,0:T(8,128)(2,1)}, bf16[4,1600,512]{2,1,0:T(8,128)(2,1)}) custom-call(s32[1]{0:T(128)} %bitcast.8.idx_ref, bf16[1024,1536]{1,0:T(8,128)(2,1)} %get-tuple-element.255.left_ref, bf16[1024,2560]{1,0:T(8,128)(2,1)} %copy-done, ...), custom_call_target="tpu_custom_call", output_to_operand_aliasing={{0}: (3, {}), {1}: (4, {})} | custom-call | flops 8 | bytes 14 | tf_op jit(solution)/shard_map/in_grad/pallas_call | solution.py:70
  491.7 15.3 %input_grad.1 = bf16[1024,1536]{1,0:T(8,128)(2,1)} custom-call(bf16[1024,2560]{1,0:T(8,128)(2,1)} %copy-done, bf16[8,1024,512]{2,1,0:T(8,128)(2,1)} %assemble.3.w_ref, bf16[1024,1536]{1,0:T(8,128)(2,1)} %bitcast.356, f32[1024,1536]{1,0:T(8,128)} %get-tuple-element.265.dresid_ref, f32[1,1536]{1,0:T(1,128)} %reshape.762.gain_ref), custom_call_target="tpu_custom_call" | custom-call | flops 8 | bytes 26 | tf_op jit(solution)/shard_map/input_grad/pallas_call | solution.py:70
  523.0 6.1 collective-permute-start.47
  533.0 11.0 %combine.1 = bf16[1024,1536]{1,0:T(8,128)(2,1)} custom-call(s32[1024,8]{1,0:T(8,128)} %bitcast.382, f32[1024,1536]{1,0:T(8,128)} %get-tuple-element.203.resid_ref, bf16[2,320,1536]{2,1,0:T(8,128)(2,1)} %get-tuple-element.214.y0_ref, bf16[2,320,1536]{2,1,0:T(8,128)(2,1)} %get-tuple-element.226.y1_ref, bf16[2,320,1536]{2,1,0:T(8,128)(2,1)} %get-tuple-element.228.y2_ref), custom_call_target="tpu_custom_call" | custom-call | flops 3 | bytes 18 | tf_op jit(solution)/shard_map/combine/pallas_call | solution.py:70
  553.9 8.7 %collective-permute-done.46 = bf16[4,2,192,512]{3,2,1,0:T(8,128)(2,1)} collective-permute-done((bf16[4,2,192,512]{3,2,1,0:T(8,128)(2,1)}, bf16[4,2,192,512]{3,2,1,0:T(8,128)(2,1)}, u32[]{:S(2)}, u32[]{:S(2)}) %collective-permute-start.46) | collective-permute-done | bytes 1572896 | tf_op jit(solution)/shard_map/ppermute | solution.py:108
  574.1 16.7 %collective-permute-done.51 = bf16[4,192,512]{2,1,0:T(8,128)(2,1)S(1)} collective-permute-done((bf16[4,192,512]{2,1,0:T(8,128)(2,1)S(1)}, bf16[4,192,512]{2,1,0:T(8,128)(2,1)S(1)}, u32[]{:S(2)}, u32[]{:S(2)}) %collective-permute-start.51) | collective-permute-done | bytes 786464 | tf_op jit(solution)/shard_map/ppermute | solution.py:108
  599.2 8.1 %collective-permute-done.58 = bf16[2,288,512]{2,1,0:T(8,128)(2,1)S(1)} collective-permute-done((bf16[2,288,512]{2,1,0:T(8,128)(2,1)S(1)}, bf16[2,288,512]{2,1,0:T(8,128)(2,1)S(1)}, u32[]{:S(2)}, u32[]{:S(2)}) %collective-permute-start.58) | collective-permute-done | bytes 589856 | tf_op jit(solution)/shard_map/ppermute | solution.py:108
  623.0 6.9 collective-permute-start.60
  635.7 32.9 %collective-permute-done.61 = f32[8,128]{1,0:T(8,128)S(1)} collective-permute-done((f32[8,128]{1,0:T(8,128)S(1)}, f32[8,128]{1,0:T(8,128)S(1)}, u32[]{:S(2)}, u32[]{:S(2)}) %collective-permute-start.61) | collective-permute-done | bytes 4128 | tf_op jit(solution)/shard_map/ppermute | solution.py:340
  671.0 12.3 %down_adam.1 = (f32[3,128,1536]{2,1,0:T(8,128)}, f32[3,128,1536]{2,1,0:T(8,128)}, f32[3,128,1536]{2,1,0:T(8,128)}, f32[3,128,1536]{2,1,0:T(8,128)}) custom-call(f32[8,128]{1,0:T(8,128)} %get-tuple-element.295.clip_ref, bf16[1152,512]{1,0:T(8,128)(2,1)} %all-reduce.5.cloned.1.call-done.g0_ref, bf16[1152,512]{1,0:T(8,128)(2,1)} %bitcast.377, ...), custom_call_target="tpu_custom_call" | custom-call | bytes 17 | tf_op jit(solution)/shard_map/down_adam/pallas_call | solution.py:70
  684.5 18.0 %up_adam.1 = (f32[3,192,2048]{2,1,0:T(8,128)}, f32[3,192,2048]{2,1,0:T(8,128)}, f32[3,192,2048]{2,1,0:T(8,128)}, f32[3,192,2048]{2,1,0:T(8,128)}) custom-call(f32[8,128]{1,0:T(8,128)} %get-tuple-element.295.clip_ref, bf16[1152,512]{1,0:T(8,128)(2,1)} %all-reduce.5.cloned.1.call-done.g0_ref, bf16[1152,512]{1,0:T(8,128)(2,1)} %bitcast.378, ...), custom_call_target="tpu_custom_call" | custom-call | bytes 35 | tf_op jit(solution)/shard_map/up_adam/pallas_call | solution.py:70
  720.0 6.5 out_adam.1
  726.6 9.5 %in_adam.1 = (f32[192,2560]{1,0:T(8,128)}, f32[192,2560]{1,0:T(8,128)}, f32[192,2560]{1,0:T(8,128)}, f32[192,2560]{1,0:T(8,128)}) custom-call(f32[8,128]{1,0:T(8,128)} %copy-done.45, bf16[1600,512]{1,0:T(8,128)(2,1)} %bitcast.369, f32[192,2560]{1,0:T(8,128)} %master_ref.6, f32[192,2560]{1,0:T(8,128)} %first_ref.6, f32[192,2560]{1,0:T(8,128)} %second_ref.6), custom_call_target="tpu_custom_call" | custom-call | bytes 14 | tf_op jit(solution)/shard_map/in_adam/pallas_call | solution.py:70
  (384 shorter events, 210.8 us)
Async XLA Ops:
  7.2 77.4 %all-gather.5.cloned.1.call-start = ((), (), s32[]{:S(2)}) async-start(), calls=%async_computation.3 | async-start | bytes 2211840 | tf_op jit(solution)/shard_map/all_gather | solution.py:177
  44.3 131.5 %all-gather.7.cloned.1.call-start = ((), (), s32[]{:S(2)}) async-start(), calls=%async_computation.4 | async-start | bytes 2949120 | tf_op jit(solution)/shard_map/all_gather | solution.py:177
  84.6 330.8 %reduce-scatter.2.cloned.1.call-start = ((), (), s32[]{:S(2)}) async-start(), calls=%async_computation.1 | async-start | bytes 5898240 | tf_op jit(solution)/shard_map/reduce_scatter | solution.py:1249
  118.5 55.6 %collective-permute-start.16 = (bf16[1728,512]{1,0:T(8,128)(2,1)S(1)}, bf16[1728,512]{1,0:T(8,128)(2,1)S(1)}, u32[]{:S(2)}, u32[]{:S(2)}) collective-permute-start(bf16[1728,512]{1,0:T(8,128)(2,1)S(1)} %copy-done.5), channel_id=1, source_target_pairs={{0,1},{1,0},{2,3},{3,2},{4,5},{5,4},{6,7},{7,6},{8,9},{9,8},{10,11... | collective-permute-start | bytes 5308424 | tf_op jit(solution)/shard_map/ppermute | solution.py:103
  133.2 40.9 %collective-permute-start.17 = (bf16[2,3,224,512]{3,2,1,0:T(8,128)(2,1)S(1)}, bf16[2,3,224,512]{3,2,1,0:T(8,128)(2,1)}, u32[]{:S(2)}, u32[]{:S(2)}) collective-permute-start(bf16[2,3,224,512]{3,2,1,0:T(8,128)(2,1)S(1)} %constant_dynamic-update-slice_fusion.4.refs_1_), channel_id=1, source_target_pairs={{0,1},{1,0},{2,3},{3,2},{4,5},{5,4},{6,7},{7,6},{8,9},{9,8},{10,11... | collective-permute-start | bytes 4128776 | tf_op jit(solution)/shard_map/ppermute | solution.py:103
  133.3 40.8 %collective-permute-start.14 = (bf16[2,3,224,512]{3,2,1,0:T(8,128)(2,1)S(1)}, bf16[2,3,224,512]{3,2,1,0:T(8,128)(2,1)}, u32[]{:S(2)}, u32[]{:S(2)}) collective-permute-start(bf16[2,3,224,512]{3,2,1,0:T(8,128)(2,1)S(1)} %constant_dynamic-update-slice_fusion.4.refs_1_), channel_id=1, source_target_pairs={{0,16},{8,24},{16,0},{24,8},{1,17},{9,25},{17,1},{25,9},{2,18},{10... | collective-permute-start | bytes 4128776 | tf_op jit(solution)/shard_map/ppermute | solution.py:108
  134.9 39.2 %collective-permute-start.18 = (bf16[2,3,208,512]{3,2,1,0:T(8,128)(2,1)S(1)}, bf16[2,3,208,512]{3,2,1,0:T(8,128)(2,1)}, u32[]{:S(2)}, u32[]{:S(2)}) collective-permute-start(bf16[2,3,208,512]{3,2,1,0:T(8,128)(2,1)S(1)} %constant_dynamic-update-slice_fusion.6.refs_3_), channel_id=1, source_target_pairs={{0,1},{1,0},{2,3},{3,2},{4,5},{5,4},{6,7},{7,6},{8,9},{9,8},{10,11... | collective-permute-start | bytes 3833864 | tf_op jit(solution)/shard_map/ppermute | solution.py:103
  135.1 39.0 %collective-permute-start.15 = (bf16[2,3,208,512]{3,2,1,0:T(8,128)(2,1)S(1)}, bf16[2,3,208,512]{3,2,1,0:T(8,128)(2,1)}, u32[]{:S(2)}, u32[]{:S(2)}) collective-permute-start(bf16[2,3,208,512]{3,2,1,0:T(8,128)(2,1)S(1)} %constant_dynamic-update-slice_fusion.6.refs_3_), channel_id=1, source_target_pairs={{0,8},{8,0},{16,24},{24,16},{1,9},{9,1},{17,25},{25,17},{2,10},{10... | collective-permute-start | bytes 3833864 | tf_op jit(solution)/shard_map/ppermute | solution.py:108
  178.8 28.7 %collective-permute-start.19 = (bf16[1,3,288,512]{3,2,1,0:T(8,128)(2,1)}, bf16[1,3,288,512]{3,2,1,0:T(8,128)(2,1)S(1)}, u32[]{:S(2)}, u32[]{:S(2)}) collective-permute-start(bf16[1,3,288,512]{3,2,1,0:T(8,128)(2,1)} %get-tuple-element.197), channel_id=1, source_target_pairs={{0,8},{8,0},{16,24},{24,16},{1,9},{9,1},{17,25},{25,17},{2,10},{10... | collective-permute-start | bytes 2654216 | tf_op jit(solution)/shard_map/ppermute | solution.py:108
  180.1 79.9 %collective-permute-start.25 = (bf16[2304,512]{1,0:T(8,128)(2,1)S(1)}, bf16[2304,512]{1,0:T(8,128)(2,1)}, u32[]{:S(2)}, u32[]{:S(2)}) collective-permute-start(bf16[2304,512]{1,0:T(8,128)(2,1)S(1)} %copy-done.6), channel_id=1, source_target_pairs={{0,1},{1,0},{2,3},{3,2},{4,5},{5,4},{6,7},{7,6},{8,9},{9,8},{10,11... | collective-permute-start | bytes 7077896 | tf_op jit(solution)/shard_map/ppermute | solution.py:103
  209.7 50.3 %collective-permute-start.27 = (bf16[2,3,288,512]{3,2,1,0:T(8,128)(2,1)}, bf16[2,3,288,512]{3,2,1,0:T(8,128)(2,1)}, u32[]{:S(2)}, u32[]{:S(2)}) collective-permute-start(bf16[2,3,288,512]{3,2,1,0:T(8,128)(2,1)} %constant_dynamic-update-slice_fusion.10.refs_3_), channel_id=1, source_target_pairs={{0,1},{1,0},{2,3},{3,2},{4,5},{5,4},{6,7},{7,6},{8,9},{9,8},{10,11... | collective-permute-start | bytes 5308424 | tf_op jit(solution)/shard_map/ppermute | solution.py:103
  210.2 49.7 %collective-permute-start.24 = (bf16[2,3,288,512]{3,2,1,0:T(8,128)(2,1)}, bf16[2,3,288,512]{3,2,1,0:T(8,128)(2,1)}, u32[]{:S(2)}, u32[]{:S(2)}) collective-permute-start(bf16[2,3,288,512]{3,2,1,0:T(8,128)(2,1)} %constant_dynamic-update-slice_fusion.10.refs_3_), channel_id=1, source_target_pairs={{0,8},{8,0},{16,24},{24,16},{1,9},{9,1},{17,25},{25,17},{2,10},{10... | collective-permute-start | bytes 5308424 | tf_op jit(solution)/shard_map/ppermute | solution.py:108
  212.5 47.4 %collective-permute-start.26 = (bf16[2,3,288,512]{3,2,1,0:T(8,128)(2,1)}, bf16[2,3,288,512]{3,2,1,0:T(8,128)(2,1)}, u32[]{:S(2)}, u32[]{:S(2)}) collective-permute-start(bf16[2,3,288,512]{3,2,1,0:T(8,128)(2,1)} %constant_dynamic-update-slice_fusion.8.refs_1_), channel_id=1, source_target_pairs={{0,1},{1,0},{2,3},{3,2},{4,5},{5,4},{6,7},{7,6},{8,9},{9,8},{10,11... | collective-permute-start | bytes 5308424 | tf_op jit(solution)/shard_map/ppermute | solution.py:103
  212.5 47.4 %collective-permute-start.23 = (bf16[2,3,288,512]{3,2,1,0:T(8,128)(2,1)}, bf16[2,3,288,512]{3,2,1,0:T(8,128)(2,1)}, u32[]{:S(2)}, u32[]{:S(2)}) collective-permute-start(bf16[2,3,288,512]{3,2,1,0:T(8,128)(2,1)} %constant_dynamic-update-slice_fusion.8.refs_1_), channel_id=1, source_target_pairs={{0,16},{8,24},{16,0},{24,8},{1,17},{9,25},{17,1},{25,9},{2,18},{10... | collective-permute-start | bytes 5308424 | tf_op jit(solution)/shard_map/ppermute | solution.py:108
  260.0 29.1 %collective-permute-start.28 = (bf16[4,1152,512]{2,1,0:T(8,128)(2,1)}, bf16[4,1152,512]{2,1,0:T(8,128)(2,1)}, u32[]{:S(2)}, u32[]{:S(2)}) collective-permute-start(bf16[4,1152,512]{2,1,0:T(8,128)(2,1)} %get-tuple-element.217), channel_id=1, source_target_pairs={{0,1},{1,0},{2,3},{3,2},{4,5},{5,4},{6,7},{7,6},{8,9},{9,8},{10,11... | collective-permute-start | bytes 14155784 | tf_op jit(solution)/shard_map/ppermute | solution.py:103
  327.6 33.9 %collective-permute-start.31 = (bf16[4,1152,512]{2,1,0:T(8,128)(2,1)}, bf16[4,1152,512]{2,1,0:T(8,128)(2,1)}, u32[]{:S(2)}, u32[]{:S(2)}) collective-permute-start(bf16[4,1152,512]{2,1,0:T(8,128)(2,1)} %get-tuple-element.225), channel_id=1, source_target_pairs={{0,1},{1,0},{2,3},{3,2},{4,5},{5,4},{6,7},{7,6},{8,9},{9,8},{10,11... | collective-permute-start | bytes 14155784 | tf_op jit(solution)/shard_map/ppermute | solution.py:103
  328.0 285.4 %all-reduce.5.cloned.1.call-start = ((), (), s32[]{:S(2)}) async-start(), calls=%async_computation.2 | async-start | bytes 2359296 | tf_op jit(solution)/shard_map/psum | solution.py:1289
  367.6 33.5 %collective-permute-start.36 = (bf16[4,1152,512]{2,1,0:T(8,128)(2,1)}, bf16[4,1152,512]{2,1,0:T(8,128)(2,1)}, u32[]{:S(2)}, u32[]{:S(2)}) collective-permute-start(bf16[4,1152,512]{2,1,0:T(8,128)(2,1)} %get-tuple-element.244), channel_id=1, source_target_pairs={{0,1},{1,0},{2,3},{3,2},{4,5},{5,4},{6,7},{7,6},{8,9},{9,8},{10,11... | collective-permute-start | bytes 14155784 | tf_op jit(solution)/shard_map/ppermute | solution.py:103
  367.7 33.4 %collective-permute-start.32 = (bf16[4,2,144,512]{3,2,1,0:T(8,128)(2,1)}, bf16[4,2,144,512]{3,2,1,0:T(8,128)(2,1)S(1)}, u32[]{:S(2)}, u32[]{:S(2)}) collective-permute-start(bf16[4,2,144,512]{3,2,1,0:T(8,128)(2,1)} %fusion.16), channel_id=1, source_target_pairs={{0,8},{8,0},{16,24},{24,16},{1,9},{9,1},{17,25},{25,17},{2,10},{10... | collective-permute-start | bytes 3538952 | tf_op jit(solution)/shard_map/ppermute | solution.py:108
  368.2 32.8 %collective-permute-start.33 = (bf16[4,2,144,512]{3,2,1,0:T(8,128)(2,1)}, bf16[4,2,144,512]{3,2,1,0:T(8,128)(2,1)S(1)}, u32[]{:S(2)}, u32[]{:S(2)}) collective-permute-start(bf16[4,2,144,512]{3,2,1,0:T(8,128)(2,1)} %fusion.17), channel_id=1, source_target_pairs={{0,16},{8,24},{16,0},{24,8},{1,17},{9,25},{17,1},{25,9},{2,18},{10... | collective-permute-start | bytes 3538952 | tf_op jit(solution)/shard_map/ppermute | solution.py:108
  405.1 58.2 %collective-permute-start.37 = (bf16[4,2,144,512]{3,2,1,0:T(8,128)(2,1)}, bf16[4,2,144,512]{3,2,1,0:T(8,128)(2,1)S(1)}, u32[]{:S(2)}, u32[]{:S(2)}) collective-permute-start(bf16[4,2,144,512]{3,2,1,0:T(8,128)(2,1)} %fusion.18), channel_id=1, source_target_pairs={{0,8},{8,0},{16,24},{24,16},{1,9},{9,1},{17,25},{25,17},{2,10},{10... | collective-permute-start | bytes 3538952 | tf_op jit(solution)/shard_map/ppermute | solution.py:108
  409.6 53.7 %collective-permute-start.38 = (bf16[4,2,144,512]{3,2,1,0:T(8,128)(2,1)}, bf16[4,2,144,512]{3,2,1,0:T(8,128)(2,1)S(1)}, u32[]{:S(2)}, u32[]{:S(2)}) collective-permute-start(bf16[4,2,144,512]{3,2,1,0:T(8,128)(2,1)} %fusion.19), channel_id=1, source_target_pairs={{0,16},{8,24},{16,0},{24,8},{1,17},{9,25},{17,1},{25,9},{2,18},{10... | collective-permute-start | bytes 3538952 | tf_op jit(solution)/shard_map/ppermute | solution.py:108
  414.3 43.4 %collective-permute-start.35 = (bf16[4,144,512]{2,1,0:T(8,128)(2,1)}, bf16[4,144,512]{2,1,0:T(8,128)(2,1)S(1)}, u32[]{:S(2)}, u32[]{:S(2)}) collective-permute-start(bf16[4,144,512]{2,1,0:T(8,128)(2,1)} %get-tuple-element.460), channel_id=1, source_target_pairs={{0,8},{8,0},{16,24},{24,16},{1,9},{9,1},{17,25},{25,17},{2,10},{10... | collective-permute-start | bytes 1769480 | tf_op jit(solution)/shard_map/ppermute | solution.py:108
  415.0 42.8 %collective-permute-start.34 = (bf16[4,144,512]{2,1,0:T(8,128)(2,1)}, bf16[4,144,512]{2,1,0:T(8,128)(2,1)S(1)}, u32[]{:S(2)}, u32[]{:S(2)}) collective-permute-start(bf16[4,144,512]{2,1,0:T(8,128)(2,1)} %get-tuple-element.461), channel_id=1, source_target_pairs={{0,16},{8,24},{16,0},{24,8},{1,17},{9,25},{17,1},{25,9},{2,18},{10... | collective-permute-start | bytes 1769480 | tf_op jit(solution)/shard_map/ppermute | solution.py:108
  514.6 48.0 %collective-permute-start.45 = (bf16[4,2,208,512]{3,2,1,0:T(8,128)(2,1)}, bf16[4,2,208,512]{3,2,1,0:T(8,128)(2,1)}, u32[]{:S(2)}, u32[]{:S(2)}) collective-permute-start(bf16[4,2,208,512]{3,2,1,0:T(8,128)(2,1)} %fusion.3), channel_id=1, source_target_pairs={{0,8},{8,0},{16,24},{24,16},{1,9},{9,1},{17,25},{25,17},{2,10},{10... | collective-permute-start | bytes 5111816 | tf_op jit(solution)/shard_map/ppermute | solution.py:108
  518.2 44.5 %collective-permute-start.46 = (bf16[4,2,192,512]{3,2,1,0:T(8,128)(2,1)}, bf16[4,2,192,512]{3,2,1,0:T(8,128)(2,1)}, u32[]{:S(2)}, u32[]{:S(2)}) collective-permute-start(bf16[4,2,192,512]{3,2,1,0:T(8,128)(2,1)} %fusion.14), channel_id=1, source_target_pairs={{0,16},{8,24},{16,0},{24,8},{1,17},{9,25},{17,1},{25,9},{2,18},{10... | collective-permute-start | bytes 4718600 | tf_op jit(solution)/shard_map/ppermute | solution.py:108
  571.7 35.6 %collective-permute-start.58 = (bf16[2,288,512]{2,1,0:T(8,128)(2,1)S(1)}, bf16[2,288,512]{2,1,0:T(8,128)(2,1)S(1)}, u32[]{:S(2)}, u32[]{:S(2)}) collective-permute-start(bf16[2,288,512]{2,1,0:T(8,128)(2,1)S(1)} %reverse_select_fusion.4), channel_id=1, source_target_pairs={{0,8},{8,0},{16,24},{24,16},{1,9},{9,1},{17,25},{25,17},{2,10},{10... | collective-permute-start | bytes 1769480 | tf_op jit(solution)/shard_map/ppermute | solution.py:108
  573.4 35.8 %collective-permute-start.57 = (bf16[2,288,512]{2,1,0:T(8,128)(2,1)S(1)}, bf16[2,288,512]{2,1,0:T(8,128)(2,1)S(1)}, u32[]{:S(2)}, u32[]{:S(2)}) collective-permute-start(bf16[2,288,512]{2,1,0:T(8,128)(2,1)S(1)} %reverse_select_fusion.5), channel_id=1, source_target_pairs={{0,16},{8,24},{16,0},{24,8},{1,17},{9,25},{17,1},{25,9},{2,18},{10... | collective-permute-start | bytes 1769480 | tf_op jit(solution)/shard_map/ppermute | solution.py:108
  629.9 39.4 %collective-permute-start.54 = (bf16[400,512]{1,0:T(8,128)(2,1)S(1)}, bf16[400,512]{1,0:T(8,128)(2,1)S(1)}, u32[]{:S(2)}, u32[]{:S(2)}) collective-permute-start(bf16[400,512]{1,0:T(8,128)(2,1)S(1)} %copy-done.40), channel_id=1, source_target_pairs={{0,2},{1,3},{2,4},{3,5},{4,6},{5,7},{6,0},{7,1},{8,10},{9,11},{10,... | collective-permute-start | bytes 1228808 | tf_op jit(solution)/shard_map/ppermute | solution.py:93
  629.9 39.3 %collective-permute-start.55 = (bf16[400,512]{1,0:T(8,128)(2,1)S(1)}, bf16[400,512]{1,0:T(8,128)(2,1)S(1)}, u32[]{:S(2)}, u32[]{:S(2)}) collective-permute-start(bf16[400,512]{1,0:T(8,128)(2,1)S(1)} %copy-done.39), channel_id=1, source_target_pairs={{0,4},{1,5},{2,6},{3,7},{4,0},{5,1},{6,2},{7,3},{8,12},{9,13},{10,... | collective-permute-start | bytes 1228808 | tf_op jit(solution)/shard_map/ppermute | solution.py:93
  631.5 37.7 %collective-permute-start.56 = (bf16[400,512]{1,0:T(8,128)(2,1)S(1)}, bf16[400,512]{1,0:T(8,128)(2,1)S(1)}, u32[]{:S(2)}, u32[]{:S(2)}) collective-permute-start(bf16[400,512]{1,0:T(8,128)(2,1)S(1)} %copy-done.38), channel_id=1, source_target_pairs={{0,6},{1,7},{2,0},{3,1},{4,2},{5,3},{6,4},{7,5},{8,14},{9,15},{10,... | collective-permute-start | bytes 1228808 | tf_op jit(solution)/shard_map/ppermute | solution.py:93
  634.4 34.2 %collective-permute-start.61 = (f32[8,128]{1,0:T(8,128)S(1)}, f32[8,128]{1,0:T(8,128)S(1)}, u32[]{:S(2)}, u32[]{:S(2)}) collective-permute-start(f32[8,128]{1,0:T(8,128)S(1)} %fusion.77), channel_id=1, source_target_pairs={{0,4},{1,5},{2,6},{3,7},{4,0},{5,1},{6,2},{7,3},{8,12},{9,13},{10,... | collective-permute-start | bytes 12296 | tf_op jit(solution)/shard_map/ppermute | solution.py:340
  (98 other events, 1287.4 us)
Sparse Core Ops, SparseCore 0:
  44.5 40.0 all-gather.4
  86.7 49.3 all-gather.6
  328.1 82.8 reduce-scatter.1
  533.1 73.3 all-reduce.4

commit v3 on v2

--- a/solution.py
+++ b/solution.py
@@ -215,7 +215,7 @@
         idx = jnp.stack([lax.axis_index("replica"), place // 2, place % 2]).astype(jnp.int32)
         ins = [self.shard]
         other = [self.own_c]
-        high_c = [swap_core(x) for x in self.received]
+        high_c = self.high_c = [swap_core(x) for x in self.received]
         for pair in zip(self.stacks, self.received):
             ins += pair
         for pair in zip(self.low_c, high_c):
@@ -256,6 +256,7 @@
         self.live = [list(reversed(self.bits)) for _ in self.cuts]
         self.terms = [[keep.reshape(shape)] for _ in self.cuts]
         self.newest = [received.reshape(shape)]
+        self.have = None
         halves = [functools.partial(self.halve, i) for i in range(n_bits)]
         gathers = [functools.partial(self.gather, i, bit) for i, bit in enumerate(self.order)]
         self.todo = [halves[:1], halves[1:], [self.along], gathers[:1], gathers[1:]]
@@ -305,12 +306,17 @@
         self.newest = [shift_core_pairs(away, k) for k, away in enumerate(aways, 1)]
         return aways
 
+    def sum_here(self, after=()):
+        if self.have is None:
+            summed = self.at_place(self.z)
+            for got in hold(self.newest, after):
+                summed = summed + got.astype(f32)
+            self.have = summed.astype(bf16)
+        return self.have
+
     def gather(self, i, bit):
         if i == 0:
-            summed = self.at_place(self.z)
-            for got in self.newest:
-                summed = summed + got.astype(f32)
-            self.have = summed.astype(bf16)
+            self.sum_here()
         else:
             self.have = self.joined()
         self.newest, self.bit = [swap_replica(self.have, bit)], bit
@@ -333,12 +339,12 @@
     return (keep.astype(f32) + got.astype(f32)).astype(bf16)
 
 
-def sum_small(x):
+def sum_small(x, bit=1, after=()):
     size = lax.axis_size("fsdp")
-    bit = 1
     while bit < size:
-        x = x + lax.ppermute(x, "fsdp", [(i, i ^ bit) for i in range(size)])
+        x = x + hold(lax.ppermute(x, "fsdp", [(i, i ^ bit) for i in range(size)]), after)
         bit *= 2
+        after = ()
     return x
 
 
@@ -1201,7 +1207,8 @@
     g_mid.start(hold(mid_mine, g_in.stacks), False)
     g_in.double(after=[late_shard])
     g_in.low_c = [swap_core(x) for x in hold(g_in.stacks, g_in.received)]
-    w_in = g_in.assemble()
+    g_mid.stack(after=g_in.received)
+    w_in = g_in.assemble(after=g_mid.stacks)
     g_late.start(hold(late_mine, g_mid.pieces), False)
 
     small_all = w_in[:, n_in * rows : n_in * rows + n_small, :].reshape(n_f, n_small * BLK)[:, : 5 * rows]
@@ -1225,7 +1232,6 @@
     cot = cotangent.reshape(total_tokens, width)
 
     qkv, n1 = qkv_call(x, gain_one, w_in, rows, n_in)
-    g_mid.stack(after=[qkv])
     g_mid.double(after=[qkv])
     g_mid.swap_early()
     probs, mixed = attention_call(length, qkv, n_seq, after=g_mid.stacks)
@@ -1243,8 +1249,8 @@
 
     y0, dbuf0, dgate0, keep0, send0 = expert(0, w_mid, 0, ())
     g_late.settle([y0])
-    got0 = swap_core(hold(send0, g_late.received))
     w_late = g_late.assemble(after=[y0])
+    got0 = swap_core(hold(send0, g_late.high_c))
     total0 = pair_sum(keep0, hold(got0, [w_late]))
     part0 = lax.psum_scatter(total0, "fsdp", axis_index_groups=core_groups())
     y1, dbuf1, dgate1, keep1, send1 = expert(1, w_late, 0, [total0])
@@ -1287,17 +1293,21 @@
     sum2.newest = hold(sum2.newest, [send])
     got = swap_core(hold(send, sum2.newest))
     sum0 = lax.psum(part0, "replica")
-    input_grad = input_grad_call(dqkv, w_in, x, dresid, gain_one, rows, n_in, [send])
-    got = hold(got, [input_grad])
-    sum1.newest = hold(sum1.newest, [input_grad])
-    io_sum = Reduce(keep, got, 0)
-    sent = io_sum.step(sum1.newest) + sum2.step(sum1.newest)
-    block_out = combine_call(slot_cols, resid, (y0, y1, y2), n_seq, sent)
-    sum2.newest = hold(sum2.newest, [block_out])
-    sent = sum1.step(sum2.newest) + sum2.step()
-    sent = io_sum.step(sent)
-    sent = sum1.step(sent) + sum2.step(sent)
-    sent = io_sum.step(sent)
+    block_out = combine_call(slot_cols, resid, (y0, y1, y2), n_seq, [send])
+    io_sum = Reduce(keep, hold(got, [block_out]), 0)
+    sent = io_sum.step()
+    input_grad = input_grad_call(dqkv, w_in, x, dresid, gain_one, rows, n_in, sent)
+    io_sum.newest = hold(io_sum.newest, [input_grad])
+    sent = io_sum.step()
+    sum1.newest = hold(sum1.newest, sent)
+    sent = sum2.step(sum1.newest)
+    io_sum.newest = hold(io_sum.newest, sent)
+    sent = sum1.step(io_sum.newest)
+    sum2.newest = hold(sum2.newest, sent)
+    sent = io_sum.step(sum2.newest)
+    sent = sum2.step(sent)
+    sent = sum1.step(sent)
+    sent = sum2.step(sent)
     sums = [hold(sum0, sent), sum1.result(sent), sum2.result(sent)]
 
     grad_scale = 1.0 / (n_seq * n_rep * n_f)
@@ -1312,42 +1322,64 @@
         both = shard[: n * rows].astype(f32) * packed[: n * rows].astype(f32)
         return jnp.sum(both.reshape(n, rows, BLK), axis=(0, 2)) * grad_scale
 
-    def rms_of(squares, which):
+    def lanes(values):
         lane = lax.broadcasted_iota(jnp.int32, (8, 128), 1)
-        values = sum(jnp.where(lane == i, value, 0.0) for i, value in enumerate(squares))
-        sizes = sum(jnp.where(lane == i, 1.0 / counts[w], 0.0) for i, w in enumerate(which))
-        rms = jnp.sqrt(sum_small(values) * sizes + epsilon)
+        return sum(jnp.where(lane == i, value, 0.0) for i, value in enumerate(values))
+
+    def rms_and_clip(squares, which):
+        rms = jnp.sqrt(squares * lanes([1.0 / counts[w] for w in which]) + epsilon)
         return rms, jnp.minimum(1.0, clip_level / rms)
 
     at_down = n_up * rows
-    early_rms, early_clip = rms_of([sum(square(s[:at_down]) for s in sums), sum(square(s[at_down:e_rows]) for s in sums)], (4, 5))
-    sent = io_sum.step([early_clip])
-    down_res = adam_experts_call(
-        hold(early_clip, sent), 1, sums, at_down, down_proj, down_first, down_second, grad_scale, "down_adam"
-    )
-    sent = io_sum.step([down_res[1]])
-    up_res = adam_experts_call(
-        hold(early_clip, sent), 0, sums, 0, up_proj, up_first, up_second, grad_scale, "up_adam"
-    )
+    up_square = sum(square(s[:at_down]) for s in sums) / n_rep
+    down_square = sum(square(s[at_down:e_rows]) for s in sums) / n_rep
     gains_low = norm_gains.astype(bf16).astype(f32)
     shards = (mid_shard, late_shard, late_shard[e_rows:])
     gain_two_grad = sum(along_rows(shard, packed, n_up) for shard, packed in zip(shards, sums))
 
-    total = io_sum.result([up_res[1], gain_two_grad])
-    in_sum, out_sum = total[: n_in * rows], total[n_in * rows : (n_in + n_out) * rows]
-    at = (n_in + n_out) * rows
-    router_grad = total[at : at + E, :rows].astype(f32) * grad_scale
+    here = io_sum.sum_here([up_square, down_square, gain_two_grad])
+    row = lax.axis_index("replica") * here.shape[0] + lax.broadcasted_iota(jnp.int32, (here.shape[0], 1), 0)
+    lane = lax.broadcasted_iota(jnp.int32, (1, BLK), 1)
+    ends = (n_in * rows, (n_in + n_out) * rows)
+    values = here.astype(f32) * grad_scale
+    values = values * values
+    spread_squares = [
+        jnp.sum(jnp.where(row < ends[0], values, 0.0)),
+        jnp.sum(jnp.where((row >= ends[0]) & (row < ends[1]), values, 0.0)),
+        jnp.sum(jnp.where((row >= ends[1]) & (row < ends[1] + E) & (lane < rows), values, 0.0)),
+    ]
+    squares = lanes(spread_squares + [up_square, down_square])
+    for bit in bit_order(0):
+        squares = squares + swap_replica(squares, bit)
+    io_sum.have = hold(io_sum.have, [squares])
+    sent = io_sum.step()
+    all_rms, all_clip = rms_and_clip(sum_small(hold(squares, sent)), (1, 2, 3, 4, 5))
+    sent = io_sum.step([all_clip])
+    down_res = adam_experts_call(
+        hold(all_clip, sent), 4, sums, at_down, down_proj, down_first, down_second, grad_scale, "down_adam"
+    )
+    up_res = adam_experts_call(
+        hold(all_clip, [down_res[1]]), 3, sums, 0, up_proj, up_first, up_second, grad_scale, "up_adam"
+    )
+    total = io_sum.result([up_res[1]])
+    in_sum = total[: ends[0]]
+    router_grad = total[ends[1] : ends[1] + E, :rows].astype(f32) * grad_scale
     gain_one_grad = along_rows(in_shard, in_sum, n_in) / gains_low[0]
     gain_two_grad = gain_two_grad + jnp.sum(router.astype(bf16).astype(f32).T * router_grad, axis=0)
     gain_two_grad = gain_two_grad / gains_low[1]
     gain_grad = jnp.stack([gain_one_grad, gain_two_grad])
-    late = [jnp.sum(gain_grad * gain_grad), square(in_sum), square(out_sum), jnp.sum(router_grad * router_grad)]
-    late_rms, late_clip = rms_of(late, (0, 1, 2, 3))
-    in_res = adam_call(late_clip, 1, total, 0, in_proj, in_first, in_second, grad_scale, "in_adam")
-    out_res = adam_call(late_clip, 2, total, n_in * rows, out_proj, out_first, out_second, grad_scale, "out_adam")
-    norm_res = adam_step(norm_gains, norm_first, norm_second, gain_grad, late_clip[0, 0], 0.0)
-    router_res = adam_step(router, router_first, router_second, router_grad.T, late_clip[0, 3], 1.0)
-    rms = jnp.concatenate([late_rms[0, :4], early_rms[0, :2]])
+    squares = lanes([jnp.sum(gain_grad * gain_grad)])
+    out_res = adam_call(
+        hold(all_clip, [squares]), 1, total, ends[0], out_proj, out_first, out_second, grad_scale, "out_adam"
+    )
+    squares = squares + hold(swap_core(squares), [out_res[1]])
+    in_res = adam_call(
+        hold(all_clip, [squares]), 0, total, 0, in_proj, in_first, in_second, grad_scale, "in_adam"
+    )
+    gain_rms, gain_clip = rms_and_clip(sum_small(squares, 2, [in_res[1]]), (0,))
+    norm_res = adam_step(norm_gains, norm_first, norm_second, gain_grad, gain_clip[0, 0], 0.0)
+    router_res = adam_step(router, router_first, router_second, router_grad.T, all_clip[0, 2], 1.0)
+    rms = jnp.concatenate([gain_rms[0, :1], all_rms[0, :5]])
     return (
         block_out.reshape(tokens.shape),
         input_grad.reshape(tokens.shape),

time: 751 us -> 716 us (0.953)
  waiting for transfers between devices: 165 us -> 120 us
  local copies, waits for them, and re-layouts: 27.4 us -> 35.2 us
    ppermute x6 -> x5, waiting for transfers between devices: 42.7 us -> 7.58 us  [sum_small(): lax.ppermute(x, 'fsdp', [(i, i ^ bit) for i in range(size)])]
    psum x1, waiting for transfers between devices: 0.01 us -> 16.8 us  [per_device(): sum0 = lax.psum(part0, 'replica')]
    ppermute x30 -> x32, waiting for transfers between devices: 77.9 us -> 62.5 us  [swap_replica(): return lax.ppermute(x, 'replica', [(i, i ^ bit) for i in range(size)])]
    unnamed x128 -> x116, local copies, waits for them, and re-layouts: 16.4 us -> 20.4 us
    ppermute x30 -> x32, starting transfers between devices: 33.5 us -> 34.5 us  [swap_replica(): return lax.ppermute(x, 'replica', [(i, i ^ bit) for i in range(size)])]
  transfers between devices with their start and end apart: 71 -> 73, of which waited for: 22 -> 20; matrix products, arithmetic and copies ran while one was open for 8% -> 11% of each run, Pallas kernels for 45% -> 49%
where the time goes in v3:
time: 716 us; the launch traced here: 711 us
  Pallas kernels  388 us (54%)
  waiting for transfers between devices  120 us (17%)
  other arithmetic  80 us (11%)
  starting transfers between devices  68.2 us (10%)
  local copies, waits for them, and re-layouts  35.2 us (5%)
  between operations  19.2 us (3%)
    pallas_call x26, Pallas kernels, kernel_call(): pl.pallas_call(kernel, grid_spec=pltpu.PrefetchScalarGridSpec(num_scalar_...  388 us
    ppermute x32, waiting for transfers between devices, swap_replica(): return lax.ppermute(x, 'replica', [(i, i ^ bit) for i in range(size)])  62.5 us
    ppermute x32, starting transfers between devices, swap_replica(): return lax.ppermute(x, 'replica', [(i, i ^ bit) for i in range(size)])  34.5 us
    convert_element_type x10, other arithmetic, halve(): away = self.part_sum([take(t, 1 - own) for t in self.terms[p]]).astype(bf16)  29.2 us
    ppermute x12, starting transfers between devices, shift_core_pairs(): lax.ppermute(x, 'fsdp', [(i, (i + 2 * k) % size) for i in range(size)])  23.6 us
    unnamed x116, local copies, waits for them, and re-layouts  20.4 us
    ppermute x12, waiting for transfers between devices, shift_core_pairs(): lax.ppermute(x, 'fsdp', [(i, (i + 2 * k) % size) for i in range(size)])  18.2 us
    psum x1, waiting for transfers between devices, per_device(): sum0 = lax.psum(part0, 'replica')  16.8 us
  transfers between devices with their start and end apart: 73, of which 20 were waited for; matrix products, arithmetic and copies ran while one was open for 11% of the time, Pallas kernels for 49%

profile of v3, /device:TPU:0, one launch (start us, length us, event | category | flops | bytes accessed | tf_op | source)
XLA Modules:
  0.0 710.7 jit_solution(17433302090343499511)
XLA Ops:
  13.1 4.6 collective-permute-start.3
  22.2 4.4 pack.5
  26.6 14.3 %collective-permute-done.2.refs_1_ = bf16[256,512]{1,0:T(8,128)(2,1)S(1)} collective-permute-done((bf16[256,512]{1,0:T(8,128)(2,1)}, bf16[256,512]{1,0:T(8,128)(2,1)S(1)}, u32[]{:S(2)}, u32[]{:S(2)}) %collective-permute-start.2) | collective-permute-done | bytes 262176 | tf_op jit(solution)/shard_map/ppermute | solution.py:93
  49.5 5.9 collective-permute-done.4
  58.9 15.9 %collective-permute-done.7.refs_4_ = bf16[2,3,128,512]{3,2,1,0:T(8,128)(2,1)} collective-permute-done((bf16[2,3,128,512]{3,2,1,0:T(8,128)(2,1)S(1)}, bf16[2,3,128,512]{3,2,1,0:T(8,128)(2,1)}, u32[]{:S(2)}, u32[]{:S(2)}) %collective-permute-start.7) | collective-permute-done | bytes 786464 | tf_op jit(solution)/shard_map/ppermute | solution.py:108
  75.8 8.7 %all-gather.5.cloned.1.call-done = bf16[1728,512]{1,0:T(8,128)(2,1)} async-done(((bf16[432,512]{1,0:T(8,128)(2,1)}), bf16[1728,512]{1,0:T(8,128)(2,1)}) %all-gather.5.cloned.1.call-update) | async-done | bytes 1769488 | tf_op jit(solution)/shard_map/all_gather | solution.py:177
  91.1 7.7 %assemble.3.w_ref = bf16[8,1024,512]{2,1,0:T(8,128)(2,1)} custom-call(s32[3]{0:T(128)} %pad_add_fusion.idx_ref, bf16[1024,512]{1,0:T(8,128)(2,1)} %get-tuple-element.181.refs_0_, bf16[2,3,128,512]{3,2,1,0:T(8,128)(2,1)} %copy-done.13, bf16[2,3,128,512]{3,2,1,0:T(8,128)(2,1)} %collective-permute-done.6.refs_2_, bf16[2,3,128,512]{3,2,1,0:T(8,128)(2,1)} %copy-done.14, ...), custom_call_target="tpu_custom_call" | custom-call | bytes 16 | tf_op jit(solution)/shard_map/assemble/pallas_call | solution.py:70
  100.5 18.2 %qkv.1 = (bf16[1024,2560]{1,0:T(8,128)(2,1)}, bf16[1024,1536]{1,0:T(8,128)(2,1)}) custom-call(bf16[1024,1536]{1,0:T(8,128)(2,1)} %bitcast.357, f32[1,1536]{1,0:T(1,128)} %reshape.788.gain_ref, bf16[8,1024,512]{2,1,0:T(8,128)(2,1)} %assemble.3.w_ref), custom_call_target="tpu_custom_call" | custom-call | flops 8 | bytes 14 | tf_op jit(solution)/shard_map/qkv/pallas_call | solution.py:70
  124.2 37.6 %attention.1 = (bf16[2,24,512,512]{3,2,1,0:T(8,128)(2,1)}, bf16[1024,1536]{1,0:T(8,128)(2,1)}) custom-call(s32[2]{0:T(128)} %bitcast.412, bf16[1024,2560]{1,0:T(8,128)(2,1)} %get-tuple-element.258.q_ref.k_ref.v_ref, bf16[1024,2560]{1,0:T(8,128)(2,1)} %get-tuple-element.258.q_ref.k_ref.v_ref, bf16[1024,2560]{1,0:T(8,128)(2,1)} %get-tuple-element.258.q_ref.k_ref.v_ref), custom_call_target="tpu_custom_call" | custom-call | flops 12 | bytes 25 | tf_op jit(solution)/shard_map/attention/pallas_call | solution.py:70
  170.7 11.5 %assemble.4.w_ref.up_a_ref.up_b_ref.down_ref = bf16[8,1728,512]{2,1,0:T(8,128)(2,1)} custom-call(s32[3]{0:T(128)} %pad_add_fusion.idx_ref, bf16[1728,512]{1,0:T(8,128)(2,1)} %get-tuple-element.183.refs_4_.refs_0_, bf16[2,3,224,512]{3,2,1,0:T(8,128)(2,1)} %copy-done.11, bf16[2,3,224,512]{3,2,1,0:T(8,128)(2,1)} %collective-permute-done.14.refs_2_, ...), custom_call_target="tpu_custom_call" | custom-call | bytes 28 | tf_op jit(solution)/shard_map/assemble/pallas_call | solution.py:70
  182.2 12.1 %resid.1 = (f32[1024,1536]{1,0:T(8,128)}, bf16[1024,1536]{1,0:T(8,128)(2,1)}, f32[8,1024]{1,0:T(8,128)}) custom-call(bf16[1024,1536]{1,0:T(8,128)(2,1)} %get-tuple-element.203.mix_ref.left_ref, bf16[8,1728,512]{2,1,0:T(8,128)(2,1)} %assemble.4.w_ref.up_a_ref.up_b_ref.down_ref, bf16[1024,1536]{1,0:T(8,128)(2,1)} %bitcast.358, f32[1,1536]{1,0:T(1,128)} %reshape.789.gain_ref, ...), custom_call_target="tpu_custom_call" | custom-call | flops 4 | bytes 23 | tf_op jit(solution)/shard_map/resid/pallas_call | solution.py:70
  202.6 12.1 %dispatch.1 = (bf16[3,2,320,1536]{3,2,1,0:T(8,128)(2,1)}, bf16[3,2,320,1536]{3,2,1,0:T(8,128)(2,1)}, f32[3,2,320,128]{3,2,1,0:T(8,128)}) custom-call(s32[2,8,512]{2,1,0:T(8,128)} %stack.96.slot_ref, f32[8,1024]{1,0:T(8,128)} %get-tuple-element.219.prob_ref, bf16[1024,1536]{1,0:T(8,128)(2,1)} %get-tuple-element.220.n2_ref, bf16[1024,1536]{1,0:T(8,128)(2,1)} %bitcast.381), custom_call_target="tpu_custom_call" | custom-call | flops 6 | bytes 31 | tf_op jit(solution)/shard_map/dispatch/pallas_call | solution.py:70
  214.7 32.9 %expert.3 = (bf16[2,320,1536]{2,1,0:T(8,128)(2,1)}, bf16[2,320,1536]{2,1,0:T(8,128)(2,1)}, f32[2,8,512]{2,1,0:T(8,128)}, bf16[4,1152,512]{2,1,0:T(8,128)(2,1)}, bf16[4,1152,512]{2,1,0:T(8,128)(2,1)}) custom-call(s32[1]{0:T(128)} %bitcast.8.idx_ref, bf16[3,2,320,1536]{3,2,1,0:T(8,128)(2,1)} %get-tuple-element.221.buf_ref, ...), custom_call_target="tpu_custom_call" | custom-call | flops 18 | bytes 62 | tf_op jit(solution)/shard_map/expert/pallas_call | solution.py:70
  255.4 14.6 %assemble.5.up_a_ref.up_b_ref.down_ref = bf16[8,2304,512]{2,1,0:T(8,128)(2,1)} custom-call(s32[3]{0:T(128)} %pad_add_fusion.idx_ref, bf16[2304,512]{1,0:T(8,128)(2,1)} %get-tuple-element.184.refs_0_, bf16[2,3,288,512]{3,2,1,0:T(8,128)(2,1)} %constant_dynamic-update-slice_fusion.8.refs_1_, bf16[2,3,288,512]{3,2,1,0:T(8,128)(2,1)} %collective-permute-done.23.refs_2_, ...), custom_call_target="tpu_custom_call" | custom-call | bytes 37 | tf_op jit(solution)/shard_map/assemble/pallas_call | solution.py:70
  270.0 5.9 add_convert_fusion
  275.9 32.6 %expert.4 = (bf16[2,320,1536]{2,1,0:T(8,128)(2,1)}, bf16[2,320,1536]{2,1,0:T(8,128)(2,1)}, f32[2,8,512]{2,1,0:T(8,128)}, bf16[4,1152,512]{2,1,0:T(8,128)(2,1)}, bf16[4,1152,512]{2,1,0:T(8,128)(2,1)}) custom-call(s32[1]{0:T(128)} %bitcast.8.idx_ref, bf16[3,2,320,1536]{3,2,1,0:T(8,128)(2,1)} %get-tuple-element.221.buf_ref, ...), custom_call_target="tpu_custom_call" | custom-call | flops 18 | bytes 62 | tf_op jit(solution)/shard_map/expert/pallas_call | solution.py:70
  309.0 33.1 %expert.5 = (bf16[2,320,1536]{2,1,0:T(8,128)(2,1)}, bf16[2,320,1536]{2,1,0:T(8,128)(2,1)}, f32[2,8,512]{2,1,0:T(8,128)}, bf16[4,1152,512]{2,1,0:T(8,128)(2,1)}, bf16[4,1152,512]{2,1,0:T(8,128)(2,1)}) custom-call(s32[1]{0:T(128)} %bitcast.8.idx_ref, bf16[3,2,320,1536]{3,2,1,0:T(8,128)(2,1)} %get-tuple-element.221.buf_ref, ...), custom_call_target="tpu_custom_call" | custom-call | flops 18 | bytes 62 | tf_op jit(solution)/shard_map/expert/pallas_call | solution.py:70
  352.3 19.9 %middle.1 = (f32[1024,1536]{1,0:T(8,128)}, bf16[1024,1536]{1,0:T(8,128)(2,1)}, bf16[1024,1536]{1,0:T(8,128)(2,1)}, f32[8,1536]{1,0:T(8,128)}) custom-call(s32[1024,8]{1,0:T(8,128)} %bitcast.383, bf16[2,320,1536]{2,1,0:T(8,128)(2,1)} %get-tuple-element.243.d0_ref, bf16[2,320,1536]{2,1,0:T(8,128)(2,1)} %get-tuple-element.244.d1_ref, ...), custom_call_target="tpu_custom_call" | custom-call | flops 7 | bytes 31 | tf_op jit(solution)/shard_map/middle/pallas_call | solution.py:70
  372.2 9.8 %out_grad.1 = (bf16[4,1600,512]{2,1,0:T(8,128)(2,1)}, bf16[4,1600,512]{2,1,0:T(8,128)(2,1)}) custom-call(s32[1]{0:T(128)} %bitcast.8.idx_ref, bf16[1024,1536]{1,0:T(8,128)(2,1)} %get-tuple-element.203.mix_ref.left_ref, bf16[1024,1536]{1,0:T(8,128)(2,1)} %get-tuple-element.249.right_ref), custom_call_target="tpu_custom_call" | custom-call | flops 4 | bytes 11 | tf_op jit(solution)/shard_map/out_grad/pallas_call | solution.py:70
  397.7 42.3 %attention_back.1 = (bf16[1024,1536]{1,0:T(8,128)(2,1)}, bf16[1024,512]{1,0:T(8,128)(2,1)}, bf16[1024,512]{1,0:T(8,128)(2,1)}) custom-call(bf16[1024,2560]{1,0:T(8,128)(2,1)} %get-tuple-element.258.q_ref.k_ref.v_ref, bf16[1024,2560]{1,0:T(8,128)(2,1)} %get-tuple-element.258.q_ref.k_ref.v_ref, bf16[1024,2560]{1,0:T(8,128)(2,1)} %get-tuple-element.258.q_ref.k_ref.v_ref, ...), custom_call_target="tpu_custom_call" | custom-call | flops 25 | bytes 25 | tf_op jit(solution)/shard_map/attention_back/pallas_call | solution.py:70
  454.1 13.4 %in_grad.1 = (bf16[4,1600,512]{2,1,0:T(8,128)(2,1)}, bf16[4,1600,512]{2,1,0:T(8,128)(2,1)}) custom-call(s32[1]{0:T(128)} %bitcast.8.idx_ref, bf16[1024,1536]{1,0:T(8,128)(2,1)} %get-tuple-element.267.left_ref, bf16[1024,2560]{1,0:T(8,128)(2,1)} %copy-done, ...), custom_call_target="tpu_custom_call", output_to_operand_aliasing={{0}: (3, {}), {1}: (4, {})} | custom-call | flops 8 | bytes 14 | tf_op jit(solution)/shard_map/in_grad/pallas_call | solution.py:70
  469.2 10.6 %combine.1 = bf16[1024,1536]{1,0:T(8,128)(2,1)} custom-call(s32[1024,8]{1,0:T(8,128)} %bitcast.384, f32[1024,1536]{1,0:T(8,128)} %get-tuple-element.215.resid_ref, bf16[2,320,1536]{2,1,0:T(8,128)(2,1)} %get-tuple-element.226.y0_ref, bf16[2,320,1536]{2,1,0:T(8,128)(2,1)} %get-tuple-element.238.y1_ref, bf16[2,320,1536]{2,1,0:T(8,128)(2,1)} %get-tuple-element.240.y2_ref), custom_call_target="tpu_custom_call" | custom-call | flops 3 | bytes 18 | tf_op jit(solution)/shard_map/combine/pallas_call | solution.py:70
  493.3 15.2 %input_grad.1 = bf16[1024,1536]{1,0:T(8,128)(2,1)} custom-call(bf16[1024,2560]{1,0:T(8,128)(2,1)} %copy-done, bf16[8,1024,512]{2,1,0:T(8,128)(2,1)} %assemble.3.w_ref, bf16[1024,1536]{1,0:T(8,128)(2,1)} %bitcast.359, f32[1024,1536]{1,0:T(8,128)} %get-tuple-element.279.dresid_ref, f32[1,1536]{1,0:T(1,128)} %reshape.788.gain_ref), custom_call_target="tpu_custom_call" | custom-call | flops 8 | bytes 26 | tf_op jit(solution)/shard_map/input_grad/pallas_call | solution.py:70
  508.5 15.6 %collective-permute-done.43 = bf16[4,2,192,512]{3,2,1,0:T(8,128)(2,1)} collective-permute-done((bf16[4,2,192,512]{3,2,1,0:T(8,128)(2,1)}, bf16[4,2,192,512]{3,2,1,0:T(8,128)(2,1)}, u32[]{:S(2)}, u32[]{:S(2)}) %collective-permute-start.43) | collective-permute-done | bytes 1572896 | tf_op jit(solution)/shard_map/ppermute | solution.py:108
  541.8 8.8 %collective-permute-done.45 = bf16[4,192,512]{2,1,0:T(8,128)(2,1)} collective-permute-done((bf16[4,192,512]{2,1,0:T(8,128)(2,1)}, bf16[4,192,512]{2,1,0:T(8,128)(2,1)}, u32[]{:S(2)}, u32[]{:S(2)}) %collective-permute-start.45) | collective-permute-done | bytes 786464 | tf_op jit(solution)/shard_map/ppermute | solution.py:108
  568.8 8.5 %collective-permute-done.55 = bf16[288,512]{1,0:T(8,128)(2,1)S(1)} collective-permute-done((bf16[288,512]{1,0:T(8,128)(2,1)S(1)}, bf16[288,512]{1,0:T(8,128)(2,1)S(1)}, u32[]{:S(2)}, u32[]{:S(2)}) %collective-permute-start.55) | collective-permute-done | bytes 294944 | tf_op jit(solution)/shard_map/ppermute | solution.py:108
  579.5 6.8 collective-permute-start.52
  590.0 16.8 %all-reduce.5.cloned.1.call-done.g0_ref = bf16[1152,512]{1,0:T(8,128)(2,1)} async-done(((bf16[1152,512]{1,0:T(8,128)(2,1)}), bf16[1152,512]{1,0:T(8,128)(2,1)}) %all-reduce.5.cloned.1.call-update) | async-done | bytes 1179664 | tf_op jit(solution)/shard_map/psum | solution.py:1295
  643.2 12.0 %down_adam.1 = (f32[3,128,1536]{2,1,0:T(8,128)}, f32[3,128,1536]{2,1,0:T(8,128)}, f32[3,128,1536]{2,1,0:T(8,128)}, f32[3,128,1536]{2,1,0:T(8,128)}) custom-call(f32[8,128]{1,0:T(8,128)} %get-tuple-element.319.clip_ref, bf16[1152,512]{1,0:T(8,128)(2,1)} %all-reduce.5.cloned.1.call-done.g0_ref, bf16[1152,512]{1,0:T(8,128)(2,1)} %bitcast.379, ...), custom_call_target="tpu_custom_call" | custom-call | bytes 17 | tf_op jit(solution)/shard_map/down_adam/pallas_call | solution.py:70
  655.2 18.0 %up_adam.1 = (f32[3,192,2048]{2,1,0:T(8,128)}, f32[3,192,2048]{2,1,0:T(8,128)}, f32[3,192,2048]{2,1,0:T(8,128)}, f32[3,192,2048]{2,1,0:T(8,128)}) custom-call(f32[8,128]{1,0:T(8,128)} %get-tuple-element.319.clip_ref, bf16[1152,512]{1,0:T(8,128)(2,1)} %all-reduce.5.cloned.1.call-done.g0_ref, bf16[1152,512]{1,0:T(8,128)(2,1)} %bitcast.380, ...), custom_call_target="tpu_custom_call" | custom-call | bytes 35 | tf_op jit(solution)/shard_map/up_adam/pallas_call | solution.py:70
  676.6 6.5 out_adam.1
  685.8 9.5 %in_adam.1 = (f32[192,2560]{1,0:T(8,128)}, f32[192,2560]{1,0:T(8,128)}, f32[192,2560]{1,0:T(8,128)}, f32[192,2560]{1,0:T(8,128)}) custom-call(f32[8,128]{1,0:T(8,128)} %get-tuple-element.319.clip_ref, bf16[1600,512]{1,0:T(8,128)(2,1)} %bitcast.371, f32[192,2560]{1,0:T(8,128)} %master_ref.7, f32[192,2560]{1,0:T(8,128)} %first_ref.7, f32[192,2560]{1,0:T(8,128)} %second_ref.7), custom_call_target="tpu_custom_call" | custom-call | bytes 14 | tf_op jit(solution)/shard_map/in_adam/pallas_call | solution.py:70
  (380 shorter events, 205.5 us)
Async XLA Ops:
  7.2 77.3 %all-gather.5.cloned.1.call-start = ((), (), s32[]{:S(2)}) async-start(), calls=%async_computation.3 | async-start | bytes 2211840 | tf_op jit(solution)/shard_map/all_gather | solution.py:177
  44.3 119.1 %all-gather.7.cloned.1.call-start = ((), (), s32[]{:S(2)}) async-start(), calls=%async_computation.4 | async-start | bytes 2949120 | tf_op jit(solution)/shard_map/all_gather | solution.py:177
  84.6 313.1 %reduce-scatter.2.cloned.1.call-start = ((), (), s32[]{:S(2)}) async-start(), calls=%async_computation.1 | async-start | bytes 5898240 | tf_op jit(solution)/shard_map/reduce_scatter | solution.py:1255
  87.5 32.4 %collective-permute-start.9 = (bf16[1,3,208,512]{3,2,1,0:T(8,128)(2,1)}, bf16[1,3,208,512]{3,2,1,0:T(8,128)(2,1)}, u32[]{:S(2)}, u32[]{:S(2)}) collective-permute-start(bf16[1,3,208,512]{3,2,1,0:T(8,128)(2,1)} %get-tuple-element.195), channel_id=1, source_target_pairs={{0,16},{8,24},{16,0},{24,8},{1,17},{9,25},{17,1},{25,9},{2,18},{10... | collective-permute-start | bytes 1916936 | tf_op jit(solution)/shard_map/ppermute | solution.py:108
  91.0 70.8 %collective-permute-start.16 = (bf16[1728,512]{1,0:T(8,128)(2,1)S(1)}, bf16[1728,512]{1,0:T(8,128)(2,1)}, u32[]{:S(2)}, u32[]{:S(2)}) collective-permute-start(bf16[1728,512]{1,0:T(8,128)(2,1)S(1)} %copy-done.5), channel_id=1, source_target_pairs={{0,1},{1,0},{2,3},{3,2},{4,5},{5,4},{6,7},{7,6},{8,9},{9,8},{10,11... | collective-permute-start | bytes 5308424 | tf_op jit(solution)/shard_map/ppermute | solution.py:103
  121.0 40.8 %collective-permute-start.17 = (bf16[2,3,224,512]{3,2,1,0:T(8,128)(2,1)S(1)}, bf16[2,3,224,512]{3,2,1,0:T(8,128)(2,1)S(1)}, u32[]{:S(2)}, u32[]{:S(2)}) collective-permute-start(bf16[2,3,224,512]{3,2,1,0:T(8,128)(2,1)S(1)} %constant_dynamic-update-slice_fusion.4.refs_1_), channel_id=1, source_target_pairs={{0,1},{1,0},{2,3},{3,2},{4,5},{5,4},{6,7},{7,6},{8,9},{9,8},{10,11... | collective-permute-start | bytes 4128776 | tf_op jit(solution)/shard_map/ppermute | solution.py:103
  121.7 40.1 %collective-permute-start.14 = (bf16[2,3,224,512]{3,2,1,0:T(8,128)(2,1)S(1)}, bf16[2,3,224,512]{3,2,1,0:T(8,128)(2,1)}, u32[]{:S(2)}, u32[]{:S(2)}) collective-permute-start(bf16[2,3,224,512]{3,2,1,0:T(8,128)(2,1)S(1)} %constant_dynamic-update-slice_fusion.4.refs_1_), channel_id=1, source_target_pairs={{0,16},{8,24},{16,0},{24,8},{1,17},{9,25},{17,1},{25,9},{2,18},{10... | collective-permute-start | bytes 4128776 | tf_op jit(solution)/shard_map/ppermute | solution.py:108
  123.4 38.4 %collective-permute-start.18 = (bf16[2,3,208,512]{3,2,1,0:T(8,128)(2,1)S(1)}, bf16[2,3,208,512]{3,2,1,0:T(8,128)(2,1)}, u32[]{:S(2)}, u32[]{:S(2)}) collective-permute-start(bf16[2,3,208,512]{3,2,1,0:T(8,128)(2,1)S(1)} %constant_dynamic-update-slice_fusion.6.refs_3_), channel_id=1, source_target_pairs={{0,1},{1,0},{2,3},{3,2},{4,5},{5,4},{6,7},{7,6},{8,9},{9,8},{10,11... | collective-permute-start | bytes 3833864 | tf_op jit(solution)/shard_map/ppermute | solution.py:103
  123.5 38.3 %collective-permute-start.15 = (bf16[2,3,208,512]{3,2,1,0:T(8,128)(2,1)S(1)}, bf16[2,3,208,512]{3,2,1,0:T(8,128)(2,1)}, u32[]{:S(2)}, u32[]{:S(2)}) collective-permute-start(bf16[2,3,208,512]{3,2,1,0:T(8,128)(2,1)S(1)} %constant_dynamic-update-slice_fusion.6.refs_3_), channel_id=1, source_target_pairs={{0,8},{8,0},{16,24},{24,16},{1,9},{9,1},{17,25},{25,17},{2,10},{10... | collective-permute-start | bytes 3833864 | tf_op jit(solution)/shard_map/ppermute | solution.py:108
  169.3 78.3 %collective-permute-start.25 = (bf16[2304,512]{1,0:T(8,128)(2,1)S(1)}, bf16[2304,512]{1,0:T(8,128)(2,1)}, u32[]{:S(2)}, u32[]{:S(2)}) collective-permute-start(bf16[2304,512]{1,0:T(8,128)(2,1)S(1)} %copy-done.6), channel_id=1, source_target_pairs={{0,1},{1,0},{2,3},{3,2},{4,5},{5,4},{6,7},{7,6},{8,9},{9,8},{10,11... | collective-permute-start | bytes 7077896 | tf_op jit(solution)/shard_map/ppermute | solution.py:103
  199.0 48.6 %collective-permute-start.27 = (bf16[2,3,288,512]{3,2,1,0:T(8,128)(2,1)}, bf16[2,3,288,512]{3,2,1,0:T(8,128)(2,1)}, u32[]{:S(2)}, u32[]{:S(2)}) collective-permute-start(bf16[2,3,288,512]{3,2,1,0:T(8,128)(2,1)} %constant_dynamic-update-slice_fusion.10.refs_3_), channel_id=1, source_target_pairs={{0,1},{1,0},{2,3},{3,2},{4,5},{5,4},{6,7},{7,6},{8,9},{9,8},{10,11... | collective-permute-start | bytes 5308424 | tf_op jit(solution)/shard_map/ppermute | solution.py:103
  199.5 48.1 %collective-permute-start.24 = (bf16[2,3,288,512]{3,2,1,0:T(8,128)(2,1)}, bf16[2,3,288,512]{3,2,1,0:T(8,128)(2,1)}, u32[]{:S(2)}, u32[]{:S(2)}) collective-permute-start(bf16[2,3,288,512]{3,2,1,0:T(8,128)(2,1)} %constant_dynamic-update-slice_fusion.10.refs_3_), channel_id=1, source_target_pairs={{0,8},{8,0},{16,24},{24,16},{1,9},{9,1},{17,25},{25,17},{2,10},{10... | collective-permute-start | bytes 5308424 | tf_op jit(solution)/shard_map/ppermute | solution.py:108
  201.1 46.6 %collective-permute-start.26 = (bf16[2,3,288,512]{3,2,1,0:T(8,128)(2,1)}, bf16[2,3,288,512]{3,2,1,0:T(8,128)(2,1)}, u32[]{:S(2)}, u32[]{:S(2)}) collective-permute-start(bf16[2,3,288,512]{3,2,1,0:T(8,128)(2,1)} %constant_dynamic-update-slice_fusion.8.refs_1_), channel_id=1, source_target_pairs={{0,1},{1,0},{2,3},{3,2},{4,5},{5,4},{6,7},{7,6},{8,9},{9,8},{10,11... | collective-permute-start | bytes 5308424 | tf_op jit(solution)/shard_map/ppermute | solution.py:103
  201.1 46.6 %collective-permute-start.23 = (bf16[2,3,288,512]{3,2,1,0:T(8,128)(2,1)}, bf16[2,3,288,512]{3,2,1,0:T(8,128)(2,1)}, u32[]{:S(2)}, u32[]{:S(2)}) collective-permute-start(bf16[2,3,288,512]{3,2,1,0:T(8,128)(2,1)} %constant_dynamic-update-slice_fusion.8.refs_1_), channel_id=1, source_target_pairs={{0,16},{8,24},{16,0},{24,8},{1,17},{9,25},{17,1},{25,9},{2,18},{10... | collective-permute-start | bytes 5308424 | tf_op jit(solution)/shard_map/ppermute | solution.py:108
  308.5 33.6 %collective-permute-start.31 = (bf16[4,1152,512]{2,1,0:T(8,128)(2,1)}, bf16[4,1152,512]{2,1,0:T(8,128)(2,1)}, u32[]{:S(2)}, u32[]{:S(2)}) collective-permute-start(bf16[4,1152,512]{2,1,0:T(8,128)(2,1)} %get-tuple-element.237), channel_id=1, source_target_pairs={{0,1},{1,0},{2,3},{3,2},{4,5},{5,4},{6,7},{7,6},{8,9},{9,8},{10,11... | collective-permute-start | bytes 14155784 | tf_op jit(solution)/shard_map/ppermute | solution.py:103
  308.9 297.9 %all-reduce.5.cloned.1.call-start = ((), (), s32[]{:S(2)}) async-start(), calls=%async_computation.2 | async-start | bytes 2359296 | tf_op jit(solution)/shard_map/psum | solution.py:1295
  348.1 35.4 %collective-permute-start.36 = (bf16[4,1152,512]{2,1,0:T(8,128)(2,1)}, bf16[4,1152,512]{2,1,0:T(8,128)(2,1)}, u32[]{:S(2)}, u32[]{:S(2)}) collective-permute-start(bf16[4,1152,512]{2,1,0:T(8,128)(2,1)} %get-tuple-element.256), channel_id=1, source_target_pairs={{0,1},{1,0},{2,3},{3,2},{4,5},{5,4},{6,7},{7,6},{8,9},{9,8},{10,11... | collective-permute-start | bytes 14155784 | tf_op jit(solution)/shard_map/ppermute | solution.py:103
  348.4 35.2 %collective-permute-start.32 = (bf16[4,2,144,512]{3,2,1,0:T(8,128)(2,1)}, bf16[4,2,144,512]{3,2,1,0:T(8,128)(2,1)S(1)}, u32[]{:S(2)}, u32[]{:S(2)}) collective-permute-start(bf16[4,2,144,512]{3,2,1,0:T(8,128)(2,1)} %fusion.13), channel_id=1, source_target_pairs={{0,8},{8,0},{16,24},{24,16},{1,9},{9,1},{17,25},{25,17},{2,10},{10... | collective-permute-start | bytes 3538952 | tf_op jit(solution)/shard_map/ppermute | solution.py:108
  349.8 33.7 %collective-permute-start.33 = (bf16[4,2,144,512]{3,2,1,0:T(8,128)(2,1)}, bf16[4,2,144,512]{3,2,1,0:T(8,128)(2,1)S(1)}, u32[]{:S(2)}, u32[]{:S(2)}) collective-permute-start(bf16[4,2,144,512]{3,2,1,0:T(8,128)(2,1)} %fusion.14), channel_id=1, source_target_pairs={{0,16},{8,24},{16,0},{24,8},{1,17},{9,25},{17,1},{25,9},{2,18},{10... | collective-permute-start | bytes 3538952 | tf_op jit(solution)/shard_map/ppermute | solution.py:108
  387.5 58.3 %collective-permute-start.37 = (bf16[4,2,144,512]{3,2,1,0:T(8,128)(2,1)}, bf16[4,2,144,512]{3,2,1,0:T(8,128)(2,1)S(1)}, u32[]{:S(2)}, u32[]{:S(2)}) collective-permute-start(bf16[4,2,144,512]{3,2,1,0:T(8,128)(2,1)} %fusion.15), channel_id=1, source_target_pairs={{0,8},{8,0},{16,24},{24,16},{1,9},{9,1},{17,25},{25,17},{2,10},{10... | collective-permute-start | bytes 3538952 | tf_op jit(solution)/shard_map/ppermute | solution.py:108
  391.2 54.6 %collective-permute-start.38 = (bf16[4,2,144,512]{3,2,1,0:T(8,128)(2,1)}, bf16[4,2,144,512]{3,2,1,0:T(8,128)(2,1)S(1)}, u32[]{:S(2)}, u32[]{:S(2)}) collective-permute-start(bf16[4,2,144,512]{3,2,1,0:T(8,128)(2,1)} %fusion.16), channel_id=1, source_target_pairs={{0,16},{8,24},{16,0},{24,8},{1,17},{9,25},{17,1},{25,9},{2,18},{10... | collective-permute-start | bytes 3538952 | tf_op jit(solution)/shard_map/ppermute | solution.py:108
  394.9 45.1 %collective-permute-start.35 = (bf16[4,144,512]{2,1,0:T(8,128)(2,1)}, bf16[4,144,512]{2,1,0:T(8,128)(2,1)}, u32[]{:S(2)}, u32[]{:S(2)}) collective-permute-start(bf16[4,144,512]{2,1,0:T(8,128)(2,1)} %get-tuple-element.482), channel_id=1, source_target_pairs={{0,8},{8,0},{16,24},{24,16},{1,9},{9,1},{17,25},{25,17},{2,10},{10... | collective-permute-start | bytes 1769480 | tf_op jit(solution)/shard_map/ppermute | solution.py:108
  396.3 43.7 %collective-permute-start.34 = (bf16[4,144,512]{2,1,0:T(8,128)(2,1)}, bf16[4,144,512]{2,1,0:T(8,128)(2,1)}, u32[]{:S(2)}, u32[]{:S(2)}) collective-permute-start(bf16[4,144,512]{2,1,0:T(8,128)(2,1)} %get-tuple-element.483), channel_id=1, source_target_pairs={{0,16},{8,24},{16,0},{24,8},{1,17},{9,25},{17,1},{25,9},{2,18},{10... | collective-permute-start | bytes 1769480 | tf_op jit(solution)/shard_map/ppermute | solution.py:108
  483.2 40.9 %collective-permute-start.42 = (bf16[4,2,208,512]{3,2,1,0:T(8,128)(2,1)}, bf16[4,2,208,512]{3,2,1,0:T(8,128)(2,1)S(1)}, u32[]{:S(2)}, u32[]{:S(2)}) collective-permute-start(bf16[4,2,208,512]{3,2,1,0:T(8,128)(2,1)} %fusion), channel_id=1, source_target_pairs={{0,8},{8,0},{16,24},{24,16},{1,9},{9,1},{17,25},{25,17},{2,10},{10... | collective-permute-start | bytes 5111816 | tf_op jit(solution)/shard_map/ppermute | solution.py:108
  487.6 36.5 %collective-permute-start.43 = (bf16[4,2,192,512]{3,2,1,0:T(8,128)(2,1)}, bf16[4,2,192,512]{3,2,1,0:T(8,128)(2,1)}, u32[]{:S(2)}, u32[]{:S(2)}) collective-permute-start(bf16[4,2,192,512]{3,2,1,0:T(8,128)(2,1)} %fusion.11), channel_id=1, source_target_pairs={{0,16},{8,24},{16,0},{24,8},{1,17},{9,25},{17,1},{25,9},{2,18},{10... | collective-permute-start | bytes 4718600 | tf_op jit(solution)/shard_map/ppermute | solution.py:108
  488.9 42.6 %collective-permute-start.46 = (bf16[288,512]{1,0:T(8,128)(2,1)}, bf16[288,512]{1,0:T(8,128)(2,1)}, u32[]{:S(2)}, u32[]{:S(2)}) collective-permute-start(bf16[288,512]{1,0:T(8,128)(2,1)} %pad_maximum_fusion.9), channel_id=1, source_target_pairs={{0,2},{1,3},{2,4},{3,5},{4,6},{5,7},{6,0},{7,1},{8,10},{9,11},{10,... | collective-permute-start | bytes 884744 | tf_op jit(solution)/shard_map/ppermute | solution.py:93
  489.4 42.1 %collective-permute-start.47 = (bf16[288,512]{1,0:T(8,128)(2,1)}, bf16[288,512]{1,0:T(8,128)(2,1)}, u32[]{:S(2)}, u32[]{:S(2)}) collective-permute-start(bf16[288,512]{1,0:T(8,128)(2,1)} %pad_maximum_fusion.10), channel_id=1, source_target_pairs={{0,4},{1,5},{2,6},{3,7},{4,0},{5,1},{6,2},{7,3},{8,12},{9,13},{10,... | collective-permute-start | bytes 884744 | tf_op jit(solution)/shard_map/ppermute | solution.py:93
  490.8 40.7 %collective-permute-start.48 = (bf16[288,512]{1,0:T(8,128)(2,1)}, bf16[288,512]{1,0:T(8,128)(2,1)}, u32[]{:S(2)}, u32[]{:S(2)}) collective-permute-start(bf16[288,512]{1,0:T(8,128)(2,1)} %pad_maximum_fusion.11), channel_id=1, source_target_pairs={{0,6},{1,7},{2,0},{3,1},{4,2},{5,3},{6,4},{7,5},{8,14},{9,15},{10,... | collective-permute-start | bytes 884744 | tf_op jit(solution)/shard_map/ppermute | solution.py:93
  579.5 39.6 %collective-permute-start.52 = (bf16[400,512]{1,0:T(8,128)(2,1)}, bf16[400,512]{1,0:T(8,128)(2,1)}, u32[]{:S(2)}, u32[]{:S(2)}) collective-permute-start(bf16[400,512]{1,0:T(8,128)(2,1)} %pad_maximum_fusion.6), channel_id=1, source_target_pairs={{0,2},{1,3},{2,4},{3,5},{4,6},{5,7},{6,0},{7,1},{8,10},{9,11},{10,... | collective-permute-start | bytes 1228808 | tf_op jit(solution)/shard_map/ppermute | solution.py:93
  586.3 32.8 %collective-permute-start.53 = (bf16[400,512]{1,0:T(8,128)(2,1)}, bf16[400,512]{1,0:T(8,128)(2,1)}, u32[]{:S(2)}, u32[]{:S(2)}) collective-permute-start(bf16[400,512]{1,0:T(8,128)(2,1)} %pad_maximum_fusion.7), channel_id=1, source_target_pairs={{0,4},{1,5},{2,6},{3,7},{4,0},{5,1},{6,2},{7,3},{8,12},{9,13},{10,... | collective-permute-start | bytes 1228808 | tf_op jit(solution)/shard_map/ppermute | solution.py:93
  586.3 32.8 %collective-permute-start.54 = (bf16[400,512]{1,0:T(8,128)(2,1)}, bf16[400,512]{1,0:T(8,128)(2,1)}, u32[]{:S(2)}, u32[]{:S(2)}) collective-permute-start(bf16[400,512]{1,0:T(8,128)(2,1)} %pad_maximum_fusion.8), channel_id=1, source_target_pairs={{0,6},{1,7},{2,0},{3,1},{4,2},{5,3},{6,4},{7,5},{8,14},{9,15},{10,... | collective-permute-start | bytes 1228808 | tf_op jit(solution)/shard_map/ppermute | solution.py:93
  642.3 31.1 %collective-permute-start.65 = (bf16[2,400,512]{2,1,0:T(8,128)(2,1)S(1)}, bf16[2,400,512]{2,1,0:T(8,128)(2,1)S(1)}, u32[]{:S(2)}, u32[]{:S(2)}) collective-permute-start(bf16[2,400,512]{2,1,0:T(8,128)(2,1)S(1)} %reverse_select_fusion.3), channel_id=1, source_target_pairs={{0,16},{8,24},{16,0},{24,8},{1,17},{9,25},{17,1},{25,9},{2,18},{10... | collective-permute-start | bytes 2457608 | tf_op jit(solution)/shard_map/ppermute | solution.py:108
  (94 other events, 1162.1 us)
Sparse Core Ops, SparseCore 0:
  44.4 40.0 all-gather.4
  86.7 49.3 all-gather.6
  309.0 84.1 reduce-scatter.1
  541.9 64.8 all-reduce.4

commit v4 on v3

--- a/solution.py
+++ b/solution.py
@@ -427,11 +427,11 @@
     w = w_ref[...].reshape(width, BLK)
 
     def body(i, _):
-        rows = pl.ds(pl.multiple_of(i * 256, 256), 256)
+        rows = pl.ds(pl.multiple_of(i * 512, 512), 512)
         qkv_ref[rows, :] = dot(n1_ref[rows, :], w).astype(bf16)
         return 0
 
-    lax.fori_loop(0, tokens // 256, body, 0)
+    lax.fori_loop(0, tokens // 512, body, 0)
 
 
 def qkv_call(x, gain, w_in, rows, n, after=()):
@@ -481,8 +481,6 @@
             raised = jnp.exp(s - jnp.max(s, axis=0, keepdims=True))
             probs = (raised * (1.0 / jnp.sum(raised, axis=0, keepdims=True))).astype(bf16)
             p_ref[0, h, :stop, start:stop] = probs
-            if stop < seq:
-                p_ref[0, h, stop:, start:stop] = jnp.zeros((seq - stop, HALF), bf16)
             mixed = dot_first(v_ref[:stop, kv], probs)
             mix_ref[start:stop, lanes] = mixed.T.astype(bf16)
 
@@ -595,12 +593,13 @@
 
 
 TILE = 256
+WIDE_TILE = 512
 
 
 def resid_kernel(rows, n, mix_ref, w_ref, x_ref, gain_ref, router_ref, resid_ref, n2_ref, prob_ref):
     width = x_ref.shape[1]
     mixed = mix_ref[...]
-    squares = jnp.zeros((TILE, 1), f32)
+    squares = jnp.zeros((WIDE_TILE, 1), f32)
     for j in range(n):
         cols = slice(j * BLK, (j + 1) * BLK)
         w = w_ref[:, j * rows : (j + 1) * rows, :].reshape(-1, BLK)
@@ -618,11 +617,11 @@
 
 def resid_call(mixed, w_out, at, x, gain, router, rows, n, after=()):
     tokens, width = x.shape
-    tile = pl.BlockSpec((TILE, width), lambda i: (i, 0))
+    tile = pl.BlockSpec((WIDE_TILE, width), lambda i: (i, 0))
     return kernel_call(
         functools.partial(resid_kernel, rows, n),
         [mixed, w_out, x, gain, router],
-        grid=(tokens // TILE,),
+        grid=(tokens // WIDE_TILE,),
         in_specs=[
             tile,
             pl.BlockSpec((w_out.shape[0], n * rows, BLK), lambda i: (0, at, 0), pipeline_mode=pl.Buffered(1)),
@@ -630,7 +629,7 @@
             whole((1, width)),
             whole((8, width)),
         ],
-        out_specs=[tile, tile, pl.BlockSpec((8, TILE), lambda i: (0, i))],
+        out_specs=[tile, tile, pl.BlockSpec((8, WIDE_TILE), lambda i: (0, i))],
         out_shape=[
             jax.ShapeDtypeStruct((tokens, width), f32),
             jax.ShapeDtypeStruct((tokens, width), bf16),
@@ -1063,13 +1062,13 @@
 
 def input_grad_call(dqkv, w_in, x, dresid, gain, rows, n, after=()):
     tokens, width = x.shape
-    tile = pl.BlockSpec((TILE, width), lambda i: (i, 0))
+    tile = pl.BlockSpec((WIDE_TILE, width), lambda i: (i, 0))
     return kernel_call(
         functools.partial(input_grad_kernel, rows, n),
         [dqkv, w_in, x, dresid, gain],
-        grid=(tokens // TILE,),
+        grid=(tokens // WIDE_TILE,),
         in_specs=[
-            pl.BlockSpec((TILE, n * BLK), lambda i: (i, 0)),
+            pl.BlockSpec((WIDE_TILE, n * BLK), lambda i: (i, 0)),
             whole((w_in.shape[0], n * rows, BLK)),
             tile,
             tile,

time: 716 us -> 718 us (level)
  no operation moved by 1% of the time
where the time goes in v4:
time: 718 us; the launch traced here: 708 us
  Pallas kernels  387 us (54%)
  waiting for transfers between devices  116 us (16%)
  other arithmetic  79.9 us (11%)
  starting transfers between devices  70.8 us (10%)
  local copies, waits for them, and re-layouts  35 us (5%)
  between operations  19 us (3%)
    pallas_call x26, Pallas kernels, kernel_call(): pl.pallas_call(kernel, grid_spec=pltpu.PrefetchScalarGridSpec(num_scalar_...  387 us
    ppermute x32, waiting for transfers between devices, swap_replica(): return lax.ppermute(x, 'replica', [(i, i ^ bit) for i in range(size)])  60.8 us
    ppermute x32, starting transfers between devices, swap_replica(): return lax.ppermute(x, 'replica', [(i, i ^ bit) for i in range(size)])  35.2 us
    convert_element_type x10, other arithmetic, halve(): away = self.part_sum([take(t, 1 - own) for t in self.terms[p]]).astype(bf16)  29.2 us
    ppermute x12, starting transfers between devices, shift_core_pairs(): lax.ppermute(x, 'fsdp', [(i, (i + 2 * k) % size) for i in range(size)])  24.2 us
    unnamed x116, local copies, waits for them, and re-layouts  20.2 us
    ppermute x12, waiting for transfers between devices, shift_core_pairs(): lax.ppermute(x, 'fsdp', [(i, (i + 2 * k) % size) for i in range(size)])  17.7 us
    psum x1, waiting for transfers between devices, per_device(): sum0 = lax.psum(part0, 'replica')  16.1 us
  transfers between devices with their start and end apart: 73, of which 20 were waited for; matrix products, arithmetic and copies ran while one was open for 11% of the time, Pallas kernels for 49%

profile of v4, /device:TPU:0, one launch (start us, length us, event | category | flops | bytes accessed | tf_op | source)
XLA Modules:
  0.0 708.2 jit_solution(6246543532771020412)
XLA Ops:
  13.1 4.6 collective-permute-start.3
  22.2 4.4 pack.5
  26.6 14.3 %collective-permute-done.2.refs_1_ = bf16[256,512]{1,0:T(8,128)(2,1)S(1)} collective-permute-done((bf16[256,512]{1,0:T(8,128)(2,1)}, bf16[256,512]{1,0:T(8,128)(2,1)S(1)}, u32[]{:S(2)}, u32[]{:S(2)}) %collective-permute-start.2) | collective-permute-done | bytes 262176 | tf_op jit(solution)/shard_map/ppermute | solution.py:93
  49.5 5.9 collective-permute-done.4
  58.9 15.9 %collective-permute-done.7.refs_4_ = bf16[2,3,128,512]{3,2,1,0:T(8,128)(2,1)} collective-permute-done((bf16[2,3,128,512]{3,2,1,0:T(8,128)(2,1)S(1)}, bf16[2,3,128,512]{3,2,1,0:T(8,128)(2,1)}, u32[]{:S(2)}, u32[]{:S(2)}) %collective-permute-start.7) | collective-permute-done | bytes 786464 | tf_op jit(solution)/shard_map/ppermute | solution.py:108
  75.8 8.7 %all-gather.5.cloned.1.call-done = bf16[1728,512]{1,0:T(8,128)(2,1)} async-done(((bf16[432,512]{1,0:T(8,128)(2,1)}), bf16[1728,512]{1,0:T(8,128)(2,1)}) %all-gather.5.cloned.1.call-update) | async-done | bytes 1769488 | tf_op jit(solution)/shard_map/all_gather | solution.py:177
  91.4 7.8 %assemble.3.w_ref = bf16[8,1024,512]{2,1,0:T(8,128)(2,1)} custom-call(s32[3]{0:T(128)} %pad_add_fusion.idx_ref, bf16[1024,512]{1,0:T(8,128)(2,1)} %get-tuple-element.181.refs_0_, bf16[2,3,128,512]{3,2,1,0:T(8,128)(2,1)} %copy-done.13, bf16[2,3,128,512]{3,2,1,0:T(8,128)(2,1)} %collective-permute-done.6.refs_2_, bf16[2,3,128,512]{3,2,1,0:T(8,128)(2,1)} %copy-done.14, ...), custom_call_target="tpu_custom_call" | custom-call | bytes 16 | tf_op jit(solution)/shard_map/assemble/pallas_call | solution.py:70
  100.9 16.5 %qkv.1 = (bf16[1024,2560]{1,0:T(8,128)(2,1)}, bf16[1024,1536]{1,0:T(8,128)(2,1)}) custom-call(bf16[1024,1536]{1,0:T(8,128)(2,1)} %bitcast.357, f32[1,1536]{1,0:T(1,128)} %reshape.788.gain_ref, bf16[8,1024,512]{2,1,0:T(8,128)(2,1)} %assemble.3.w_ref), custom_call_target="tpu_custom_call" | custom-call | flops 8 | bytes 14 | tf_op jit(solution)/shard_map/qkv/pallas_call | solution.py:70
  122.8 37.3 %attention.1 = (bf16[2,24,512,512]{3,2,1,0:T(8,128)(2,1)}, bf16[1024,1536]{1,0:T(8,128)(2,1)}) custom-call(s32[2]{0:T(128)} %bitcast.412, bf16[1024,2560]{1,0:T(8,128)(2,1)} %get-tuple-element.258.q_ref.k_ref.v_ref, bf16[1024,2560]{1,0:T(8,128)(2,1)} %get-tuple-element.258.q_ref.k_ref.v_ref, bf16[1024,2560]{1,0:T(8,128)(2,1)} %get-tuple-element.258.q_ref.k_ref.v_ref), custom_call_target="tpu_custom_call" | custom-call | flops 12 | bytes 25 | tf_op jit(solution)/shard_map/attention/pallas_call | solution.py:70
  168.9 11.5 %assemble.4.w_ref.up_a_ref.up_b_ref.down_ref = bf16[8,1728,512]{2,1,0:T(8,128)(2,1)} custom-call(s32[3]{0:T(128)} %pad_add_fusion.idx_ref, bf16[1728,512]{1,0:T(8,128)(2,1)} %get-tuple-element.183.refs_4_.refs_0_, bf16[2,3,224,512]{3,2,1,0:T(8,128)(2,1)} %copy-done.11, bf16[2,3,224,512]{3,2,1,0:T(8,128)(2,1)} %collective-permute-done.14.refs_2_, ...), custom_call_target="tpu_custom_call" | custom-call | bytes 28 | tf_op jit(solution)/shard_map/assemble/pallas_call | solution.py:70
  180.4 11.5 %resid.1 = (f32[1024,1536]{1,0:T(8,128)}, bf16[1024,1536]{1,0:T(8,128)(2,1)}, f32[8,1024]{1,0:T(8,128)}) custom-call(bf16[1024,1536]{1,0:T(8,128)(2,1)} %get-tuple-element.203.mix_ref.left_ref, bf16[8,1728,512]{2,1,0:T(8,128)(2,1)} %assemble.4.w_ref.up_a_ref.up_b_ref.down_ref, bf16[1024,1536]{1,0:T(8,128)(2,1)} %bitcast.358, f32[1,1536]{1,0:T(1,128)} %reshape.789.gain_ref, ...), custom_call_target="tpu_custom_call" | custom-call | flops 4 | bytes 23 | tf_op jit(solution)/shard_map/resid/pallas_call | solution.py:70
  200.2 12.1 %dispatch.1 = (bf16[3,2,320,1536]{3,2,1,0:T(8,128)(2,1)}, bf16[3,2,320,1536]{3,2,1,0:T(8,128)(2,1)}, f32[3,2,320,128]{3,2,1,0:T(8,128)}) custom-call(s32[2,8,512]{2,1,0:T(8,128)} %stack.96.slot_ref, f32[8,1024]{1,0:T(8,128)} %get-tuple-element.219.prob_ref, bf16[1024,1536]{1,0:T(8,128)(2,1)} %get-tuple-element.220.n2_ref, bf16[1024,1536]{1,0:T(8,128)(2,1)} %bitcast.381), custom_call_target="tpu_custom_call" | custom-call | flops 6 | bytes 31 | tf_op jit(solution)/shard_map/dispatch/pallas_call | solution.py:70
  212.3 32.6 %expert.3 = (bf16[2,320,1536]{2,1,0:T(8,128)(2,1)}, bf16[2,320,1536]{2,1,0:T(8,128)(2,1)}, f32[2,8,512]{2,1,0:T(8,128)}, bf16[4,1152,512]{2,1,0:T(8,128)(2,1)}, bf16[4,1152,512]{2,1,0:T(8,128)(2,1)}) custom-call(s32[1]{0:T(128)} %bitcast.8.idx_ref, bf16[3,2,320,1536]{3,2,1,0:T(8,128)(2,1)} %get-tuple-element.221.buf_ref, ...), custom_call_target="tpu_custom_call" | custom-call | flops 18 | bytes 62 | tf_op jit(solution)/shard_map/expert/pallas_call | solution.py:70
  252.7 14.6 %assemble.5.up_a_ref.up_b_ref.down_ref = bf16[8,2304,512]{2,1,0:T(8,128)(2,1)} custom-call(s32[3]{0:T(128)} %pad_add_fusion.idx_ref, bf16[2304,512]{1,0:T(8,128)(2,1)} %get-tuple-element.184.refs_0_, bf16[2,3,288,512]{3,2,1,0:T(8,128)(2,1)} %constant_dynamic-update-slice_fusion.8.refs_1_, bf16[2,3,288,512]{3,2,1,0:T(8,128)(2,1)} %collective-permute-done.23.refs_2_, ...), custom_call_target="tpu_custom_call" | custom-call | bytes 37 | tf_op jit(solution)/shard_map/assemble/pallas_call | solution.py:70
  267.3 5.9 add_convert_fusion
  273.3 32.8 %expert.4 = (bf16[2,320,1536]{2,1,0:T(8,128)(2,1)}, bf16[2,320,1536]{2,1,0:T(8,128)(2,1)}, f32[2,8,512]{2,1,0:T(8,128)}, bf16[4,1152,512]{2,1,0:T(8,128)(2,1)}, bf16[4,1152,512]{2,1,0:T(8,128)(2,1)}) custom-call(s32[1]{0:T(128)} %bitcast.8.idx_ref, bf16[3,2,320,1536]{3,2,1,0:T(8,128)(2,1)} %get-tuple-element.221.buf_ref, ...), custom_call_target="tpu_custom_call" | custom-call | flops 18 | bytes 62 | tf_op jit(solution)/shard_map/expert/pallas_call | solution.py:70
  306.5 32.9 %expert.5 = (bf16[2,320,1536]{2,1,0:T(8,128)(2,1)}, bf16[2,320,1536]{2,1,0:T(8,128)(2,1)}, f32[2,8,512]{2,1,0:T(8,128)}, bf16[4,1152,512]{2,1,0:T(8,128)(2,1)}, bf16[4,1152,512]{2,1,0:T(8,128)(2,1)}) custom-call(s32[1]{0:T(128)} %bitcast.8.idx_ref, bf16[3,2,320,1536]{3,2,1,0:T(8,128)(2,1)} %get-tuple-element.221.buf_ref, ...), custom_call_target="tpu_custom_call" | custom-call | flops 18 | bytes 62 | tf_op jit(solution)/shard_map/expert/pallas_call | solution.py:70
  349.5 19.9 %middle.1 = (f32[1024,1536]{1,0:T(8,128)}, bf16[1024,1536]{1,0:T(8,128)(2,1)}, bf16[1024,1536]{1,0:T(8,128)(2,1)}, f32[8,1536]{1,0:T(8,128)}) custom-call(s32[1024,8]{1,0:T(8,128)} %bitcast.383, bf16[2,320,1536]{2,1,0:T(8,128)(2,1)} %get-tuple-element.243.d0_ref, bf16[2,320,1536]{2,1,0:T(8,128)(2,1)} %get-tuple-element.244.d1_ref, ...), custom_call_target="tpu_custom_call" | custom-call | flops 7 | bytes 31 | tf_op jit(solution)/shard_map/middle/pallas_call | solution.py:70
  369.5 9.8 %out_grad.1 = (bf16[4,1600,512]{2,1,0:T(8,128)(2,1)}, bf16[4,1600,512]{2,1,0:T(8,128)(2,1)}) custom-call(s32[1]{0:T(128)} %bitcast.8.idx_ref, bf16[1024,1536]{1,0:T(8,128)(2,1)} %get-tuple-element.203.mix_ref.left_ref, bf16[1024,1536]{1,0:T(8,128)(2,1)} %get-tuple-element.249.right_ref), custom_call_target="tpu_custom_call" | custom-call | flops 4 | bytes 11 | tf_op jit(solution)/shard_map/out_grad/pallas_call | solution.py:70
  395.0 42.5 %attention_back.1 = (bf16[1024,1536]{1,0:T(8,128)(2,1)}, bf16[1024,512]{1,0:T(8,128)(2,1)}, bf16[1024,512]{1,0:T(8,128)(2,1)}) custom-call(bf16[1024,2560]{1,0:T(8,128)(2,1)} %get-tuple-element.258.q_ref.k_ref.v_ref, bf16[1024,2560]{1,0:T(8,128)(2,1)} %get-tuple-element.258.q_ref.k_ref.v_ref, bf16[1024,2560]{1,0:T(8,128)(2,1)} %get-tuple-element.258.q_ref.k_ref.v_ref, ...), custom_call_target="tpu_custom_call" | custom-call | flops 25 | bytes 25 | tf_op jit(solution)/shard_map/attention_back/pallas_call | solution.py:70
  451.7 13.4 %in_grad.1 = (bf16[4,1600,512]{2,1,0:T(8,128)(2,1)}, bf16[4,1600,512]{2,1,0:T(8,128)(2,1)}) custom-call(s32[1]{0:T(128)} %bitcast.8.idx_ref, bf16[1024,1536]{1,0:T(8,128)(2,1)} %get-tuple-element.267.left_ref, bf16[1024,2560]{1,0:T(8,128)(2,1)} %copy-done, ...), custom_call_target="tpu_custom_call", output_to_operand_aliasing={{0}: (3, {}), {1}: (4, {})} | custom-call | flops 8 | bytes 14 | tf_op jit(solution)/shard_map/in_grad/pallas_call | solution.py:70
  466.8 10.6 %combine.1 = bf16[1024,1536]{1,0:T(8,128)(2,1)} custom-call(s32[1024,8]{1,0:T(8,128)} %bitcast.384, f32[1024,1536]{1,0:T(8,128)} %get-tuple-element.215.resid_ref, bf16[2,320,1536]{2,1,0:T(8,128)(2,1)} %get-tuple-element.226.y0_ref, bf16[2,320,1536]{2,1,0:T(8,128)(2,1)} %get-tuple-element.238.y1_ref, bf16[2,320,1536]{2,1,0:T(8,128)(2,1)} %get-tuple-element.240.y2_ref), custom_call_target="tpu_custom_call" | custom-call | flops 3 | bytes 18 | tf_op jit(solution)/shard_map/combine/pallas_call | solution.py:70
  490.8 17.0 %input_grad.1 = bf16[1024,1536]{1,0:T(8,128)(2,1)} custom-call(bf16[1024,2560]{1,0:T(8,128)(2,1)} %copy-done, bf16[8,1024,512]{2,1,0:T(8,128)(2,1)} %assemble.3.w_ref, bf16[1024,1536]{1,0:T(8,128)(2,1)} %bitcast.359, f32[1024,1536]{1,0:T(8,128)} %get-tuple-element.279.dresid_ref, f32[1,1536]{1,0:T(1,128)} %reshape.788.gain_ref), custom_call_target="tpu_custom_call" | custom-call | flops 8 | bytes 26 | tf_op jit(solution)/shard_map/input_grad/pallas_call | solution.py:70
  507.8 13.9 %collective-permute-done.43 = bf16[4,2,192,512]{3,2,1,0:T(8,128)(2,1)} collective-permute-done((bf16[4,2,192,512]{3,2,1,0:T(8,128)(2,1)}, bf16[4,2,192,512]{3,2,1,0:T(8,128)(2,1)}, u32[]{:S(2)}, u32[]{:S(2)}) %collective-permute-start.43) | collective-permute-done | bytes 1572896 | tf_op jit(solution)/shard_map/ppermute | solution.py:108
  539.3 9.4 %collective-permute-done.45 = bf16[4,192,512]{2,1,0:T(8,128)(2,1)} collective-permute-done((bf16[4,192,512]{2,1,0:T(8,128)(2,1)}, bf16[4,192,512]{2,1,0:T(8,128)(2,1)}, u32[]{:S(2)}, u32[]{:S(2)}) %collective-permute-start.45) | collective-permute-done | bytes 786464 | tf_op jit(solution)/shard_map/ppermute | solution.py:108
  566.4 8.3 %collective-permute-done.55 = bf16[288,512]{1,0:T(8,128)(2,1)S(1)} collective-permute-done((bf16[288,512]{1,0:T(8,128)(2,1)S(1)}, bf16[288,512]{1,0:T(8,128)(2,1)S(1)}, u32[]{:S(2)}, u32[]{:S(2)}) %collective-permute-start.55) | collective-permute-done | bytes 294944 | tf_op jit(solution)/shard_map/ppermute | solution.py:108
  576.8 7.2 %collective-permute-start.52 = (bf16[400,512]{1,0:T(8,128)(2,1)}, bf16[400,512]{1,0:T(8,128)(2,1)}, u32[]{:S(2)}, u32[]{:S(2)}) collective-permute-start(bf16[400,512]{1,0:T(8,128)(2,1)} %pad_maximum_fusion.6), channel_id=1, source_target_pairs={{0,2},{1,3},{2,4},{3,5},{4,6},{5,7},{6,0},{7,1},{8,10},{9,11},{10,... | collective-permute-start | bytes 1228808 | tf_op jit(solution)/shard_map/ppermute | solution.py:93
  588.1 16.1 %all-reduce.5.cloned.1.call-done.g0_ref = bf16[1152,512]{1,0:T(8,128)(2,1)} async-done(((bf16[1152,512]{1,0:T(8,128)(2,1)}), bf16[1152,512]{1,0:T(8,128)(2,1)}) %all-reduce.5.cloned.1.call-update) | async-done | bytes 1179664 | tf_op jit(solution)/shard_map/psum | solution.py:1294
  640.6 12.0 %down_adam.1 = (f32[3,128,1536]{2,1,0:T(8,128)}, f32[3,128,1536]{2,1,0:T(8,128)}, f32[3,128,1536]{2,1,0:T(8,128)}, f32[3,128,1536]{2,1,0:T(8,128)}) custom-call(f32[8,128]{1,0:T(8,128)} %get-tuple-element.319.clip_ref, bf16[1152,512]{1,0:T(8,128)(2,1)} %all-reduce.5.cloned.1.call-done.g0_ref, bf16[1152,512]{1,0:T(8,128)(2,1)} %bitcast.379, ...), custom_call_target="tpu_custom_call" | custom-call | bytes 17 | tf_op jit(solution)/shard_map/down_adam/pallas_call | solution.py:70
  652.5 18.0 %up_adam.1 = (f32[3,192,2048]{2,1,0:T(8,128)}, f32[3,192,2048]{2,1,0:T(8,128)}, f32[3,192,2048]{2,1,0:T(8,128)}, f32[3,192,2048]{2,1,0:T(8,128)}) custom-call(f32[8,128]{1,0:T(8,128)} %get-tuple-element.319.clip_ref, bf16[1152,512]{1,0:T(8,128)(2,1)} %all-reduce.5.cloned.1.call-done.g0_ref, bf16[1152,512]{1,0:T(8,128)(2,1)} %bitcast.380, ...), custom_call_target="tpu_custom_call" | custom-call | bytes 35 | tf_op jit(solution)/shard_map/up_adam/pallas_call | solution.py:70
  674.0 6.5 out_adam.1
  683.6 9.5 %in_adam.1 = (f32[192,2560]{1,0:T(8,128)}, f32[192,2560]{1,0:T(8,128)}, f32[192,2560]{1,0:T(8,128)}, f32[192,2560]{1,0:T(8,128)}) custom-call(f32[8,128]{1,0:T(8,128)} %get-tuple-element.319.clip_ref, bf16[1600,512]{1,0:T(8,128)(2,1)} %bitcast.371, f32[192,2560]{1,0:T(8,128)} %master_ref.7, f32[192,2560]{1,0:T(8,128)} %first_ref.7, f32[192,2560]{1,0:T(8,128)} %second_ref.7), custom_call_target="tpu_custom_call" | custom-call | bytes 14 | tf_op jit(solution)/shard_map/in_adam/pallas_call | solution.py:70
  (380 shorter events, 205.8 us)
Async XLA Ops:
  7.2 77.3 %all-gather.5.cloned.1.call-start = ((), (), s32[]{:S(2)}) async-start(), calls=%async_computation.3 | async-start | bytes 2211840 | tf_op jit(solution)/shard_map/all_gather | solution.py:177
  44.3 117.4 %all-gather.7.cloned.1.call-start = ((), (), s32[]{:S(2)}) async-start(), calls=%async_computation.4 | async-start | bytes 2949120 | tf_op jit(solution)/shard_map/all_gather | solution.py:177
  84.6 310.4 %reduce-scatter.2.cloned.1.call-start = ((), (), s32[]{:S(2)}) async-start(), calls=%async_computation.1 | async-start | bytes 5898240 | tf_op jit(solution)/shard_map/reduce_scatter | solution.py:1254
  87.8 30.8 %collective-permute-start.9 = (bf16[1,3,208,512]{3,2,1,0:T(8,128)(2,1)}, bf16[1,3,208,512]{3,2,1,0:T(8,128)(2,1)}, u32[]{:S(2)}, u32[]{:S(2)}) collective-permute-start(bf16[1,3,208,512]{3,2,1,0:T(8,128)(2,1)} %get-tuple-element.195), channel_id=1, source_target_pairs={{0,16},{8,24},{16,0},{24,8},{1,17},{9,25},{17,1},{25,9},{2,18},{10... | collective-permute-start | bytes 1916936 | tf_op jit(solution)/shard_map/ppermute | solution.py:108
  91.3 68.8 %collective-permute-start.16 = (bf16[1728,512]{1,0:T(8,128)(2,1)S(1)}, bf16[1728,512]{1,0:T(8,128)(2,1)}, u32[]{:S(2)}, u32[]{:S(2)}) collective-permute-start(bf16[1728,512]{1,0:T(8,128)(2,1)S(1)} %copy-done.5), channel_id=1, source_target_pairs={{0,1},{1,0},{2,3},{3,2},{4,5},{5,4},{6,7},{7,6},{8,9},{9,8},{10,11... | collective-permute-start | bytes 5308424 | tf_op jit(solution)/shard_map/ppermute | solution.py:103
  119.7 40.4 %collective-permute-start.17 = (bf16[2,3,224,512]{3,2,1,0:T(8,128)(2,1)S(1)}, bf16[2,3,224,512]{3,2,1,0:T(8,128)(2,1)S(1)}, u32[]{:S(2)}, u32[]{:S(2)}) collective-permute-start(bf16[2,3,224,512]{3,2,1,0:T(8,128)(2,1)S(1)} %constant_dynamic-update-slice_fusion.4.refs_1_), channel_id=1, source_target_pairs={{0,1},{1,0},{2,3},{3,2},{4,5},{5,4},{6,7},{7,6},{8,9},{9,8},{10,11... | collective-permute-start | bytes 4128776 | tf_op jit(solution)/shard_map/ppermute | solution.py:103
  120.2 39.9 %collective-permute-start.14 = (bf16[2,3,224,512]{3,2,1,0:T(8,128)(2,1)S(1)}, bf16[2,3,224,512]{3,2,1,0:T(8,128)(2,1)}, u32[]{:S(2)}, u32[]{:S(2)}) collective-permute-start(bf16[2,3,224,512]{3,2,1,0:T(8,128)(2,1)S(1)} %constant_dynamic-update-slice_fusion.4.refs_1_), channel_id=1, source_target_pairs={{0,16},{8,24},{16,0},{24,8},{1,17},{9,25},{17,1},{25,9},{2,18},{10... | collective-permute-start | bytes 4128776 | tf_op jit(solution)/shard_map/ppermute | solution.py:108
  122.0 38.1 %collective-permute-start.18 = (bf16[2,3,208,512]{3,2,1,0:T(8,128)(2,1)S(1)}, bf16[2,3,208,512]{3,2,1,0:T(8,128)(2,1)}, u32[]{:S(2)}, u32[]{:S(2)}) collective-permute-start(bf16[2,3,208,512]{3,2,1,0:T(8,128)(2,1)S(1)} %constant_dynamic-update-slice_fusion.6.refs_3_), channel_id=1, source_target_pairs={{0,1},{1,0},{2,3},{3,2},{4,5},{5,4},{6,7},{7,6},{8,9},{9,8},{10,11... | collective-permute-start | bytes 3833864 | tf_op jit(solution)/shard_map/ppermute | solution.py:103
  122.1 38.0 %collective-permute-start.15 = (bf16[2,3,208,512]{3,2,1,0:T(8,128)(2,1)S(1)}, bf16[2,3,208,512]{3,2,1,0:T(8,128)(2,1)}, u32[]{:S(2)}, u32[]{:S(2)}) collective-permute-start(bf16[2,3,208,512]{3,2,1,0:T(8,128)(2,1)S(1)} %constant_dynamic-update-slice_fusion.6.refs_3_), channel_id=1, source_target_pairs={{0,8},{8,0},{16,24},{24,16},{1,9},{9,1},{17,25},{25,17},{2,10},{10... | collective-permute-start | bytes 3833864 | tf_op jit(solution)/shard_map/ppermute | solution.py:108
  167.5 77.4 %collective-permute-start.25 = (bf16[2304,512]{1,0:T(8,128)(2,1)S(1)}, bf16[2304,512]{1,0:T(8,128)(2,1)}, u32[]{:S(2)}, u32[]{:S(2)}) collective-permute-start(bf16[2304,512]{1,0:T(8,128)(2,1)S(1)} %copy-done.6), channel_id=1, source_target_pairs={{0,1},{1,0},{2,3},{3,2},{4,5},{5,4},{6,7},{7,6},{8,9},{9,8},{10,11... | collective-permute-start | bytes 7077896 | tf_op jit(solution)/shard_map/ppermute | solution.py:103
  196.5 48.4 %collective-permute-start.27 = (bf16[2,3,288,512]{3,2,1,0:T(8,128)(2,1)}, bf16[2,3,288,512]{3,2,1,0:T(8,128)(2,1)}, u32[]{:S(2)}, u32[]{:S(2)}) collective-permute-start(bf16[2,3,288,512]{3,2,1,0:T(8,128)(2,1)} %constant_dynamic-update-slice_fusion.10.refs_3_), channel_id=1, source_target_pairs={{0,1},{1,0},{2,3},{3,2},{4,5},{5,4},{6,7},{7,6},{8,9},{9,8},{10,11... | collective-permute-start | bytes 5308424 | tf_op jit(solution)/shard_map/ppermute | solution.py:103
  197.1 47.9 %collective-permute-start.24 = (bf16[2,3,288,512]{3,2,1,0:T(8,128)(2,1)}, bf16[2,3,288,512]{3,2,1,0:T(8,128)(2,1)}, u32[]{:S(2)}, u32[]{:S(2)}) collective-permute-start(bf16[2,3,288,512]{3,2,1,0:T(8,128)(2,1)} %constant_dynamic-update-slice_fusion.10.refs_3_), channel_id=1, source_target_pairs={{0,8},{8,0},{16,24},{24,16},{1,9},{9,1},{17,25},{25,17},{2,10},{10... | collective-permute-start | bytes 5308424 | tf_op jit(solution)/shard_map/ppermute | solution.py:108
  198.7 46.3 %collective-permute-start.26 = (bf16[2,3,288,512]{3,2,1,0:T(8,128)(2,1)}, bf16[2,3,288,512]{3,2,1,0:T(8,128)(2,1)}, u32[]{:S(2)}, u32[]{:S(2)}) collective-permute-start(bf16[2,3,288,512]{3,2,1,0:T(8,128)(2,1)} %constant_dynamic-update-slice_fusion.8.refs_1_), channel_id=1, source_target_pairs={{0,1},{1,0},{2,3},{3,2},{4,5},{5,4},{6,7},{7,6},{8,9},{9,8},{10,11... | collective-permute-start | bytes 5308424 | tf_op jit(solution)/shard_map/ppermute | solution.py:103
  198.7 46.3 %collective-permute-start.23 = (bf16[2,3,288,512]{3,2,1,0:T(8,128)(2,1)}, bf16[2,3,288,512]{3,2,1,0:T(8,128)(2,1)}, u32[]{:S(2)}, u32[]{:S(2)}) collective-permute-start(bf16[2,3,288,512]{3,2,1,0:T(8,128)(2,1)} %constant_dynamic-update-slice_fusion.8.refs_1_), channel_id=1, source_target_pairs={{0,16},{8,24},{16,0},{24,8},{1,17},{9,25},{17,1},{25,9},{2,18},{10... | collective-permute-start | bytes 5308424 | tf_op jit(solution)/shard_map/ppermute | solution.py:108
  306.1 33.3 %collective-permute-start.31 = (bf16[4,1152,512]{2,1,0:T(8,128)(2,1)}, bf16[4,1152,512]{2,1,0:T(8,128)(2,1)}, u32[]{:S(2)}, u32[]{:S(2)}) collective-permute-start(bf16[4,1152,512]{2,1,0:T(8,128)(2,1)} %get-tuple-element.237), channel_id=1, source_target_pairs={{0,1},{1,0},{2,3},{3,2},{4,5},{5,4},{6,7},{7,6},{8,9},{9,8},{10,11... | collective-permute-start | bytes 14155784 | tf_op jit(solution)/shard_map/ppermute | solution.py:103
  306.4 297.7 %all-reduce.5.cloned.1.call-start = ((), (), s32[]{:S(2)}) async-start(), calls=%async_computation.2 | async-start | bytes 2359296 | tf_op jit(solution)/shard_map/psum | solution.py:1294
  345.5 35.4 %collective-permute-start.36 = (bf16[4,1152,512]{2,1,0:T(8,128)(2,1)}, bf16[4,1152,512]{2,1,0:T(8,128)(2,1)}, u32[]{:S(2)}, u32[]{:S(2)}) collective-permute-start(bf16[4,1152,512]{2,1,0:T(8,128)(2,1)} %get-tuple-element.256), channel_id=1, source_target_pairs={{0,1},{1,0},{2,3},{3,2},{4,5},{5,4},{6,7},{7,6},{8,9},{9,8},{10,11... | collective-permute-start | bytes 14155784 | tf_op jit(solution)/shard_map/ppermute | solution.py:103
  345.8 35.1 %collective-permute-start.32 = (bf16[4,2,144,512]{3,2,1,0:T(8,128)(2,1)}, bf16[4,2,144,512]{3,2,1,0:T(8,128)(2,1)S(1)}, u32[]{:S(2)}, u32[]{:S(2)}) collective-permute-start(bf16[4,2,144,512]{3,2,1,0:T(8,128)(2,1)} %fusion.13), channel_id=1, source_target_pairs={{0,8},{8,0},{16,24},{24,16},{1,9},{9,1},{17,25},{25,17},{2,10},{10... | collective-permute-start | bytes 3538952 | tf_op jit(solution)/shard_map/ppermute | solution.py:108
  347.2 33.7 %collective-permute-start.33 = (bf16[4,2,144,512]{3,2,1,0:T(8,128)(2,1)}, bf16[4,2,144,512]{3,2,1,0:T(8,128)(2,1)S(1)}, u32[]{:S(2)}, u32[]{:S(2)}) collective-permute-start(bf16[4,2,144,512]{3,2,1,0:T(8,128)(2,1)} %fusion.14), channel_id=1, source_target_pairs={{0,16},{8,24},{16,0},{24,8},{1,17},{9,25},{17,1},{25,9},{2,18},{10... | collective-permute-start | bytes 3538952 | tf_op jit(solution)/shard_map/ppermute | solution.py:108
  384.9 58.4 %collective-permute-start.37 = (bf16[4,2,144,512]{3,2,1,0:T(8,128)(2,1)}, bf16[4,2,144,512]{3,2,1,0:T(8,128)(2,1)S(1)}, u32[]{:S(2)}, u32[]{:S(2)}) collective-permute-start(bf16[4,2,144,512]{3,2,1,0:T(8,128)(2,1)} %fusion.15), channel_id=1, source_target_pairs={{0,8},{8,0},{16,24},{24,16},{1,9},{9,1},{17,25},{25,17},{2,10},{10... | collective-permute-start | bytes 3538952 | tf_op jit(solution)/shard_map/ppermute | solution.py:108
  388.5 54.8 %collective-permute-start.38 = (bf16[4,2,144,512]{3,2,1,0:T(8,128)(2,1)}, bf16[4,2,144,512]{3,2,1,0:T(8,128)(2,1)S(1)}, u32[]{:S(2)}, u32[]{:S(2)}) collective-permute-start(bf16[4,2,144,512]{3,2,1,0:T(8,128)(2,1)} %fusion.16), channel_id=1, source_target_pairs={{0,16},{8,24},{16,0},{24,8},{1,17},{9,25},{17,1},{25,9},{2,18},{10... | collective-permute-start | bytes 3538952 | tf_op jit(solution)/shard_map/ppermute | solution.py:108
  392.3 45.3 %collective-permute-start.35 = (bf16[4,144,512]{2,1,0:T(8,128)(2,1)}, bf16[4,144,512]{2,1,0:T(8,128)(2,1)}, u32[]{:S(2)}, u32[]{:S(2)}) collective-permute-start(bf16[4,144,512]{2,1,0:T(8,128)(2,1)} %get-tuple-element.482), channel_id=1, source_target_pairs={{0,8},{8,0},{16,24},{24,16},{1,9},{9,1},{17,25},{25,17},{2,10},{10... | collective-permute-start | bytes 1769480 | tf_op jit(solution)/shard_map/ppermute | solution.py:108
  393.7 43.9 %collective-permute-start.34 = (bf16[4,144,512]{2,1,0:T(8,128)(2,1)}, bf16[4,144,512]{2,1,0:T(8,128)(2,1)}, u32[]{:S(2)}, u32[]{:S(2)}) collective-permute-start(bf16[4,144,512]{2,1,0:T(8,128)(2,1)} %get-tuple-element.483), channel_id=1, source_target_pairs={{0,16},{8,24},{16,0},{24,8},{1,17},{9,25},{17,1},{25,9},{2,18},{10... | collective-permute-start | bytes 1769480 | tf_op jit(solution)/shard_map/ppermute | solution.py:108
  480.8 40.9 %collective-permute-start.42 = (bf16[4,2,208,512]{3,2,1,0:T(8,128)(2,1)}, bf16[4,2,208,512]{3,2,1,0:T(8,128)(2,1)S(1)}, u32[]{:S(2)}, u32[]{:S(2)}) collective-permute-start(bf16[4,2,208,512]{3,2,1,0:T(8,128)(2,1)} %fusion), channel_id=1, source_target_pairs={{0,8},{8,0},{16,24},{24,16},{1,9},{9,1},{17,25},{25,17},{2,10},{10... | collective-permute-start | bytes 5111816 | tf_op jit(solution)/shard_map/ppermute | solution.py:108
  485.2 36.5 %collective-permute-start.43 = (bf16[4,2,192,512]{3,2,1,0:T(8,128)(2,1)}, bf16[4,2,192,512]{3,2,1,0:T(8,128)(2,1)}, u32[]{:S(2)}, u32[]{:S(2)}) collective-permute-start(bf16[4,2,192,512]{3,2,1,0:T(8,128)(2,1)} %fusion.11), channel_id=1, source_target_pairs={{0,16},{8,24},{16,0},{24,8},{1,17},{9,25},{17,1},{25,9},{2,18},{10... | collective-permute-start | bytes 4718600 | tf_op jit(solution)/shard_map/ppermute | solution.py:108
  486.4 42.6 %collective-permute-start.46 = (bf16[288,512]{1,0:T(8,128)(2,1)}, bf16[288,512]{1,0:T(8,128)(2,1)}, u32[]{:S(2)}, u32[]{:S(2)}) collective-permute-start(bf16[288,512]{1,0:T(8,128)(2,1)} %pad_maximum_fusion.9), channel_id=1, source_target_pairs={{0,2},{1,3},{2,4},{3,5},{4,6},{5,7},{6,0},{7,1},{8,10},{9,11},{10,... | collective-permute-start | bytes 884744 | tf_op jit(solution)/shard_map/ppermute | solution.py:93
  486.9 42.2 %collective-permute-start.47 = (bf16[288,512]{1,0:T(8,128)(2,1)}, bf16[288,512]{1,0:T(8,128)(2,1)}, u32[]{:S(2)}, u32[]{:S(2)}) collective-permute-start(bf16[288,512]{1,0:T(8,128)(2,1)} %pad_maximum_fusion.10), channel_id=1, source_target_pairs={{0,4},{1,5},{2,6},{3,7},{4,0},{5,1},{6,2},{7,3},{8,12},{9,13},{10,... | collective-permute-start | bytes 884744 | tf_op jit(solution)/shard_map/ppermute | solution.py:93
  488.6 40.5 %collective-permute-start.48 = (bf16[288,512]{1,0:T(8,128)(2,1)}, bf16[288,512]{1,0:T(8,128)(2,1)}, u32[]{:S(2)}, u32[]{:S(2)}) collective-permute-start(bf16[288,512]{1,0:T(8,128)(2,1)} %pad_maximum_fusion.11), channel_id=1, source_target_pairs={{0,6},{1,7},{2,0},{3,1},{4,2},{5,3},{6,4},{7,5},{8,14},{9,15},{10,... | collective-permute-start | bytes 884744 | tf_op jit(solution)/shard_map/ppermute | solution.py:93
  576.8 39.7 %collective-permute-start.52 = (bf16[400,512]{1,0:T(8,128)(2,1)}, bf16[400,512]{1,0:T(8,128)(2,1)}, u32[]{:S(2)}, u32[]{:S(2)}) collective-permute-start(bf16[400,512]{1,0:T(8,128)(2,1)} %pad_maximum_fusion.6), channel_id=1, source_target_pairs={{0,2},{1,3},{2,4},{3,5},{4,6},{5,7},{6,0},{7,1},{8,10},{9,11},{10,... | collective-permute-start | bytes 1228808 | tf_op jit(solution)/shard_map/ppermute | solution.py:93
  584.1 32.5 %collective-permute-start.53 = (bf16[400,512]{1,0:T(8,128)(2,1)}, bf16[400,512]{1,0:T(8,128)(2,1)}, u32[]{:S(2)}, u32[]{:S(2)}) collective-permute-start(bf16[400,512]{1,0:T(8,128)(2,1)} %pad_maximum_fusion.7), channel_id=1, source_target_pairs={{0,4},{1,5},{2,6},{3,7},{4,0},{5,1},{6,2},{7,3},{8,12},{9,13},{10,... | collective-permute-start | bytes 1228808 | tf_op jit(solution)/shard_map/ppermute | solution.py:93
  584.1 32.5 %collective-permute-start.54 = (bf16[400,512]{1,0:T(8,128)(2,1)}, bf16[400,512]{1,0:T(8,128)(2,1)}, u32[]{:S(2)}, u32[]{:S(2)}) collective-permute-start(bf16[400,512]{1,0:T(8,128)(2,1)} %pad_maximum_fusion.8), channel_id=1, source_target_pairs={{0,6},{1,7},{2,0},{3,1},{4,2},{5,3},{6,4},{7,5},{8,14},{9,15},{10,... | collective-permute-start | bytes 1228808 | tf_op jit(solution)/shard_map/ppermute | solution.py:93
  639.7 31.1 %collective-permute-start.65 = (bf16[2,400,512]{2,1,0:T(8,128)(2,1)S(1)}, bf16[2,400,512]{2,1,0:T(8,128)(2,1)S(1)}, u32[]{:S(2)}, u32[]{:S(2)}) collective-permute-start(bf16[2,400,512]{2,1,0:T(8,128)(2,1)S(1)} %reverse_select_fusion.3), channel_id=1, source_target_pairs={{0,16},{8,24},{16,0},{24,8},{1,17},{9,25},{17,1},{25,9},{2,18},{10... | collective-permute-start | bytes 2457608 | tf_op jit(solution)/shard_map/ppermute | solution.py:108
  (94 other events, 1159.9 us)
Sparse Core Ops, SparseCore 0:
  44.4 40.0 all-gather.4
  86.7 49.3 all-gather.6
  306.6 84.1 reduce-scatter.1
  539.4 64.7 all-reduce.4

commit v5 on v4

--- a/solution.py
+++ b/solution.py
@@ -1062,13 +1062,13 @@
 
 def input_grad_call(dqkv, w_in, x, dresid, gain, rows, n, after=()):
     tokens, width = x.shape
-    tile = pl.BlockSpec((WIDE_TILE, width), lambda i: (i, 0))
+    tile = pl.BlockSpec((TILE, width), lambda i: (i, 0))
     return kernel_call(
         functools.partial(input_grad_kernel, rows, n),
         [dqkv, w_in, x, dresid, gain],
-        grid=(tokens // WIDE_TILE,),
+        grid=(tokens // TILE,),
         in_specs=[
-            pl.BlockSpec((WIDE_TILE, n * BLK), lambda i: (i, 0)),
+            pl.BlockSpec((TILE, n * BLK), lambda i: (i, 0)),
             whole((w_in.shape[0], n * rows, BLK)),
             tile,
             tile,

time: 718 us -> 713 us (level)
  no operation moved by 1% of the time
where the time goes in v5:
time: 713 us; the launch traced here: 708 us
  Pallas kernels  385 us (54%)
  waiting for transfers between devices  120 us (17%)
  other arithmetic  80 us (11%)
  starting transfers between devices  68.2 us (10%)
  local copies, waits for them, and re-layouts  35.3 us (5%)
  between operations  19.2 us (3%)
    pallas_call x26, Pallas kernels, kernel_call(): pl.pallas_call(kernel, grid_spec=pltpu.PrefetchScalarGridSpec(num_scalar_...  385 us
    ppermute x32, waiting for transfers between devices, swap_replica(): return lax.ppermute(x, 'replica', [(i, i ^ bit) for i in range(size)])  62.4 us
    ppermute x32, starting transfers between devices, swap_replica(): return lax.ppermute(x, 'replica', [(i, i ^ bit) for i in range(size)])  34.5 us
    convert_element_type x10, other arithmetic, halve(): away = self.part_sum([take(t, 1 - own) for t in self.terms[p]]).astype(bf16)  29.2 us
    ppermute x12, starting transfers between devices, shift_core_pairs(): lax.ppermute(x, 'fsdp', [(i, (i + 2 * k) % size) for i in range(size)])  23.5 us
    unnamed x116, local copies, waits for them, and re-layouts  20.5 us
    ppermute x12, waiting for transfers between devices, shift_core_pairs(): lax.ppermute(x, 'fsdp', [(i, (i + 2 * k) % size) for i in range(size)])  18.2 us
    psum x1, waiting for transfers between devices, per_device(): sum0 = lax.psum(part0, 'replica')  16.8 us
  transfers between devices with their start and end apart: 73, of which 20 were waited for; matrix products, arithmetic and copies ran while one was open for 11% of the time, Pallas kernels for 49%

profile of v5, /device:TPU:0, one launch (start us, length us, event | category | flops | bytes accessed | tf_op | source)
XLA Modules:
  0.0 708.0 jit_solution(7192059985636618765)
XLA Ops:
  13.1 4.6 collective-permute-start.3
  22.2 4.4 pack.5
  26.6 14.3 %collective-permute-done.2.refs_1_ = bf16[256,512]{1,0:T(8,128)(2,1)S(1)} collective-permute-done((bf16[256,512]{1,0:T(8,128)(2,1)}, bf16[256,512]{1,0:T(8,128)(2,1)S(1)}, u32[]{:S(2)}, u32[]{:S(2)}) %collective-permute-start.2) | collective-permute-done | bytes 262176 | tf_op jit(solution)/shard_map/ppermute | solution.py:93
  49.5 5.9 collective-permute-done.4
  58.9 15.9 %collective-permute-done.7.refs_4_ = bf16[2,3,128,512]{3,2,1,0:T(8,128)(2,1)} collective-permute-done((bf16[2,3,128,512]{3,2,1,0:T(8,128)(2,1)S(1)}, bf16[2,3,128,512]{3,2,1,0:T(8,128)(2,1)}, u32[]{:S(2)}, u32[]{:S(2)}) %collective-permute-start.7) | collective-permute-done | bytes 786464 | tf_op jit(solution)/shard_map/ppermute | solution.py:108
  75.8 8.7 %all-gather.5.cloned.1.call-done = bf16[1728,512]{1,0:T(8,128)(2,1)} async-done(((bf16[432,512]{1,0:T(8,128)(2,1)}), bf16[1728,512]{1,0:T(8,128)(2,1)}) %all-gather.5.cloned.1.call-update) | async-done | bytes 1769488 | tf_op jit(solution)/shard_map/all_gather | solution.py:177
  91.1 7.7 %assemble.3.w_ref = bf16[8,1024,512]{2,1,0:T(8,128)(2,1)} custom-call(s32[3]{0:T(128)} %pad_add_fusion.idx_ref, bf16[1024,512]{1,0:T(8,128)(2,1)} %get-tuple-element.181.refs_0_, bf16[2,3,128,512]{3,2,1,0:T(8,128)(2,1)} %copy-done.13, bf16[2,3,128,512]{3,2,1,0:T(8,128)(2,1)} %collective-permute-done.6.refs_2_, bf16[2,3,128,512]{3,2,1,0:T(8,128)(2,1)} %copy-done.14, ...), custom_call_target="tpu_custom_call" | custom-call | bytes 16 | tf_op jit(solution)/shard_map/assemble/pallas_call | solution.py:70
  100.5 16.4 %qkv.1 = (bf16[1024,2560]{1,0:T(8,128)(2,1)}, bf16[1024,1536]{1,0:T(8,128)(2,1)}) custom-call(bf16[1024,1536]{1,0:T(8,128)(2,1)} %bitcast.357, f32[1,1536]{1,0:T(1,128)} %reshape.788.gain_ref, bf16[8,1024,512]{2,1,0:T(8,128)(2,1)} %assemble.3.w_ref), custom_call_target="tpu_custom_call" | custom-call | flops 8 | bytes 14 | tf_op jit(solution)/shard_map/qkv/pallas_call | solution.py:70
  122.4 37.3 %attention.1 = (bf16[2,24,512,512]{3,2,1,0:T(8,128)(2,1)}, bf16[1024,1536]{1,0:T(8,128)(2,1)}) custom-call(s32[2]{0:T(128)} %bitcast.412, bf16[1024,2560]{1,0:T(8,128)(2,1)} %get-tuple-element.258.q_ref.k_ref.v_ref, bf16[1024,2560]{1,0:T(8,128)(2,1)} %get-tuple-element.258.q_ref.k_ref.v_ref, bf16[1024,2560]{1,0:T(8,128)(2,1)} %get-tuple-element.258.q_ref.k_ref.v_ref), custom_call_target="tpu_custom_call" | custom-call | flops 12 | bytes 25 | tf_op jit(solution)/shard_map/attention/pallas_call | solution.py:70
  168.7 11.5 %assemble.4.w_ref.up_a_ref.up_b_ref.down_ref = bf16[8,1728,512]{2,1,0:T(8,128)(2,1)} custom-call(s32[3]{0:T(128)} %pad_add_fusion.idx_ref, bf16[1728,512]{1,0:T(8,128)(2,1)} %get-tuple-element.183.refs_4_.refs_0_, bf16[2,3,224,512]{3,2,1,0:T(8,128)(2,1)} %copy-done.11, bf16[2,3,224,512]{3,2,1,0:T(8,128)(2,1)} %collective-permute-done.14.refs_2_, ...), custom_call_target="tpu_custom_call" | custom-call | bytes 28 | tf_op jit(solution)/shard_map/assemble/pallas_call | solution.py:70
  180.2 11.5 %resid.1 = (f32[1024,1536]{1,0:T(8,128)}, bf16[1024,1536]{1,0:T(8,128)(2,1)}, f32[8,1024]{1,0:T(8,128)}) custom-call(bf16[1024,1536]{1,0:T(8,128)(2,1)} %get-tuple-element.203.mix_ref.left_ref, bf16[8,1728,512]{2,1,0:T(8,128)(2,1)} %assemble.4.w_ref.up_a_ref.up_b_ref.down_ref, bf16[1024,1536]{1,0:T(8,128)(2,1)} %bitcast.358, f32[1,1536]{1,0:T(1,128)} %reshape.789.gain_ref, ...), custom_call_target="tpu_custom_call" | custom-call | flops 4 | bytes 23 | tf_op jit(solution)/shard_map/resid/pallas_call | solution.py:70
  199.9 12.1 %dispatch.1 = (bf16[3,2,320,1536]{3,2,1,0:T(8,128)(2,1)}, bf16[3,2,320,1536]{3,2,1,0:T(8,128)(2,1)}, f32[3,2,320,128]{3,2,1,0:T(8,128)}) custom-call(s32[2,8,512]{2,1,0:T(8,128)} %stack.96.slot_ref, f32[8,1024]{1,0:T(8,128)} %get-tuple-element.219.prob_ref, bf16[1024,1536]{1,0:T(8,128)(2,1)} %get-tuple-element.220.n2_ref, bf16[1024,1536]{1,0:T(8,128)(2,1)} %bitcast.381), custom_call_target="tpu_custom_call" | custom-call | flops 6 | bytes 31 | tf_op jit(solution)/shard_map/dispatch/pallas_call | solution.py:70
  212.0 32.9 %expert.3 = (bf16[2,320,1536]{2,1,0:T(8,128)(2,1)}, bf16[2,320,1536]{2,1,0:T(8,128)(2,1)}, f32[2,8,512]{2,1,0:T(8,128)}, bf16[4,1152,512]{2,1,0:T(8,128)(2,1)}, bf16[4,1152,512]{2,1,0:T(8,128)(2,1)}) custom-call(s32[1]{0:T(128)} %bitcast.8.idx_ref, bf16[3,2,320,1536]{3,2,1,0:T(8,128)(2,1)} %get-tuple-element.221.buf_ref, ...), custom_call_target="tpu_custom_call" | custom-call | flops 18 | bytes 62 | tf_op jit(solution)/shard_map/expert/pallas_call | solution.py:70
  252.7 14.6 %assemble.5.up_a_ref.up_b_ref.down_ref = bf16[8,2304,512]{2,1,0:T(8,128)(2,1)} custom-call(s32[3]{0:T(128)} %pad_add_fusion.idx_ref, bf16[2304,512]{1,0:T(8,128)(2,1)} %get-tuple-element.184.refs_0_, bf16[2,3,288,512]{3,2,1,0:T(8,128)(2,1)} %constant_dynamic-update-slice_fusion.8.refs_1_, bf16[2,3,288,512]{3,2,1,0:T(8,128)(2,1)} %collective-permute-done.23.refs_2_, ...), custom_call_target="tpu_custom_call" | custom-call | bytes 37 | tf_op jit(solution)/shard_map/assemble/pallas_call | solution.py:70
  267.3 5.9 add_convert_fusion
  273.2 32.6 %expert.4 = (bf16[2,320,1536]{2,1,0:T(8,128)(2,1)}, bf16[2,320,1536]{2,1,0:T(8,128)(2,1)}, f32[2,8,512]{2,1,0:T(8,128)}, bf16[4,1152,512]{2,1,0:T(8,128)(2,1)}, bf16[4,1152,512]{2,1,0:T(8,128)(2,1)}) custom-call(s32[1]{0:T(128)} %bitcast.8.idx_ref, bf16[3,2,320,1536]{3,2,1,0:T(8,128)(2,1)} %get-tuple-element.221.buf_ref, ...), custom_call_target="tpu_custom_call" | custom-call | flops 18 | bytes 62 | tf_op jit(solution)/shard_map/expert/pallas_call | solution.py:70
  306.3 33.1 %expert.5 = (bf16[2,320,1536]{2,1,0:T(8,128)(2,1)}, bf16[2,320,1536]{2,1,0:T(8,128)(2,1)}, f32[2,8,512]{2,1,0:T(8,128)}, bf16[4,1152,512]{2,1,0:T(8,128)(2,1)}, bf16[4,1152,512]{2,1,0:T(8,128)(2,1)}) custom-call(s32[1]{0:T(128)} %bitcast.8.idx_ref, bf16[3,2,320,1536]{3,2,1,0:T(8,128)(2,1)} %get-tuple-element.221.buf_ref, ...), custom_call_target="tpu_custom_call" | custom-call | flops 18 | bytes 62 | tf_op jit(solution)/shard_map/expert/pallas_call | solution.py:70
  349.6 19.9 %middle.1 = (f32[1024,1536]{1,0:T(8,128)}, bf16[1024,1536]{1,0:T(8,128)(2,1)}, bf16[1024,1536]{1,0:T(8,128)(2,1)}, f32[8,1536]{1,0:T(8,128)}) custom-call(s32[1024,8]{1,0:T(8,128)} %bitcast.383, bf16[2,320,1536]{2,1,0:T(8,128)(2,1)} %get-tuple-element.243.d0_ref, bf16[2,320,1536]{2,1,0:T(8,128)(2,1)} %get-tuple-element.244.d1_ref, ...), custom_call_target="tpu_custom_call" | custom-call | flops 7 | bytes 31 | tf_op jit(solution)/shard_map/middle/pallas_call | solution.py:70
  369.5 9.8 %out_grad.1 = (bf16[4,1600,512]{2,1,0:T(8,128)(2,1)}, bf16[4,1600,512]{2,1,0:T(8,128)(2,1)}) custom-call(s32[1]{0:T(128)} %bitcast.8.idx_ref, bf16[1024,1536]{1,0:T(8,128)(2,1)} %get-tuple-element.203.mix_ref.left_ref, bf16[1024,1536]{1,0:T(8,128)(2,1)} %get-tuple-element.249.right_ref), custom_call_target="tpu_custom_call" | custom-call | flops 4 | bytes 11 | tf_op jit(solution)/shard_map/out_grad/pallas_call | solution.py:70
  395.0 42.3 %attention_back.1 = (bf16[1024,1536]{1,0:T(8,128)(2,1)}, bf16[1024,512]{1,0:T(8,128)(2,1)}, bf16[1024,512]{1,0:T(8,128)(2,1)}) custom-call(bf16[1024,2560]{1,0:T(8,128)(2,1)} %get-tuple-element.258.q_ref.k_ref.v_ref, bf16[1024,2560]{1,0:T(8,128)(2,1)} %get-tuple-element.258.q_ref.k_ref.v_ref, bf16[1024,2560]{1,0:T(8,128)(2,1)} %get-tuple-element.258.q_ref.k_ref.v_ref, ...), custom_call_target="tpu_custom_call" | custom-call | flops 25 | bytes 25 | tf_op jit(solution)/shard_map/attention_back/pallas_call | solution.py:70
  451.4 13.4 %in_grad.1 = (bf16[4,1600,512]{2,1,0:T(8,128)(2,1)}, bf16[4,1600,512]{2,1,0:T(8,128)(2,1)}) custom-call(s32[1]{0:T(128)} %bitcast.8.idx_ref, bf16[1024,1536]{1,0:T(8,128)(2,1)} %get-tuple-element.267.left_ref, bf16[1024,2560]{1,0:T(8,128)(2,1)} %copy-done, ...), custom_call_target="tpu_custom_call", output_to_operand_aliasing={{0}: (3, {}), {1}: (4, {})} | custom-call | flops 8 | bytes 14 | tf_op jit(solution)/shard_map/in_grad/pallas_call | solution.py:70
  466.5 10.6 %combine.1 = bf16[1024,1536]{1,0:T(8,128)(2,1)} custom-call(s32[1024,8]{1,0:T(8,128)} %bitcast.384, f32[1024,1536]{1,0:T(8,128)} %get-tuple-element.215.resid_ref, bf16[2,320,1536]{2,1,0:T(8,128)(2,1)} %get-tuple-element.226.y0_ref, bf16[2,320,1536]{2,1,0:T(8,128)(2,1)} %get-tuple-element.238.y1_ref, bf16[2,320,1536]{2,1,0:T(8,128)(2,1)} %get-tuple-element.240.y2_ref), custom_call_target="tpu_custom_call" | custom-call | flops 3 | bytes 18 | tf_op jit(solution)/shard_map/combine/pallas_call | solution.py:70
  490.6 15.2 %input_grad.1 = bf16[1024,1536]{1,0:T(8,128)(2,1)} custom-call(bf16[1024,2560]{1,0:T(8,128)(2,1)} %copy-done, bf16[8,1024,512]{2,1,0:T(8,128)(2,1)} %assemble.3.w_ref, bf16[1024,1536]{1,0:T(8,128)(2,1)} %bitcast.359, f32[1024,1536]{1,0:T(8,128)} %get-tuple-element.279.dresid_ref, f32[1,1536]{1,0:T(1,128)} %reshape.788.gain_ref), custom_call_target="tpu_custom_call" | custom-call | flops 8 | bytes 26 | tf_op jit(solution)/shard_map/input_grad/pallas_call | solution.py:70
  505.9 15.6 %collective-permute-done.43 = bf16[4,2,192,512]{3,2,1,0:T(8,128)(2,1)} collective-permute-done((bf16[4,2,192,512]{3,2,1,0:T(8,128)(2,1)}, bf16[4,2,192,512]{3,2,1,0:T(8,128)(2,1)}, u32[]{:S(2)}, u32[]{:S(2)}) %collective-permute-start.43) | collective-permute-done | bytes 1572896 | tf_op jit(solution)/shard_map/ppermute | solution.py:108
  539.1 8.8 %collective-permute-done.45 = bf16[4,192,512]{2,1,0:T(8,128)(2,1)} collective-permute-done((bf16[4,192,512]{2,1,0:T(8,128)(2,1)}, bf16[4,192,512]{2,1,0:T(8,128)(2,1)}, u32[]{:S(2)}, u32[]{:S(2)}) %collective-permute-start.45) | collective-permute-done | bytes 786464 | tf_op jit(solution)/shard_map/ppermute | solution.py:108
  566.1 8.5 %collective-permute-done.55 = bf16[288,512]{1,0:T(8,128)(2,1)S(1)} collective-permute-done((bf16[288,512]{1,0:T(8,128)(2,1)S(1)}, bf16[288,512]{1,0:T(8,128)(2,1)S(1)}, u32[]{:S(2)}, u32[]{:S(2)}) %collective-permute-start.55) | collective-permute-done | bytes 294944 | tf_op jit(solution)/shard_map/ppermute | solution.py:108
  576.8 6.8 collective-permute-start.52
  587.3 16.8 %all-reduce.5.cloned.1.call-done.g0_ref = bf16[1152,512]{1,0:T(8,128)(2,1)} async-done(((bf16[1152,512]{1,0:T(8,128)(2,1)}), bf16[1152,512]{1,0:T(8,128)(2,1)}) %all-reduce.5.cloned.1.call-update) | async-done | bytes 1179664 | tf_op jit(solution)/shard_map/psum | solution.py:1294
  640.5 12.0 %down_adam.1 = (f32[3,128,1536]{2,1,0:T(8,128)}, f32[3,128,1536]{2,1,0:T(8,128)}, f32[3,128,1536]{2,1,0:T(8,128)}, f32[3,128,1536]{2,1,0:T(8,128)}) custom-call(f32[8,128]{1,0:T(8,128)} %get-tuple-element.319.clip_ref, bf16[1152,512]{1,0:T(8,128)(2,1)} %all-reduce.5.cloned.1.call-done.g0_ref, bf16[1152,512]{1,0:T(8,128)(2,1)} %bitcast.379, ...), custom_call_target="tpu_custom_call" | custom-call | bytes 17 | tf_op jit(solution)/shard_map/down_adam/pallas_call | solution.py:70
  652.5 18.0 %up_adam.1 = (f32[3,192,2048]{2,1,0:T(8,128)}, f32[3,192,2048]{2,1,0:T(8,128)}, f32[3,192,2048]{2,1,0:T(8,128)}, f32[3,192,2048]{2,1,0:T(8,128)}) custom-call(f32[8,128]{1,0:T(8,128)} %get-tuple-element.319.clip_ref, bf16[1152,512]{1,0:T(8,128)(2,1)} %all-reduce.5.cloned.1.call-done.g0_ref, bf16[1152,512]{1,0:T(8,128)(2,1)} %bitcast.380, ...), custom_call_target="tpu_custom_call" | custom-call | bytes 35 | tf_op jit(solution)/shard_map/up_adam/pallas_call | solution.py:70
  673.9 6.5 out_adam.1
  683.1 9.5 %in_adam.1 = (f32[192,2560]{1,0:T(8,128)}, f32[192,2560]{1,0:T(8,128)}, f32[192,2560]{1,0:T(8,128)}, f32[192,2560]{1,0:T(8,128)}) custom-call(f32[8,128]{1,0:T(8,128)} %get-tuple-element.319.clip_ref, bf16[1600,512]{1,0:T(8,128)(2,1)} %bitcast.371, f32[192,2560]{1,0:T(8,128)} %master_ref.7, f32[192,2560]{1,0:T(8,128)} %first_ref.7, f32[192,2560]{1,0:T(8,128)} %second_ref.7), custom_call_target="tpu_custom_call" | custom-call | bytes 14 | tf_op jit(solution)/shard_map/in_adam/pallas_call | solution.py:70
  (380 shorter events, 205.6 us)
Async XLA Ops:
  7.2 77.3 %all-gather.5.cloned.1.call-start = ((), (), s32[]{:S(2)}) async-start(), calls=%async_computation.3 | async-start | bytes 2211840 | tf_op jit(solution)/shard_map/all_gather | solution.py:177
  44.3 117.1 %all-gather.7.cloned.1.call-start = ((), (), s32[]{:S(2)}) async-start(), calls=%async_computation.4 | async-start | bytes 2949120 | tf_op jit(solution)/shard_map/all_gather | solution.py:177
  84.6 310.4 %reduce-scatter.2.cloned.1.call-start = ((), (), s32[]{:S(2)}) async-start(), calls=%async_computation.1 | async-start | bytes 5898240 | tf_op jit(solution)/shard_map/reduce_scatter | solution.py:1254
  87.5 30.6 %collective-permute-start.9 = (bf16[1,3,208,512]{3,2,1,0:T(8,128)(2,1)}, bf16[1,3,208,512]{3,2,1,0:T(8,128)(2,1)}, u32[]{:S(2)}, u32[]{:S(2)}) collective-permute-start(bf16[1,3,208,512]{3,2,1,0:T(8,128)(2,1)} %get-tuple-element.195), channel_id=1, source_target_pairs={{0,16},{8,24},{16,0},{24,8},{1,17},{9,25},{17,1},{25,9},{2,18},{10... | collective-permute-start | bytes 1916936 | tf_op jit(solution)/shard_map/ppermute | solution.py:108
  91.0 68.8 %collective-permute-start.16 = (bf16[1728,512]{1,0:T(8,128)(2,1)S(1)}, bf16[1728,512]{1,0:T(8,128)(2,1)}, u32[]{:S(2)}, u32[]{:S(2)}) collective-permute-start(bf16[1728,512]{1,0:T(8,128)(2,1)S(1)} %copy-done.5), channel_id=1, source_target_pairs={{0,1},{1,0},{2,3},{3,2},{4,5},{5,4},{6,7},{7,6},{8,9},{9,8},{10,11... | collective-permute-start | bytes 5308424 | tf_op jit(solution)/shard_map/ppermute | solution.py:103
  119.3 40.5 %collective-permute-start.17 = (bf16[2,3,224,512]{3,2,1,0:T(8,128)(2,1)S(1)}, bf16[2,3,224,512]{3,2,1,0:T(8,128)(2,1)S(1)}, u32[]{:S(2)}, u32[]{:S(2)}) collective-permute-start(bf16[2,3,224,512]{3,2,1,0:T(8,128)(2,1)S(1)} %constant_dynamic-update-slice_fusion.4.refs_1_), channel_id=1, source_target_pairs={{0,1},{1,0},{2,3},{3,2},{4,5},{5,4},{6,7},{7,6},{8,9},{9,8},{10,11... | collective-permute-start | bytes 4128776 | tf_op jit(solution)/shard_map/ppermute | solution.py:103
  120.0 39.9 %collective-permute-start.14 = (bf16[2,3,224,512]{3,2,1,0:T(8,128)(2,1)S(1)}, bf16[2,3,224,512]{3,2,1,0:T(8,128)(2,1)}, u32[]{:S(2)}, u32[]{:S(2)}) collective-permute-start(bf16[2,3,224,512]{3,2,1,0:T(8,128)(2,1)S(1)} %constant_dynamic-update-slice_fusion.4.refs_1_), channel_id=1, source_target_pairs={{0,16},{8,24},{16,0},{24,8},{1,17},{9,25},{17,1},{25,9},{2,18},{10... | collective-permute-start | bytes 4128776 | tf_op jit(solution)/shard_map/ppermute | solution.py:108
  121.7 38.1 %collective-permute-start.18 = (bf16[2,3,208,512]{3,2,1,0:T(8,128)(2,1)S(1)}, bf16[2,3,208,512]{3,2,1,0:T(8,128)(2,1)}, u32[]{:S(2)}, u32[]{:S(2)}) collective-permute-start(bf16[2,3,208,512]{3,2,1,0:T(8,128)(2,1)S(1)} %constant_dynamic-update-slice_fusion.6.refs_3_), channel_id=1, source_target_pairs={{0,1},{1,0},{2,3},{3,2},{4,5},{5,4},{6,7},{7,6},{8,9},{9,8},{10,11... | collective-permute-start | bytes 3833864 | tf_op jit(solution)/shard_map/ppermute | solution.py:103
  121.8 38.0 %collective-permute-start.15 = (bf16[2,3,208,512]{3,2,1,0:T(8,128)(2,1)S(1)}, bf16[2,3,208,512]{3,2,1,0:T(8,128)(2,1)}, u32[]{:S(2)}, u32[]{:S(2)}) collective-permute-start(bf16[2,3,208,512]{3,2,1,0:T(8,128)(2,1)S(1)} %constant_dynamic-update-slice_fusion.6.refs_3_), channel_id=1, source_target_pairs={{0,8},{8,0},{16,24},{24,16},{1,9},{9,1},{17,25},{25,17},{2,10},{10... | collective-permute-start | bytes 3833864 | tf_op jit(solution)/shard_map/ppermute | solution.py:108
  167.3 77.6 %collective-permute-start.25 = (bf16[2304,512]{1,0:T(8,128)(2,1)S(1)}, bf16[2304,512]{1,0:T(8,128)(2,1)}, u32[]{:S(2)}, u32[]{:S(2)}) collective-permute-start(bf16[2304,512]{1,0:T(8,128)(2,1)S(1)} %copy-done.6), channel_id=1, source_target_pairs={{0,1},{1,0},{2,3},{3,2},{4,5},{5,4},{6,7},{7,6},{8,9},{9,8},{10,11... | collective-permute-start | bytes 7077896 | tf_op jit(solution)/shard_map/ppermute | solution.py:103
  196.3 48.6 %collective-permute-start.27 = (bf16[2,3,288,512]{3,2,1,0:T(8,128)(2,1)}, bf16[2,3,288,512]{3,2,1,0:T(8,128)(2,1)}, u32[]{:S(2)}, u32[]{:S(2)}) collective-permute-start(bf16[2,3,288,512]{3,2,1,0:T(8,128)(2,1)} %constant_dynamic-update-slice_fusion.10.refs_3_), channel_id=1, source_target_pairs={{0,1},{1,0},{2,3},{3,2},{4,5},{5,4},{6,7},{7,6},{8,9},{9,8},{10,11... | collective-permute-start | bytes 5308424 | tf_op jit(solution)/shard_map/ppermute | solution.py:103
  196.8 48.1 %collective-permute-start.24 = (bf16[2,3,288,512]{3,2,1,0:T(8,128)(2,1)}, bf16[2,3,288,512]{3,2,1,0:T(8,128)(2,1)}, u32[]{:S(2)}, u32[]{:S(2)}) collective-permute-start(bf16[2,3,288,512]{3,2,1,0:T(8,128)(2,1)} %constant_dynamic-update-slice_fusion.10.refs_3_), channel_id=1, source_target_pairs={{0,8},{8,0},{16,24},{24,16},{1,9},{9,1},{17,25},{25,17},{2,10},{10... | collective-permute-start | bytes 5308424 | tf_op jit(solution)/shard_map/ppermute | solution.py:108
  198.4 46.6 %collective-permute-start.26 = (bf16[2,3,288,512]{3,2,1,0:T(8,128)(2,1)}, bf16[2,3,288,512]{3,2,1,0:T(8,128)(2,1)}, u32[]{:S(2)}, u32[]{:S(2)}) collective-permute-start(bf16[2,3,288,512]{3,2,1,0:T(8,128)(2,1)} %constant_dynamic-update-slice_fusion.8.refs_1_), channel_id=1, source_target_pairs={{0,1},{1,0},{2,3},{3,2},{4,5},{5,4},{6,7},{7,6},{8,9},{9,8},{10,11... | collective-permute-start | bytes 5308424 | tf_op jit(solution)/shard_map/ppermute | solution.py:103
  198.4 46.6 %collective-permute-start.23 = (bf16[2,3,288,512]{3,2,1,0:T(8,128)(2,1)}, bf16[2,3,288,512]{3,2,1,0:T(8,128)(2,1)}, u32[]{:S(2)}, u32[]{:S(2)}) collective-permute-start(bf16[2,3,288,512]{3,2,1,0:T(8,128)(2,1)} %constant_dynamic-update-slice_fusion.8.refs_1_), channel_id=1, source_target_pairs={{0,16},{8,24},{16,0},{24,8},{1,17},{9,25},{17,1},{25,9},{2,18},{10... | collective-permute-start | bytes 5308424 | tf_op jit(solution)/shard_map/ppermute | solution.py:108
  305.8 33.6 %collective-permute-start.31 = (bf16[4,1152,512]{2,1,0:T(8,128)(2,1)}, bf16[4,1152,512]{2,1,0:T(8,128)(2,1)}, u32[]{:S(2)}, u32[]{:S(2)}) collective-permute-start(bf16[4,1152,512]{2,1,0:T(8,128)(2,1)} %get-tuple-element.237), channel_id=1, source_target_pairs={{0,1},{1,0},{2,3},{3,2},{4,5},{5,4},{6,7},{7,6},{8,9},{9,8},{10,11... | collective-permute-start | bytes 14155784 | tf_op jit(solution)/shard_map/ppermute | solution.py:103
  306.2 297.9 %all-reduce.5.cloned.1.call-start = ((), (), s32[]{:S(2)}) async-start(), calls=%async_computation.2 | async-start | bytes 2359296 | tf_op jit(solution)/shard_map/psum | solution.py:1294
  345.5 35.4 %collective-permute-start.36 = (bf16[4,1152,512]{2,1,0:T(8,128)(2,1)}, bf16[4,1152,512]{2,1,0:T(8,128)(2,1)}, u32[]{:S(2)}, u32[]{:S(2)}) collective-permute-start(bf16[4,1152,512]{2,1,0:T(8,128)(2,1)} %get-tuple-element.256), channel_id=1, source_target_pairs={{0,1},{1,0},{2,3},{3,2},{4,5},{5,4},{6,7},{7,6},{8,9},{9,8},{10,11... | collective-permute-start | bytes 14155784 | tf_op jit(solution)/shard_map/ppermute | solution.py:103
  345.7 35.1 %collective-permute-start.32 = (bf16[4,2,144,512]{3,2,1,0:T(8,128)(2,1)}, bf16[4,2,144,512]{3,2,1,0:T(8,128)(2,1)S(1)}, u32[]{:S(2)}, u32[]{:S(2)}) collective-permute-start(bf16[4,2,144,512]{3,2,1,0:T(8,128)(2,1)} %fusion.13), channel_id=1, source_target_pairs={{0,8},{8,0},{16,24},{24,16},{1,9},{9,1},{17,25},{25,17},{2,10},{10... | collective-permute-start | bytes 3538952 | tf_op jit(solution)/shard_map/ppermute | solution.py:108
  347.1 33.7 %collective-permute-start.33 = (bf16[4,2,144,512]{3,2,1,0:T(8,128)(2,1)}, bf16[4,2,144,512]{3,2,1,0:T(8,128)(2,1)S(1)}, u32[]{:S(2)}, u32[]{:S(2)}) collective-permute-start(bf16[4,2,144,512]{3,2,1,0:T(8,128)(2,1)} %fusion.14), channel_id=1, source_target_pairs={{0,16},{8,24},{16,0},{24,8},{1,17},{9,25},{17,1},{25,9},{2,18},{10... | collective-permute-start | bytes 3538952 | tf_op jit(solution)/shard_map/ppermute | solution.py:108
  384.9 58.3 %collective-permute-start.37 = (bf16[4,2,144,512]{3,2,1,0:T(8,128)(2,1)}, bf16[4,2,144,512]{3,2,1,0:T(8,128)(2,1)S(1)}, u32[]{:S(2)}, u32[]{:S(2)}) collective-permute-start(bf16[4,2,144,512]{3,2,1,0:T(8,128)(2,1)} %fusion.15), channel_id=1, source_target_pairs={{0,8},{8,0},{16,24},{24,16},{1,9},{9,1},{17,25},{25,17},{2,10},{10... | collective-permute-start | bytes 3538952 | tf_op jit(solution)/shard_map/ppermute | solution.py:108
  388.5 54.6 %collective-permute-start.38 = (bf16[4,2,144,512]{3,2,1,0:T(8,128)(2,1)}, bf16[4,2,144,512]{3,2,1,0:T(8,128)(2,1)S(1)}, u32[]{:S(2)}, u32[]{:S(2)}) collective-permute-start(bf16[4,2,144,512]{3,2,1,0:T(8,128)(2,1)} %fusion.16), channel_id=1, source_target_pairs={{0,16},{8,24},{16,0},{24,8},{1,17},{9,25},{17,1},{25,9},{2,18},{10... | collective-permute-start | bytes 3538952 | tf_op jit(solution)/shard_map/ppermute | solution.py:108
  392.2 45.1 %collective-permute-start.35 = (bf16[4,144,512]{2,1,0:T(8,128)(2,1)}, bf16[4,144,512]{2,1,0:T(8,128)(2,1)}, u32[]{:S(2)}, u32[]{:S(2)}) collective-permute-start(bf16[4,144,512]{2,1,0:T(8,128)(2,1)} %get-tuple-element.482), channel_id=1, source_target_pairs={{0,8},{8,0},{16,24},{24,16},{1,9},{9,1},{17,25},{25,17},{2,10},{10... | collective-permute-start | bytes 1769480 | tf_op jit(solution)/shard_map/ppermute | solution.py:108
  393.7 43.7 %collective-permute-start.34 = (bf16[4,144,512]{2,1,0:T(8,128)(2,1)}, bf16[4,144,512]{2,1,0:T(8,128)(2,1)}, u32[]{:S(2)}, u32[]{:S(2)}) collective-permute-start(bf16[4,144,512]{2,1,0:T(8,128)(2,1)} %get-tuple-element.483), channel_id=1, source_target_pairs={{0,16},{8,24},{16,0},{24,8},{1,17},{9,25},{17,1},{25,9},{2,18},{10... | collective-permute-start | bytes 1769480 | tf_op jit(solution)/shard_map/ppermute | solution.py:108
  480.6 40.9 %collective-permute-start.42 = (bf16[4,2,208,512]{3,2,1,0:T(8,128)(2,1)}, bf16[4,2,208,512]{3,2,1,0:T(8,128)(2,1)S(1)}, u32[]{:S(2)}, u32[]{:S(2)}) collective-permute-start(bf16[4,2,208,512]{3,2,1,0:T(8,128)(2,1)} %fusion), channel_id=1, source_target_pairs={{0,8},{8,0},{16,24},{24,16},{1,9},{9,1},{17,25},{25,17},{2,10},{10... | collective-permute-start | bytes 5111816 | tf_op jit(solution)/shard_map/ppermute | solution.py:108
  485.0 36.5 %collective-permute-start.43 = (bf16[4,2,192,512]{3,2,1,0:T(8,128)(2,1)}, bf16[4,2,192,512]{3,2,1,0:T(8,128)(2,1)}, u32[]{:S(2)}, u32[]{:S(2)}) collective-permute-start(bf16[4,2,192,512]{3,2,1,0:T(8,128)(2,1)} %fusion.11), channel_id=1, source_target_pairs={{0,16},{8,24},{16,0},{24,8},{1,17},{9,25},{17,1},{25,9},{2,18},{10... | collective-permute-start | bytes 4718600 | tf_op jit(solution)/shard_map/ppermute | solution.py:108
  486.2 42.7 %collective-permute-start.46 = (bf16[288,512]{1,0:T(8,128)(2,1)}, bf16[288,512]{1,0:T(8,128)(2,1)}, u32[]{:S(2)}, u32[]{:S(2)}) collective-permute-start(bf16[288,512]{1,0:T(8,128)(2,1)} %pad_maximum_fusion.9), channel_id=1, source_target_pairs={{0,2},{1,3},{2,4},{3,5},{4,6},{5,7},{6,0},{7,1},{8,10},{9,11},{10,... | collective-permute-start | bytes 884744 | tf_op jit(solution)/shard_map/ppermute | solution.py:93
  486.8 42.1 %collective-permute-start.47 = (bf16[288,512]{1,0:T(8,128)(2,1)}, bf16[288,512]{1,0:T(8,128)(2,1)}, u32[]{:S(2)}, u32[]{:S(2)}) collective-permute-start(bf16[288,512]{1,0:T(8,128)(2,1)} %pad_maximum_fusion.10), channel_id=1, source_target_pairs={{0,4},{1,5},{2,6},{3,7},{4,0},{5,1},{6,2},{7,3},{8,12},{9,13},{10,... | collective-permute-start | bytes 884744 | tf_op jit(solution)/shard_map/ppermute | solution.py:93
  488.1 40.8 %collective-permute-start.48 = (bf16[288,512]{1,0:T(8,128)(2,1)}, bf16[288,512]{1,0:T(8,128)(2,1)}, u32[]{:S(2)}, u32[]{:S(2)}) collective-permute-start(bf16[288,512]{1,0:T(8,128)(2,1)} %pad_maximum_fusion.11), channel_id=1, source_target_pairs={{0,6},{1,7},{2,0},{3,1},{4,2},{5,3},{6,4},{7,5},{8,14},{9,15},{10,... | collective-permute-start | bytes 884744 | tf_op jit(solution)/shard_map/ppermute | solution.py:93
  576.8 39.6 %collective-permute-start.52 = (bf16[400,512]{1,0:T(8,128)(2,1)}, bf16[400,512]{1,0:T(8,128)(2,1)}, u32[]{:S(2)}, u32[]{:S(2)}) collective-permute-start(bf16[400,512]{1,0:T(8,128)(2,1)} %pad_maximum_fusion.6), channel_id=1, source_target_pairs={{0,2},{1,3},{2,4},{3,5},{4,6},{5,7},{6,0},{7,1},{8,10},{9,11},{10,... | collective-permute-start | bytes 1228808 | tf_op jit(solution)/shard_map/ppermute | solution.py:93
  583.6 32.9 %collective-permute-start.53 = (bf16[400,512]{1,0:T(8,128)(2,1)}, bf16[400,512]{1,0:T(8,128)(2,1)}, u32[]{:S(2)}, u32[]{:S(2)}) collective-permute-start(bf16[400,512]{1,0:T(8,128)(2,1)} %pad_maximum_fusion.7), channel_id=1, source_target_pairs={{0,4},{1,5},{2,6},{3,7},{4,0},{5,1},{6,2},{7,3},{8,12},{9,13},{10,... | collective-permute-start | bytes 1228808 | tf_op jit(solution)/shard_map/ppermute | solution.py:93
  583.6 32.9 %collective-permute-start.54 = (bf16[400,512]{1,0:T(8,128)(2,1)}, bf16[400,512]{1,0:T(8,128)(2,1)}, u32[]{:S(2)}, u32[]{:S(2)}) collective-permute-start(bf16[400,512]{1,0:T(8,128)(2,1)} %pad_maximum_fusion.8), channel_id=1, source_target_pairs={{0,6},{1,7},{2,0},{3,1},{4,2},{5,3},{6,4},{7,5},{8,14},{9,15},{10,... | collective-permute-start | bytes 1228808 | tf_op jit(solution)/shard_map/ppermute | solution.py:93
  639.6 31.1 %collective-permute-start.65 = (bf16[2,400,512]{2,1,0:T(8,128)(2,1)S(1)}, bf16[2,400,512]{2,1,0:T(8,128)(2,1)S(1)}, u32[]{:S(2)}, u32[]{:S(2)}) collective-permute-start(bf16[2,400,512]{2,1,0:T(8,128)(2,1)S(1)} %reverse_select_fusion.3), channel_id=1, source_target_pairs={{0,16},{8,24},{16,0},{24,8},{1,17},{9,25},{17,1},{25,9},{2,18},{10... | collective-permute-start | bytes 2457608 | tf_op jit(solution)/shard_map/ppermute | solution.py:108
  (94 other events, 1156.0 us)
Sparse Core Ops, SparseCore 0:
  44.4 40.0 all-gather.4
  86.7 49.3 all-gather.6
  306.3 84.1 reduce-scatter.1
  539.3 64.8 all-reduce.4
